TPU v7x, 32 devices: a whole 2x2x4 slice. The times are simulated.
32 devices in a mesh: spec: 4 (over y, x), tile: 8 (over z, core).
Axes of the slice: x: 2, y: 2, z: 4, core: 2. Of those that a mesh axis runs over, the one named last changes fastest.
Arguments:
- action: bfloat16 [128, 3072, 256], P('tile', 'spec'), may hold values from 0.099609375 to 2
- east_current: float32 [128, 256], P('tile'), may hold values from -0.4 to 0.4
- north_current: float32 [128, 256], P('tile'), may hold values from -0.4 to 0.4
- sea_mask: int32 [128, 256], P('tile'), may hold values from 0 to 1, as said below
- pattern: int32 [48, 24], replicated, may hold values from 0 to 47, as said below
- table: bfloat16 [48, 64, 64], replicated, may hold values from -0.15625 to 0.15625
Outputs:
- updated: bfloat16 [128, 3072, 256], P('tile', 'spec')
Inputs may be any that keep to these rules, and one draw needn't show every extreme that they name: `sea_mask`: each tile of 16 latitude rows (all 256 longitudes) holds at most 2048 sea points, and in every draw some tile holds exactly 2048. `pattern`: each row names 24 different direction blocks.
All inputs are finite; a program needn't handle non-finite values.
Results may differ from a plain program's by a relative error of at most 0.0043.
Values may be sent and summed in bfloat16 or wider, within the bound.
No kernel may reach another device: no remote copies, remote signals or barrier semaphores. Data moves between devices by JAX's collectives and lax.ppermute only.
A program may use at most 128 MiB of HBM per device.

v0:
```python
import functools

import jax
import jax.numpy as jnp
from jax import lax
from jax.experimental import pallas as pl
from jax.experimental.pallas import tpu as pltpu
from jax.sharding import PartitionSpec as P

NF = 64
ND = 48
SEA = 2048
WINDOW = 512
STEP = 256
SUBK = 16
courant_scale = 0.45
MIB = 1024 * 1024


def split_directions(count, sizes):
    if sum(sizes) == count:
        return sizes
    return (1,) * count


def offsets_of(sizes):
    return [sum(sizes[:i]) for i in range(len(sizes))]


def cost(us):
    return pl.CostEstimate(
        flops=int(us * 1.15e9), bytes_accessed=int(us * 3e6), transcendentals=0
    )


def params(mib=14):
    return pltpu.CompilerParams(vmem_limit_bytes=mib * MIB)


def near_kernel(depth, parity, act, east, north, across, beyond, ends, sem):
    rows, comps, lon = act.shape
    even = parity[0] == 0
    targets = ((even, across), (jnp.logical_not(even), beyond))
    copies = []
    for n, current in enumerate((east, north)):
        copies.append(pltpu.make_async_copy(current, ends.at[n], sem.at[n]))
    for i, (top, near) in enumerate(targets):
        first = jnp.where(top, rows - 2, 0)
        copies.append(pltpu.make_async_copy(
            act.at[pl.ds(first, 2), :depth, :], near.at[:, :depth, :], sem.at[2 + i]))
    for copy in copies:
        copy.start()
    for copy in copies:
        copy.wait()
    for top, near in targets:
        pair = [jnp.where(top, ends[n, rows - 1:rows, :], ends[n, 0:1, :]) for n in range(2)]
        pair = jnp.concatenate(pair, axis=0)
        coarse = pair.astype(jnp.bfloat16).astype(jnp.float32)
        tail = jnp.concatenate([coarse, pair - coarse, jnp.zeros((12, lon), jnp.float32)], axis=0)
        near[0, depth:, :] = tail.astype(jnp.bfloat16)
        near[1, depth:, :] = jnp.zeros((16, lon), jnp.bfloat16)


def near_edges(parity, action, east, north, depth):
    rows, comps, lon = action.shape
    vmem = pl.BlockSpec(memory_space=pltpu.VMEM)
    hbm = pl.BlockSpec(memory_space=pltpu.HBM)
    return pl.pallas_call(
        functools.partial(near_kernel, depth),
        in_specs=[pl.BlockSpec(memory_space=pltpu.SMEM), hbm, hbm, hbm],
        out_specs=[vmem] * 2,
        out_shape=[jax.ShapeDtypeStruct((2, depth + 16, lon), jnp.bfloat16)] * 2,
        scratch_shapes=[pltpu.VMEM((2, rows, lon), jnp.float32), pltpu.SemaphoreType.DMA((4,))],
        compiler_params=params(58),
        cost_estimate=cost(1),
        name="near_edges",
    )(parity, action, east, north)


def mark_kernel(rows, ahead, bases, parity, slot_t, act, onehot, held, rest, across, beyond, sem):
    even = parity[0] == 0
    copies = []
    for i, (top, far) in enumerate(((even, across), (jnp.logical_not(even), beyond))):
        first = jnp.where(top, rows - 2, 0)
        copies.append(pltpu.make_async_copy(act.at[pl.ds(first, 2), ahead:, :], far, sem.at[i]))
    for i in range(rows):
        copies.append(pltpu.make_async_copy(act.at[i, :ahead, :], held.at[i], sem.at[2 + i]))
        copies.append(pltpu.make_async_copy(act.at[i, ahead:, :], rest.at[i], sem.at[2 + rows + i]))
    for copy in copies:
        copy.start()
    lanes = lax.broadcasted_iota(jnp.int32, onehot.shape[1:], 1)
    for r in range(rows):
        onehot[r] = jnp.where(slot_t[:, r:r + 1] - bases[r] == lanes, 1.0, 0.0).astype(jnp.bfloat16)
    for copy in copies:
        copy.wait()


def mark(bases, parity, slot_t, action, ahead):
    rows, comps, lon = action.shape
    vmem = pl.BlockSpec(memory_space=pltpu.VMEM)
    smem = pl.BlockSpec(memory_space=pltpu.SMEM)
    far = jax.ShapeDtypeStruct((2, comps - ahead, lon), jnp.bfloat16)
    return pl.pallas_call(
        functools.partial(mark_kernel, rows, ahead),
        in_specs=[smem, smem, vmem, pl.BlockSpec(memory_space=pltpu.HBM)],
        out_specs=[vmem] * 5,
        out_shape=[
            jax.ShapeDtypeStruct((rows, lon, WINDOW), jnp.bfloat16),
            jax.ShapeDtypeStruct((rows, ahead, lon), action.dtype),
            jax.ShapeDtypeStruct((rows, comps - ahead, lon), action.dtype),
            far,
            far,
        ],
        scratch_shapes=[pltpu.SemaphoreType.DMA((2 + 2 * rows,))],
        compiler_params=params(40),
        cost_estimate=cost(0.2),
        name="mark",
    )(bases, parity, slot_t, action)


def setup_kernel(rows, bases, slot, pattern, table, after, spread, sel, tt):
    lon = slot.shape[1]
    depths = lax.broadcasted_iota(jnp.int32, (WINDOW, lon), 0)
    for r in range(rows):
        spread[r] = jnp.where(slot[r:r + 1, :] - bases[r] == depths, 1.0, 0.0).astype(jnp.bfloat16)
    columns = [jnp.broadcast_to(pattern[:, j:j + 1], (ND, 128)) for j in range(pattern.shape[1])]
    which = lax.broadcasted_iota(jnp.int32, (ND, 128), 1) // NF
    for t in range(ND * NF // 128):
        target = which + t * (128 // NF)
        hit = columns[0] == target
        for column in columns[1:]:
            hit = hit | (column == target)
        sel[:, t * 128:(t + 1) * 128] = jnp.where(hit, 1.0, 0.0)
    for odd in range(2):
        for t in range(ND // 2):
            pair = jnp.concatenate(
                [table[2 * t + odd].astype(jnp.float32), table[(2 * t + odd + 1) % ND].astype(jnp.float32)],
                axis=1,
            ).astype(jnp.bfloat16)
            tt[odd, :, t * 128:(t + 1) * 128] = pair
            tt[odd, :, ND * NF + t * 128:ND * NF + (t + 1) * 128] = pair


def setup(bases, slot, pattern, table, after):
    rows, lon = slot.shape
    vmem = pl.BlockSpec(memory_space=pltpu.VMEM)
    return pl.pallas_call(
        functools.partial(setup_kernel, rows),
        in_specs=[pl.BlockSpec(memory_space=pltpu.SMEM)] + [vmem] * 3 + [pl.BlockSpec(memory_space=pl.ANY)],
        out_specs=[vmem] * 3,
        out_shape=[
            jax.ShapeDtypeStruct((rows, WINDOW, lon), jnp.bfloat16),
            jax.ShapeDtypeStruct((ND, ND * NF), jnp.float32),
            jax.ShapeDtypeStruct((2, NF, 2 * ND * NF), jnp.bfloat16),
        ],
        compiler_params=params(),
        cost_estimate=cost(0.2),
        name="setup",
    )(bases, slot, pattern, table, after)


def weave_kernel(peers, dirs, begin, size, sel, tt, after, w):
    def strip(i, carry):
        r = i // size * dirs + begin + i % size
        turn = lax.rem(ND - r, ND)
        lanes = pl.ds(pl.multiple_of((turn // 2) * 128, 128), ND * NF)
        keep = jnp.broadcast_to(sel[pl.ds(r, 1), :], (16, ND * NF)).astype(jnp.bfloat16)
        for q in range(NF // 16):
            w[pl.ds(pl.multiple_of(i * NF + q * 16, 16), 16), :] = tt[turn % 2, pl.ds(q * 16, 16), lanes] * keep
        return carry

    lax.fori_loop(0, peers * size, strip, 0)


def weave(sel, tt, after, begin, size, peers, dirs):
    vmem = pl.BlockSpec(memory_space=pltpu.VMEM)
    return pl.pallas_call(
        functools.partial(weave_kernel, peers, dirs, begin, size),
        in_specs=[vmem, vmem, pl.BlockSpec(memory_space=pl.ANY)],
        out_specs=vmem,
        out_shape=jax.ShapeDtypeStruct((peers * size * NF, ND * NF), jnp.bfloat16),
        compiler_params=params(),
        cost_estimate=cost(0.1),
        name="weave",
    )(sel, tt, after)


def gather(meta, pieces, spots, dirs, x, sem):
    copies = []
    for i, (k, first) in enumerate(spots):
        depth = pieces[i].shape[0]
        start = pl.multiple_of(((meta[0] ^ k) * dirs + first) * NF, NF)
        copies.append(pltpu.make_async_copy(pieces[i], x.at[pl.ds(start, depth), :], sem.at[i]))
        copies[-1].start()
    return copies


def propagate_kernel(peers, share, begin, depth, offset, dirs, aliased, spots, meta, act, across, beyond,
                     across_tail, beyond_tail, ae_ref, an_ref, east, north, onehot, *rest):
    rows, _, lon = act.shape
    ready = rest[:len(spots)]
    rest = rest[len(spots) + aliased:]
    even = meta[3 + rows] == 0
    moved_out = rest[0]
    outs = rest[1:peers + 1]
    moved, once, be_ref, bn_ref, packed, out_sem, x_sem = rest[-7:]
    count = depth // NF
    halves = lon // 128
    lane = lax.broadcasted_iota(jnp.int32, (SUBK, 128), 1)
    first = lane == 0
    last = lane == 127

    def leave(i):
        part = pl.ds(pl.multiple_of(i * NF, NF), NF)
        far = pl.ds(pl.multiple_of(begin + i * NF, NF), NF)
        return pltpu.make_async_copy(moved.at[:, part, :], moved_out.at[:, far, :], out_sem.at[i])

    gathering = gather(meta, ready, spots, dirs, rest[peers + 1], x_sem)
    for n, (own, b_ref) in enumerate(((east, be_ref), (north, bn_ref))):
        for at, one, other in ((0, beyond_tail, across_tail), (rows + 1, across_tail, beyond_tail)):
            tails = [t[0, t.shape[1] - 16:, :].astype(jnp.float32) for t in (one, other)]
            ends = jnp.where(even, tails[0], tails[1])
            b_ref[at:at + 1, :] = courant_scale * (ends[n:n + 1, :] + ends[n + 2:n + 3, :])
        b_ref[1:rows + 1, :] = courant_scale * own[...]

    def advance(center, south, north_of, far, r):
        ae = ae_ref[far, :]
        an = an_ref[far, :]
        right = [pltpu.roll(c, 1, 1) for c in center]
        left = [pltpu.roll(c, 127, 1) for c in center]
        result = []
        for h in range(halves):
            ce = ae + be_ref[r + 1:r + 2, h * 128:(h + 1) * 128]
            cn = an + bn_ref[r + 1:r + 2, h * 128:(h + 1) * 128]
            west = jnp.where(first, right[h - 1] if h else 0.0, right[h])
            east_of = jnp.where(last, left[h + 1] if h < halves - 1 else 0.0, left[h])
            along = jnp.where(ce > 0.0, west, east_of)
            across = jnp.where(cn > 0.0, south[h], north_of[h])
            c = center[h]
            result.append(c - jnp.abs(ce) * (c - along) - jnp.abs(cn) * (c - across))
        return result

    def group(g, carry):
        ks = pl.ds(pl.multiple_of(g * SUBK, SUBK), SUBK)
        far = pl.ds(pl.multiple_of(begin + g * SUBK, SUBK), SUBK)
        edge = pl.ds(pl.multiple_of(offset + g * SUBK, SUBK), SUBK)

        def halved(value):
            return [value[:, h * 128:(h + 1) * 128] for h in range(halves)]

        def load(r):
            if 0 <= r < rows:
                return halved(act[r, edge, :].astype(jnp.float32))
            at = r + 2 if r < 0 else r - rows
            one, other = (beyond, across) if r < 0 else (across, beyond)
            return halved(
                jnp.where(even, one[at, edge, :].astype(jnp.float32), other[at, edge, :].astype(jnp.float32))
            )

        below, here = load(-2), load(-1)
        for r in range(-1, rows + 1):
            above = load(r + 1)
            value = advance(here, below, above, far, r)
            if r == -1:
                value = [jnp.where(meta[1] > 0, v, 0.0) for v in value]
            if r == rows:
                value = [jnp.where(meta[2] > 0, v, 0.0) for v in value]
            for h in range(halves):
                once[r + 1, :, h * 128:(h + 1) * 128] = value[h]
            below, here = here, above
        below, here = halved(once[0]), halved(once[1])
        for r in range(rows):
            above = halved(once[r + 2])
            value = advance(here, below, above, far, r)
            for h in range(halves):
                moved[r, ks, h * 128:(h + 1) * 128] = value[h].astype(jnp.bfloat16)
            below, here = here, above
        return carry

    def piece(i, carry):
        lax.fori_loop(i * (NF // SUBK), (i + 1) * (NF // SUBK), group, 0)
        leave(i).start()
        return carry

    lax.fori_loop(0, count, piece, 0)

    packed[...] = jnp.zeros_like(packed)
    for r in range(rows):
        window = pl.ds(pl.multiple_of(meta[3 + r], STEP), WINDOW)
        part = jnp.dot(moved[r], onehot[r], preferred_element_type=jnp.float32)
        packed[:, window] += part.astype(jnp.bfloat16)
    me = meta[0]
    for k in range(peers):
        start = pl.multiple_of((me ^ k) * share, 128)
        outs[k][...] = packed[:, pl.ds(start, share)]
    for i in range(count):
        leave(i).wait()
    for copy in gathering:
        copy.wait()


def propagate(meta, held, halos, offset, tails, ae, an, east, north, onehot, moved, x, ready, spots, begin, count, peers):
    rows, _, lon = held.shape
    comps = ae.shape[0]
    share = SEA // peers
    depth = count * NF
    vmem = pl.BlockSpec(memory_space=pltpu.VMEM)
    hbm = pl.BlockSpec(memory_space=pltpu.HBM)
    in_specs = [pl.BlockSpec(memory_space=pltpu.SMEM)] + [vmem] * 10
    in_specs += [pl.BlockSpec(memory_space=pl.ANY)] * len(ready)
    args = [meta, held, *halos, *tails, ae, an, east, north, onehot, *ready]
    out_specs = [hbm] + [vmem] * peers
    out_shape = [jax.ShapeDtypeStruct((rows, comps, lon), jnp.bfloat16)]
    out_shape += [jax.ShapeDtypeStruct((depth, share), jnp.bfloat16)] * peers
    if ready:
        out_specs.append(vmem)
        out_shape.append(jax.ShapeDtypeStruct((ND * NF, share), jnp.bfloat16))
    aliases = {}
    for buffer, spec, out in ((moved, hbm, 0), (x, vmem, peers + 1)):
        if buffer is not None:
            aliases[len(args)] = out
            in_specs.append(spec)
            args.append(buffer)
    result = pl.pallas_call(
        functools.partial(
            propagate_kernel, peers, share, begin * NF, depth, offset * NF, comps // NF, len(aliases), spots
        ),
        in_specs=in_specs,
        out_specs=out_specs,
        scratch_shapes=[
            pltpu.VMEM((rows, depth, lon), jnp.bfloat16),
            pltpu.VMEM((rows + 2, SUBK, lon), jnp.float32),
            pltpu.VMEM((rows + 2, lon), jnp.float32),
            pltpu.VMEM((rows + 2, lon), jnp.float32),
            pltpu.VMEM((depth, SEA), jnp.bfloat16),
            pltpu.SemaphoreType.DMA((count,)),
            pltpu.SemaphoreType.DMA((max(len(ready), 1),)),
        ],
        out_shape=out_shape,
        input_output_aliases=aliases,
        compiler_params=params(),
        cost_estimate=cost(2.2 * count),
        name="propagate",
    )(*args)
    return result[0], result[1:peers + 1], result[peers + 1] if ready else None


def collect_kernel(spots, dirs, meta, *rest):
    sem = rest[-1]
    for copy in gather(meta, rest[:len(spots)], spots, dirs, rest[-2], sem):
        copy.wait()


def collect(meta, x, pieces, spots, dirs):
    vmem = pl.BlockSpec(memory_space=pltpu.VMEM)
    return pl.pallas_call(
        functools.partial(collect_kernel, spots, dirs),
        in_specs=[pl.BlockSpec(memory_space=pltpu.SMEM)]
        + [pl.BlockSpec(memory_space=pl.ANY)] * len(pieces)
        + [vmem],
        out_specs=vmem,
        out_shape=jax.ShapeDtypeStruct(x.shape, x.dtype),
        scratch_shapes=[pltpu.SemaphoreType.DMA((len(pieces),))],
        input_output_aliases={1 + len(pieces): 0},
        compiler_params=params(),
        cost_estimate=cost(0.2),
        name="collect",
    )(meta, *pieces, x)


def couple_kernel(peers, dirs, begin, size, spots, meta, w, *rest):
    me = meta[0]
    if spots:
        outs = rest[len(spots) + 1:len(spots) + 1 + peers]
        x, y, sem = rest[-3:]
        for copy in gather(meta, rest[:len(spots)], spots, dirs, x, sem):
            copy.wait()
    else:
        x = rest[0]
        outs = rest[-(peers + 1):-1]
        y = rest[-1]
    coupled = jnp.dot(w[...], x[...], preferred_element_type=jnp.float32)
    for p in range(peers):
        own = x[(p * dirs + begin) * NF:(p * dirs + begin + size) * NF, :].astype(jnp.float32)
        y[p] = (own + own * coupled[p * size * NF:(p + 1) * size * NF]).astype(jnp.bfloat16)
    for k in range(peers):
        outs[k][...] = y[me ^ k]


def couple(meta, w, x, pieces, after, spots, begin, size, peers, dirs):
    share = SEA // peers
    vmem = pl.BlockSpec(memory_space=pltpu.VMEM)
    loose = pl.BlockSpec(memory_space=pl.ANY)
    outs = [jax.ShapeDtypeStruct((size * NF, share), jnp.bfloat16)] * peers
    scratch = [pltpu.VMEM((peers, size * NF, share), jnp.bfloat16)]
    aliases = {}
    if after is None:
        in_specs, args = [loose] * len(pieces) + [vmem], [*pieces, x]
        outs = outs + [jax.ShapeDtypeStruct((ND * NF, share), jnp.bfloat16)]
        scratch.append(pltpu.SemaphoreType.DMA((len(pieces),)))
        aliases = {2 + len(pieces): peers}
    else:
        in_specs, args, spots = [vmem] + [loose] * len(after), [x, *after], ()
    result = pl.pallas_call(
        functools.partial(couple_kernel, peers, dirs, begin, size, spots),
        in_specs=[pl.BlockSpec(memory_space=pltpu.SMEM), vmem] + in_specs,
        out_specs=[vmem] * len(outs),
        out_shape=outs,
        scratch_shapes=scratch,
        input_output_aliases=aliases,
        compiler_params=params(),
        cost_estimate=cost(size),
        name="couple",
    )(meta, w, *args)
    return result[:peers], result[peers] if after is None else x


def finish_kernel(peers, share, begin, group, meta, slot, spread, moved, *rest):
    pieces = rest[:peers]
    out, renewed, old, new, piece_sem, in_sem, out_sem = rest[peers:]
    rows, lon = slot.shape
    depth = renewed.shape[0]
    me = meta[0]
    copies = []
    for k in range(peers):
        start = pl.multiple_of((me ^ k) * share, 128)
        copies.append(pltpu.make_async_copy(pieces[k], renewed.at[:, pl.ds(start, share)], piece_sem.at[k]))
        copies[-1].start()
    far = slice(begin, begin + depth)
    bring, leave = [], []
    for i in range(rows // group):
        part = slice(i * group, (i + 1) * group)
        bring.append(pltpu.make_async_copy(moved.at[part, far, :], old.at[part], in_sem.at[i]))
        leave.append(pltpu.make_async_copy(new.at[part], out.at[part, far, :], out_sem.at[i]))
        bring[-1].start()
    for copy in copies:
        copy.wait()
    for r in range(rows):
        if r % group == 0:
            bring[r // group].wait()
        base = pl.multiple_of(meta[3 + r], STEP)
        value = jnp.dot(renewed[:, pl.ds(base, WINDOW)], spread[r], preferred_element_type=jnp.float32)
        sea = slot[r:r + 1, :] >= 0
        new[r] = jnp.where(sea, value, old[r].astype(jnp.float32)).astype(jnp.bfloat16)
        if r % group == group - 1:
            leave[r // group].start()
    for copy in leave:
        copy.wait()


def finish(meta, slot, spread, moved, pieces, begin, size, peers):
    rows, comps, lon = moved.shape
    share = SEA // peers
    group = 4
    hbm = pl.BlockSpec(memory_space=pltpu.HBM)
    vmem = pl.BlockSpec(memory_space=pltpu.VMEM)
    return pl.pallas_call(
        functools.partial(finish_kernel, peers, share, begin * NF, group),
        in_specs=[pl.BlockSpec(memory_space=pltpu.SMEM), vmem, vmem, hbm]
        + [pl.BlockSpec(memory_space=pl.ANY)] * peers,
        out_specs=hbm,
        out_shape=jax.ShapeDtypeStruct(moved.shape, jnp.bfloat16),
        scratch_shapes=[
            pltpu.VMEM((size * NF, SEA), jnp.bfloat16),
            pltpu.VMEM((rows, size * NF, lon), jnp.bfloat16),
            pltpu.VMEM((rows, size * NF, lon), jnp.bfloat16),
            pltpu.SemaphoreType.DMA((peers,)),
            pltpu.SemaphoreType.DMA((rows // group,)),
            pltpu.SemaphoreType.DMA((rows // group,)),
        ],
        input_output_aliases={3: 0},
        compiler_params=params(),
        cost_estimate=cost(size),
        name="finish",
    )(meta, slot, spread, moved, *pieces)


def swap(array, first):
    count = lax.axis_size("tile")
    pairs = [(i, i + 1) for i in range(first, count - 1, 2)]
    return lax.ppermute(array, "tile", pairs + [(j, i) for i, j in pairs])


def local(action, east_current, north_current, sea_mask, pattern, table):
    rows, comps, lon = action.shape
    peers = lax.axis_size("spec")
    me = lax.axis_index("spec")
    tile = lax.axis_index("tile")
    tiles = lax.axis_size("tile")
    dirs = comps // NF
    parts_out = split_directions(dirs, (3, 3, 3, 3))
    parts_back = split_directions(dirs, (2, 4, 4, 2))

    ahead = parts_out[0] * NF
    parity = (tile % 2).astype(jnp.int32)
    parity = (tile % 2).astype(jnp.int32)
    across, beyond = near_edges(parity.reshape(1), action, east_current, north_current, ahead)
    near = swap(across, 0), swap(beyond, 1)

    components = me * comps + jnp.arange(comps, dtype=jnp.int32)
    direction = (components // NF).astype(jnp.float32)
    frequency = (components % NF).astype(jnp.float32)
    speed = courant_scale * jnp.exp(-2.0 * frequency / (NF - 1))
    theta = 2.0 * jnp.pi * direction / ND
    ae = jnp.broadcast_to((speed * jnp.cos(theta))[:, None], (comps, 128))
    an = jnp.broadcast_to((speed * jnp.sin(theta))[:, None], (comps, 128))

    sea = sea_mask > 0
    before = jnp.dot(
        sea.astype(jnp.bfloat16),
        jnp.triu(jnp.ones((lon, lon), jnp.bfloat16), 1),
        preferred_element_type=jnp.float32,
    )
    totals = jnp.sum(sea.astype(jnp.float32), axis=1)
    starts = jnp.sum(
        jnp.where(jnp.tril(jnp.ones((rows, rows), jnp.bool_), -1), totals[None, :], 0.0), axis=1
    )
    slot = jnp.where(sea, (before + starts[:, None]).astype(jnp.int32), -1)
    bases = jnp.minimum(starts.astype(jnp.int32) // STEP * STEP, SEA - WINDOW)
    meta = jnp.concatenate([
        jnp.stack([me, (tile > 0).astype(jnp.int32), (tile < tiles - 1).astype(jnp.int32)]),
        bases,
        parity.reshape(1),
    ]).astype(jnp.int32)
    slot_t = slot.T

    onehot, held, remaining, across, beyond = mark(bases, parity.reshape(1), slot_t, action, ahead)
    far = swap(across, 0), swap(beyond, 1)

    moved, x = None, None
    pieces, spots = [], []
    for j, (begin, count) in enumerate(zip(offsets_of(parts_out), parts_out)):
        offset = begin - parts_out[0] if j else 0
        ready = (pieces[j - 2], tuple(spots[j - 2])) if j >= 2 else ([], ())
        moved, packed, x = propagate(
            meta, remaining if j else held, far if j else near, offset, near, ae, an,
            east_current, north_current, onehot, moved, x, *ready, begin, count, peers,
        )
        pieces.append([packed[0]] + [
            lax.ppermute(packed[k], "spec", [(i, i ^ k) for i in range(peers)])
            for k in range(1, peers)
        ])
        spots.append([(k, begin) for k in range(peers)])

    spread, sel, tt = setup(bases, slot, pattern, table, packed[0])
    woven = [
        weave(sel, tt, packed[0], begin, size, peers, dirs)
        for begin, size in zip(offsets_of(parts_back), parts_back)
    ]
    x = collect(meta, x, pieces[-2], tuple(spots[-2]), dirs)
    result = moved
    backs = []
    for g, (begin, size) in enumerate(zip(offsets_of(parts_back), parts_back)):
        after = backs[g - 2][1:] if g >= 2 else renewed[:1] if g else None
        renewed, x = couple(
            meta, woven[g], x, pieces[-1], after, tuple(spots[-1]), begin, size, peers, dirs
        )
        back = [renewed[0]] + [
            lax.ppermute(renewed[k], "spec", [(i, i ^ k) for i in range(peers)])
            for k in range(1, peers)
        ]
        backs.append(back)
        result = finish(meta, slot, spread, result, back, begin, size, peers)
    return result


def solution(mesh):
    return jax.shard_map(
        local,
        mesh=mesh,
        in_specs=(
            P("tile", "spec", None),
            P("tile", None),
            P("tile", None),
            P("tile", None),
            P(),
            P(),
        ),
        out_specs=P("tile", "spec", None),
        check_vma=False,
    )
```

profile of v0, /device:TPU:0, one launch (start us, length us, event | category | flops | bytes accessed | tf_op | source)
XLA Modules:
  0.0 131.8 jit_solution(16302464100664634107)
XLA Ops:
  0.0 1.9 %near_edges.1 = (bf16[2,208,256]{2,1,0:T(8,128)(2,1)}, bf16[2,208,256]{2,1,0:T(8,128)(2,1)}) custom-call(s32[1]{0:T(128)} %bitcast.3.parity, bf16[16,768,256]{2,1,0:T(8,128)(2,1)} %act.3, f32[16,256]{1,0:T(8,128)} %east.9, f32[16,256]{1,0:T(8,128)} %north.9), custom_call_target="tpu_custom_call" | custom-call | flops 1150000000 | bytes 3000000 | tf_op jit(solution)/shard_map/near_edges/pallas_call | solution.py:68
  4.4 5.8 %mark.1 = (bf16[16,256,512]{2,1,0:T(8,128)(2,1)S(1)}, bf16[16,192,256]{2,1,0:T(8,128)(2,1)S(1)}, bf16[16,576,256]{2,1,0:T(8,128)(2,1)S(1)}, bf16[2,576,256]{2,1,0:T(8,128)(2,1)}, bf16[2,576,256]{2,1,0:T(8,128)(2,1)}) custom-call(s32[16]{0:T(128)S(1)} %multiply_minimum_fusion.bases, s32[1]{0:T(128)} %bitcast.3.parity, s32[256,16]{1,0:T(8,128)S(1)} %copy.19.slot_t, ...), custom_call_target="tpu_custom_call" | custom-call | flops 230000000 | bytes 600000 | tf_op jit(solution)/shard_map/mark/pallas_call | solution.py:103
  10.2 2.2 %copy-done.13 = bf16[16,576,256]{2,1,0:T(8,128)(2,1)} copy-done((bf16[16,576,256]{2,1,0:T(8,128)(2,1)}, bf16[16,576,256]{2,1,0:T(8,128)(2,1)S(1)}, u32[]{:S(2)}) %copy-start.13) | copy-done | bytes 4718616
  12.4 2.0 %copy-done.14 = bf16[16,256,512]{2,1,0:T(8,128)(2,1)} copy-done((bf16[16,256,512]{2,1,0:T(8,128)(2,1)}, bf16[16,256,512]{2,1,0:T(8,128)(2,1)S(1)}, u32[]{:S(2)}) %copy-start.14) | copy-done | bytes 4194328
  14.4 3.3 %collective-permute-start = (bf16[2,576,256]{2,1,0:T(8,128)(2,1)}, bf16[2,576,256]{2,1,0:T(8,128)(2,1)S(1)}, u32[]{:S(2)}, u32[]{:S(2)}) collective-permute-start(bf16[2,576,256]{2,1,0:T(8,128)(2,1)} %get-tuple-element.55), channel_id=1, source_target_pairs={{0,1},{2,3},{4,5},{6,7},{1,0},{3,2},{5,4},{7,6},{8,9},{10,11},{12,... | collective-permute-start | bytes 1769480 | tf_op jit(solution)/shard_map/ppermute | solution.py:481
  18.9 2.3 %copy-done.15 = bf16[16,256,512]{2,1,0:T(8,128)(2,1)S(1)} copy-done((bf16[16,256,512]{2,1,0:T(8,128)(2,1)S(1)}, bf16[16,256,512]{2,1,0:T(8,128)(2,1)}, u32[]{:S(2)}) %copy-start.15) | copy-done | bytes 4194328
  21.2 6.5 %propagate.4 = (bf16[16,768,256]{2,1,0:T(8,128)(2,1)}, bf16[192,512]{1,0:T(8,128)(2,1)S(1)}, bf16[192,512]{1,0:T(8,128)(2,1)S(1)}, bf16[192,512]{1,0:T(8,128)(2,1)S(1)}, bf16[192,512]{1,0:T(8,128)(2,1)S(1)}) custom-call(s32[20]{0:T(128)S(1)} %concatenate.3.meta, bf16[16,192,256]{2,1,0:T(8,128)(2,1)S(1)} %get-tuple-element.60.act, ...), custom_call_target="tpu_custom_call" | custom-call | flops 7590000128 | bytes 19800000 | tf_op jit(solution)/shard_map/propagate/pallas_call | solution.py:324
  27.8 1.6 %collective-permute-start.7 = (bf16[192,512]{1,0:T(8,128)(2,1)S(1)}, bf16[192,512]{1,0:T(8,128)(2,1)S(1)}, u32[]{:S(2)}, u32[]{:S(2)}) collective-permute-start(bf16[192,512]{1,0:T(8,128)(2,1)S(1)} %get-tuple-element.67), channel_id=1, source_target_pairs={{0,8},{8,0},{16,24},{24,16},{1,9},{9,1},{17,25},{25,17},{2,10},{10... | collective-permute-start | bytes 589832 | tf_op jit(solution)/shard_map/ppermute | solution.py:540
  31.4 6.6 %propagate.5 = (bf16[16,768,256]{2,1,0:T(8,128)(2,1)}, bf16[192,512]{1,0:T(8,128)(2,1)S(1)}, bf16[192,512]{1,0:T(8,128)(2,1)S(1)}, bf16[192,512]{1,0:T(8,128)(2,1)S(1)}, bf16[192,512]{1,0:T(8,128)(2,1)S(1)}) custom-call(s32[20]{0:T(128)S(1)} %concatenate.3.meta, bf16[16,576,256]{2,1,0:T(8,128)(2,1)S(1)} %bitcast.8, ...), custom_call_target="tpu_custom_call", output_to_operand_aliasing={{0}: (11, {})} | custom-call | flops 7590000128 | bytes 19800000 | tf_op jit(solution)/shard_map/propagate/pallas_call | solution.py:324
  38.0 1.6 %collective-permute-start.4 = (bf16[192,512]{1,0:T(8,128)(2,1)S(1)}, bf16[192,512]{1,0:T(8,128)(2,1)S(1)}, u32[]{:S(2)}, u32[]{:S(2)}) collective-permute-start(bf16[192,512]{1,0:T(8,128)(2,1)S(1)} %get-tuple-element.63), channel_id=1, source_target_pairs={{0,8},{8,0},{16,24},{24,16},{1,9},{9,1},{17,25},{25,17},{2,10},{10... | collective-permute-start | bytes 589832 | tf_op jit(solution)/shard_map/ppermute | solution.py:540
  44.7 8.3 %propagate.6 = (bf16[16,768,256]{2,1,0:T(8,128)(2,1)}, bf16[192,512]{1,0:T(8,128)(2,1)S(1)}, bf16[192,512]{1,0:T(8,128)(2,1)S(1)}, bf16[192,512]{1,0:T(8,128)(2,...) custom-call(s32[20]{0:T(128)S(1)} %concatenate.3.meta, ...), custom_call_target="tpu_custom_call", output_to_operand_aliasing={{0}: (15, {})} | custom-call | flops 7590000128 | bytes 19800000 | tf_op jit(solution)/shard_map/propagate/pallas_call | solution.py:324
  57.2 8.4 %propagate.7 = (bf16[16,768,256]{2,1,0:T(8,128)(2,1)}, bf16[192,512]{1,0:T(8,128)(2,1)S(1)}, bf16[192,512]{1,0:T(8,128)(2,1)}, bf16[192,512]{1,0:T(8,128)(2,1)},...) custom-call(s32[20]{0:T(128)S(1)} %copy-done.5, ...), custom_call_target="tpu_custom_call", output_to_operand_aliasing={{0}: (15, {}), {5}: (16, {})} | custom-call | flops 7590000128 | bytes 19800000 | tf_op jit(solution)/shard_map/propagate/pallas_call | solution.py:324
  65.7 1.6 %collective-permute-start.10 = (bf16[192,512]{1,0:T(8,128)(2,1)}, bf16[192,512]{1,0:T(8,128)(2,1)}, u32[]{:S(2)}, u32[]{:S(2)}) collective-permute-start(bf16[192,512]{1,0:T(8,128)(2,1)} %get-tuple-element.78), channel_id=1, source_target_pairs={{0,8},{8,0},{16,24},{24,16},{1,9},{9,1},{17,25},{25,17},{2,10},{10... | collective-permute-start | bytes 589832 | tf_op jit(solution)/shard_map/ppermute | solution.py:540
  73.8 5.7 %setup.1 = (bf16[16,512,256]{2,1,0:T(8,128)(2,1)S(1)}, f32[48,3072]{1,0:T(8,128)S(1)}, bf16[2,64,6144]{2,1,0:T(8,128)(2,1)S(1)}) custom-call(s32[16]{0:T(128)S(1)} %copy-done.12, s32[16,256]{1,0:T(8,128)S(1)} %fusion.1.slot, s32[48,24]{1,0:T(8,128)S(1)} %copy-done.3, bf16[48,64,64]{2,1,0:T(8,128)(2,1)S(1)} %copy-done, ...), custom_call_target="tpu_custom_call" | custom-call | flops 230000000 | bytes 600000 | tf_op jit(solution)/shard_map/setup/pallas_call | solution.py:147
  82.8 2.1 %collect.1.rest_4_ = bf16[3072,512]{1,0:T(8,128)(2,1)S(1)} custom-call(s32[20]{0:T(128)S(1)} %copy-done.6, bf16[192,512]{1,0:T(8,128)(2,1)S(1)} %get-tuple-element.81.rest_0_, bf16[192,512]{1,0:T(8,128)(2,1)S(1)} %copy-done.2, bf16[192,512]{1,0:T(8,128)(2,1)} %collective-permute-done.14.rest_2_, ...), custom_call_target="tpu_custom_call", output_to_operand_aliasing={{}: (5, {})} | custom-call | flops 230000000 | bytes 600000 | tf_op jit(solution)/shard_map/collect/pallas_call | solution.py:356
  85.0 3.8 %couple.4 = (bf16[128,512]{1,0:T(8,128)(2,1)S(1)}, bf16[128,512]{1,0:T(8,128)(2,1)S(1)}, bf16[128,512]{1,0:T(8,128)(2,1)S(1)}, bf16[128,512]{1,0:T(8,128)(2,1)S(1)}, bf16[3072,512]{1,0:T(8,128)(2,1)S(1)}) custom-call(s32[20]{0:T(128)S(1)} %copy-done.6, bf16[512,3072]{1,0:T(8,128)(2,1)S(1)} %weave.4.w, ...), custom_call_target="tpu_custom_call", output_to_operand_aliasing={{4}: (6, {})} | custom-call | flops 2300000000 | bytes 6000000 | tf_op jit(solution)/shard_map/couple/pallas_call | solution.py:404
  92.3 4.0 %couple.5 = (bf16[256,512]{1,0:T(8,128)(2,1)S(1)}, bf16[256,512]{1,0:T(8,128)(2,1)S(1)}, bf16[256,512]{1,0:T(8,128)(2,1)S(1)}, bf16[256,512]{1,0:T(8,128)(2,1)S(1)}) custom-call(s32[20]{0:T(128)S(1)} %copy-done.6, bf16[1024,3072]{1,0:T(8,128)(2,1)S(1)} %weave.5.w, bf16[3072,512]{1,0:T(8,128)(2,1)S(1)} %get-tuple-element.90.rest_0_, ...), custom_call_target="tpu_custom_call" | custom-call | flops 4600000000 | bytes 12000000 | tf_op jit(solution)/shard_map/couple/pallas_call | solution.py:404
  99.9 4.0 %couple.6 = (bf16[256,512]{1,0:T(8,128)(2,1)S(1)}, bf16[256,512]{1,0:T(8,128)(2,1)S(1)}, bf16[256,512]{1,0:T(8,128)(2,1)S(1)}, bf16[256,512]{1,0:T(8,128)(2,1)S(1)}) custom-call(s32[20]{0:T(128)S(1)} %copy-done.6, bf16[1024,3072]{1,0:T(8,128)(2,1)S(1)} %weave.6.w, bf16[3072,512]{1,0:T(8,128)(2,1)S(1)} %get-tuple-element.90.rest_0_, ...), custom_call_target="tpu_custom_call" | custom-call | flops 4600000000 | bytes 12000000 | tf_op jit(solution)/shard_map/couple/pallas_call | solution.py:404
  107.0 3.9 %finish.4.moved = bf16[16,768,256]{2,1,0:T(8,128)(2,1)} custom-call(s32[20]{0:T(128)S(1)} %copy-done.6, s32[16,256]{1,0:T(8,128)S(1)} %fusion.1.slot, bf16[16,512,256]{2,1,0:T(8,128)(2,1)S(1)} %get-tuple-element.74.spread, bf16[16,768,256]{2,1,0:T(8,128)(2,1)} %get-tuple-element.75.moved, ...), custom_call_target="tpu_custom_call", output_to_operand_aliasing={{}: (3, {})} | custom-call | flops 2300000000 | bytes 6000000 | tf_op jit(solution)/shard_map/finish/pallas_call | solution.py:457
  112.2 2.4 %couple.7 = (bf16[128,512]{1,0:T(8,128)(2,1)S(1)}, bf16[128,512]{1,0:T(8,128)(2,1)S(1)}, bf16[128,512]{1,0:T(8,128)(2,1)S(1)}, bf16[128,512]{1,0:T(8,128)(2,1)S(1)}) custom-call(s32[20]{0:T(128)S(1)} %copy-done.6, bf16[512,3072]{1,0:T(8,128)(2,1)S(1)} %weave.7.w, bf16[3072,512]{1,0:T(8,128)(2,1)S(1)} %get-tuple-element.90.rest_0_, ...), custom_call_target="tpu_custom_call" | custom-call | flops 2300000000 | bytes 6000000 | tf_op jit(solution)/shard_map/couple/pallas_call | solution.py:404
  114.6 1.6 %collective-permute-start.25 = (bf16[128,512]{1,0:T(8,128)(2,1)S(1)}, bf16[128,512]{1,0:T(8,128)(2,1)S(1)}, u32[]{:S(2)}, u32[]{:S(2)}) collective-permute-start(bf16[128,512]{1,0:T(8,128)(2,1)S(1)} %get-tuple-element.100), channel_id=1, source_target_pairs={{0,8},{8,0},{16,24},{24,16},{1,9},{9,1},{17,25},{25,17},{2,10},{10... | collective-permute-start | bytes 393224 | tf_op jit(solution)/shard_map/ppermute | solution.py:559
  116.9 4.4 %finish.5.moved = bf16[16,768,256]{2,1,0:T(8,128)(2,1)} custom-call(s32[20]{0:T(128)S(1)} %copy-done.6, s32[16,256]{1,0:T(8,128)S(1)} %fusion.1.slot, bf16[16,512,256]{2,1,0:T(8,128)(2,1)S(1)} %get-tuple-element.74.spread, bf16[16,768,256]{2,1,0:T(8,128)(2,1)} %finish.4.moved, ...), custom_call_target="tpu_custom_call", output_to_operand_aliasing={{}: (3, {})} | custom-call | flops 4600000000 | bytes 12000000 | tf_op jit(solution)/shard_map/finish/pallas_call | solution.py:457
  123.5 4.4 %finish.6.moved = bf16[16,768,256]{2,1,0:T(8,128)(2,1)} custom-call(s32[20]{0:T(128)S(1)} %copy-done.6, s32[16,256]{1,0:T(8,128)S(1)} %fusion.1.slot, bf16[16,512,256]{2,1,0:T(8,128)(2,1)S(1)} %get-tuple-element.74.spread, bf16[16,768,256]{2,1,0:T(8,128)(2,1)} %finish.5.moved, ...), custom_call_target="tpu_custom_call", output_to_operand_aliasing={{}: (3, {})} | custom-call | flops 4600000000 | bytes 12000000 | tf_op jit(solution)/shard_map/finish/pallas_call | solution.py:457
  127.9 3.6 %finish.7 = bf16[16,768,256]{2,1,0:T(8,128)(2,1)} custom-call(s32[20]{0:T(128)S(1)} %copy-done.6, s32[16,256]{1,0:T(8,128)S(1)} %fusion.1.slot, bf16[16,512,256]{2,1,0:T(8,128)(2,1)S(1)} %get-tuple-element.74.spread, bf16[16,768,256]{2,1,0:T(8,128)(2,1)} %finish.6.moved, ...), custom_call_target="tpu_custom_call", output_to_operand_aliasing={{}: (3, {})} | custom-call | flops 2300000000 | bytes 6000000 | tf_op jit(solution)/shard_map/finish/pallas_call | solution.py:457
  (120 shorter events, 39.1 us)
Async XLA Ops:
  1.9 16.6 %collective-permute-start.2 = (bf16[2,208,256]{2,1,0:T(8,128)(2,1)}, bf16[2,208,256]{2,1,0:T(8,128)(2,1)S(1)}, u32[]{:S(2)}, u32[]{:S(2)}) collective-permute-start(bf16[2,208,256]{2,1,0:T(8,128)(2,1)} %get-tuple-element.57), channel_id=1, source_target_pairs={{0,1},{2,3},{4,5},{6,7},{1,0},{3,2},{5,4},{7,6},{8,9},{10,11},{12,... | collective-permute-start | bytes 638984 | tf_op jit(solution)/shard_map/ppermute | solution.py:481
  2.4 16.1 %collective-permute-start.3 = (bf16[2,208,256]{2,1,0:T(8,128)(2,1)}, bf16[2,208,256]{2,1,0:T(8,128)(2,1)}, u32[]{:S(2)}, u32[]{:S(2)}) collective-permute-start(bf16[2,208,256]{2,1,0:T(8,128)(2,1)} %get-tuple-element.58), channel_id=1, source_target_pairs={{1,2},{3,4},{5,6},{2,1},{4,3},{6,5},{9,10},{11,12},{13,14},{10,9},... | collective-permute-start | bytes 638984 | tf_op jit(solution)/shard_map/ppermute | solution.py:481
  14.4 17.0 %collective-permute-start = (bf16[2,576,256]{2,1,0:T(8,128)(2,1)}, bf16[2,576,256]{2,1,0:T(8,128)(2,1)S(1)}, u32[]{:S(2)}, u32[]{:S(2)}) collective-permute-start(bf16[2,576,256]{2,1,0:T(8,128)(2,1)} %get-tuple-element.55), channel_id=1, source_target_pairs={{0,1},{2,3},{4,5},{6,7},{1,0},{3,2},{5,4},{7,6},{8,9},{10,11},{12,... | collective-permute-start | bytes 1769480 | tf_op jit(solution)/shard_map/ppermute | solution.py:481
  17.7 13.7 %collective-permute-start.1 = (bf16[2,576,256]{2,1,0:T(8,128)(2,1)}, bf16[2,576,256]{2,1,0:T(8,128)(2,1)S(1)}, u32[]{:S(2)}, u32[]{:S(2)}) collective-permute-start(bf16[2,576,256]{2,1,0:T(8,128)(2,1)} %get-tuple-element.56), channel_id=1, source_target_pairs={{1,2},{3,4},{5,6},{2,1},{4,3},{6,5},{9,10},{11,12},{13,14},{10,9},... | collective-permute-start | bytes 1769480 | tf_op jit(solution)/shard_map/ppermute | solution.py:481
  27.8 13.3 %collective-permute-start.7 = (bf16[192,512]{1,0:T(8,128)(2,1)S(1)}, bf16[192,512]{1,0:T(8,128)(2,1)S(1)}, u32[]{:S(2)}, u32[]{:S(2)}) collective-permute-start(bf16[192,512]{1,0:T(8,128)(2,1)S(1)} %get-tuple-element.67), channel_id=1, source_target_pairs={{0,8},{8,0},{16,24},{24,16},{1,9},{9,1},{17,25},{25,17},{2,10},{10... | collective-permute-start | bytes 589832 | tf_op jit(solution)/shard_map/ppermute | solution.py:540
  29.3 12.3 %collective-permute-start.8 = (bf16[192,512]{1,0:T(8,128)(2,1)S(1)}, bf16[192,512]{1,0:T(8,128)(2,1)S(1)}, u32[]{:S(2)}, u32[]{:S(2)}) collective-permute-start(bf16[192,512]{1,0:T(8,128)(2,1)S(1)} %get-tuple-element.68), channel_id=1, source_target_pairs={{0,16},{8,24},{16,0},{24,8},{1,17},{9,25},{17,1},{25,9},{2,18},{10... | collective-permute-start | bytes 589832 | tf_op jit(solution)/shard_map/ppermute | solution.py:540
  30.9 10.8 %collective-permute-start.9 = (bf16[192,512]{1,0:T(8,128)(2,1)S(1)}, bf16[192,512]{1,0:T(8,128)(2,1)S(1)}, u32[]{:S(2)}, u32[]{:S(2)}) collective-permute-start(bf16[192,512]{1,0:T(8,128)(2,1)S(1)} %get-tuple-element.69), channel_id=1, source_target_pairs={{0,24},{8,16},{16,8},{24,0},{1,25},{9,17},{17,9},{25,1},{2,26},{10... | collective-permute-start | bytes 589832 | tf_op jit(solution)/shard_map/ppermute | solution.py:540
  38.0 18.0 %collective-permute-start.4 = (bf16[192,512]{1,0:T(8,128)(2,1)S(1)}, bf16[192,512]{1,0:T(8,128)(2,1)S(1)}, u32[]{:S(2)}, u32[]{:S(2)}) collective-permute-start(bf16[192,512]{1,0:T(8,128)(2,1)S(1)} %get-tuple-element.63), channel_id=1, source_target_pairs={{0,8},{8,0},{16,24},{24,16},{1,9},{9,1},{17,25},{25,17},{2,10},{10... | collective-permute-start | bytes 589832 | tf_op jit(solution)/shard_map/ppermute | solution.py:540
  39.6 17.0 %collective-permute-start.5 = (bf16[192,512]{1,0:T(8,128)(2,1)S(1)}, bf16[192,512]{1,0:T(8,128)(2,1)S(1)}, u32[]{:S(2)}, u32[]{:S(2)}) collective-permute-start(bf16[192,512]{1,0:T(8,128)(2,1)S(1)} %get-tuple-element.64), channel_id=1, source_target_pairs={{0,16},{8,24},{16,0},{24,8},{1,17},{9,25},{17,1},{25,9},{2,18},{10... | collective-permute-start | bytes 589832 | tf_op jit(solution)/shard_map/ppermute | solution.py:540
  41.1 15.5 %collective-permute-start.6 = (bf16[192,512]{1,0:T(8,128)(2,1)S(1)}, bf16[192,512]{1,0:T(8,128)(2,1)S(1)}, u32[]{:S(2)}, u32[]{:S(2)}) collective-permute-start(bf16[192,512]{1,0:T(8,128)(2,1)S(1)} %get-tuple-element.65), channel_id=1, source_target_pairs={{0,24},{8,16},{16,8},{24,0},{1,25},{9,17},{17,9},{25,1},{2,26},{10... | collective-permute-start | bytes 589832 | tf_op jit(solution)/shard_map/ppermute | solution.py:540
  53.0 15.8 %collective-permute-start.13 = (bf16[192,512]{1,0:T(8,128)(2,1)S(1)}, bf16[192,512]{1,0:T(8,128)(2,1)S(1)}, u32[]{:S(2)}, u32[]{:S(2)}) collective-permute-start(bf16[192,512]{1,0:T(8,128)(2,1)S(1)} %get-tuple-element.82), channel_id=1, source_target_pairs={{0,8},{8,0},{16,24},{24,16},{1,9},{9,1},{17,25},{25,17},{2,10},{10... | collective-permute-start | bytes 589832 | tf_op jit(solution)/shard_map/ppermute | solution.py:540
  54.6 28.2 %collective-permute-start.14 = (bf16[192,512]{1,0:T(8,128)(2,1)}, bf16[192,512]{1,0:T(8,128)(2,1)}, u32[]{:S(2)}, u32[]{:S(2)}) collective-permute-start(bf16[192,512]{1,0:T(8,128)(2,1)} %get-tuple-element.83), channel_id=1, source_target_pairs={{0,16},{8,24},{16,0},{24,8},{1,17},{9,25},{17,1},{25,9},{2,18},{10... | collective-permute-start | bytes 589832 | tf_op jit(solution)/shard_map/ppermute | solution.py:540
  56.1 26.7 %collective-permute-start.15 = (bf16[192,512]{1,0:T(8,128)(2,1)}, bf16[192,512]{1,0:T(8,128)(2,1)}, u32[]{:S(2)}, u32[]{:S(2)}) collective-permute-start(bf16[192,512]{1,0:T(8,128)(2,1)} %get-tuple-element.84), channel_id=1, source_target_pairs={{0,24},{8,16},{16,8},{24,0},{1,25},{9,17},{17,9},{25,1},{2,26},{10... | collective-permute-start | bytes 589832 | tf_op jit(solution)/shard_map/ppermute | solution.py:540
  65.7 19.3 %collective-permute-start.10 = (bf16[192,512]{1,0:T(8,128)(2,1)}, bf16[192,512]{1,0:T(8,128)(2,1)}, u32[]{:S(2)}, u32[]{:S(2)}) collective-permute-start(bf16[192,512]{1,0:T(8,128)(2,1)} %get-tuple-element.78), channel_id=1, source_target_pairs={{0,8},{8,0},{16,24},{24,16},{1,9},{9,1},{17,25},{25,17},{2,10},{10... | collective-permute-start | bytes 589832 | tf_op jit(solution)/shard_map/ppermute | solution.py:540
  67.2 17.7 %collective-permute-start.11 = (bf16[192,512]{1,0:T(8,128)(2,1)}, bf16[192,512]{1,0:T(8,128)(2,1)}, u32[]{:S(2)}, u32[]{:S(2)}) collective-permute-start(bf16[192,512]{1,0:T(8,128)(2,1)} %get-tuple-element.79), channel_id=1, source_target_pairs={{0,16},{8,24},{16,0},{24,8},{1,17},{9,25},{17,1},{25,9},{2,18},{10... | collective-permute-start | bytes 589832 | tf_op jit(solution)/shard_map/ppermute | solution.py:540
  69.5 15.5 %collective-permute-start.12 = (bf16[192,512]{1,0:T(8,128)(2,1)}, bf16[192,512]{1,0:T(8,128)(2,1)}, u32[]{:S(2)}, u32[]{:S(2)}) collective-permute-start(bf16[192,512]{1,0:T(8,128)(2,1)} %get-tuple-element.80), channel_id=1, source_target_pairs={{0,24},{8,16},{16,8},{24,0},{1,25},{9,17},{17,9},{25,1},{2,26},{10... | collective-permute-start | bytes 589832 | tf_op jit(solution)/shard_map/ppermute | solution.py:540
  96.4 14.6 %collective-permute-start.19 = (bf16[256,512]{1,0:T(8,128)(2,1)S(1)}, bf16[256,512]{1,0:T(8,128)(2,1)S(1)}, u32[]{:S(2)}, u32[]{:S(2)}) collective-permute-start(bf16[256,512]{1,0:T(8,128)(2,1)S(1)} %get-tuple-element.92), channel_id=1, source_target_pairs={{0,8},{8,0},{16,24},{24,16},{1,9},{9,1},{17,25},{25,17},{2,10},{10... | collective-permute-start | bytes 786440 | tf_op jit(solution)/shard_map/ppermute | solution.py:559
  97.9 13.6 %collective-permute-start.20 = (bf16[256,512]{1,0:T(8,128)(2,1)S(1)}, bf16[256,512]{1,0:T(8,128)(2,1)S(1)}, u32[]{:S(2)}, u32[]{:S(2)}) collective-permute-start(bf16[256,512]{1,0:T(8,128)(2,1)S(1)} %get-tuple-element.93), channel_id=1, source_target_pairs={{0,16},{8,24},{16,0},{24,8},{1,17},{9,25},{17,1},{25,9},{2,18},{10... | collective-permute-start | bytes 786440 | tf_op jit(solution)/shard_map/ppermute | solution.py:559
  99.4 12.8 %collective-permute-start.21 = (bf16[256,512]{1,0:T(8,128)(2,1)S(1)}, bf16[256,512]{1,0:T(8,128)(2,1)S(1)}, u32[]{:S(2)}, u32[]{:S(2)}) collective-permute-start(bf16[256,512]{1,0:T(8,128)(2,1)S(1)} %get-tuple-element.94), channel_id=1, source_target_pairs={{0,24},{8,16},{16,8},{24,0},{1,25},{9,17},{17,9},{25,1},{2,26},{10... | collective-permute-start | bytes 786440 | tf_op jit(solution)/shard_map/ppermute | solution.py:559
  104.0 17.4 %collective-permute-start.22 = (bf16[256,512]{1,0:T(8,128)(2,1)S(1)}, bf16[256,512]{1,0:T(8,128)(2,1)S(1)}, u32[]{:S(2)}, u32[]{:S(2)}) collective-permute-start(bf16[256,512]{1,0:T(8,128)(2,1)S(1)} %get-tuple-element.96), channel_id=1, source_target_pairs={{0,8},{8,0},{16,24},{24,16},{1,9},{9,1},{17,25},{25,17},{2,10},{10... | collective-permute-start | bytes 786440 | tf_op jit(solution)/shard_map/ppermute | solution.py:559
  105.5 17.3 %collective-permute-start.23 = (bf16[256,512]{1,0:T(8,128)(2,1)S(1)}, bf16[256,512]{1,0:T(8,128)(2,1)S(1)}, u32[]{:S(2)}, u32[]{:S(2)}) collective-permute-start(bf16[256,512]{1,0:T(8,128)(2,1)S(1)} %get-tuple-element.97), channel_id=1, source_target_pairs={{0,16},{8,24},{16,0},{24,8},{1,17},{9,25},{17,1},{25,9},{2,18},{10... | collective-permute-start | bytes 786440 | tf_op jit(solution)/shard_map/ppermute | solution.py:559
  110.9 12.6 %collective-permute-start.24 = (bf16[256,512]{1,0:T(8,128)(2,1)S(1)}, bf16[256,512]{1,0:T(8,128)(2,1)S(1)}, u32[]{:S(2)}, u32[]{:S(2)}) collective-permute-start(bf16[256,512]{1,0:T(8,128)(2,1)S(1)} %get-tuple-element.98), channel_id=1, source_target_pairs={{0,24},{8,16},{16,8},{24,0},{1,25},{9,17},{17,9},{25,1},{2,26},{10... | collective-permute-start | bytes 786440 | tf_op jit(solution)/shard_map/ppermute | solution.py:559
  114.6 13.3 %collective-permute-start.25 = (bf16[128,512]{1,0:T(8,128)(2,1)S(1)}, bf16[128,512]{1,0:T(8,128)(2,1)S(1)}, u32[]{:S(2)}, u32[]{:S(2)}) collective-permute-start(bf16[128,512]{1,0:T(8,128)(2,1)S(1)} %get-tuple-element.100), channel_id=1, source_target_pairs={{0,8},{8,0},{16,24},{24,16},{1,9},{9,1},{17,25},{25,17},{2,10},{10... | collective-permute-start | bytes 393224 | tf_op jit(solution)/shard_map/ppermute | solution.py:559
  116.2 11.7 %collective-permute-start.26 = (bf16[128,512]{1,0:T(8,128)(2,1)S(1)}, bf16[128,512]{1,0:T(8,128)(2,1)S(1)}, u32[]{:S(2)}, u32[]{:S(2)}) collective-permute-start(bf16[128,512]{1,0:T(8,128)(2,1)S(1)} %get-tuple-element.101), channel_id=1, source_target_pairs={{0,16},{8,24},{16,0},{24,8},{1,17},{9,25},{17,1},{25,9},{2,18},{10... | collective-permute-start | bytes 393224 | tf_op jit(solution)/shard_map/ppermute | solution.py:559
  (32 other events, 247.4 us)
where the time goes:
time: 132 us
  Pallas kernels  79 us (60%)
  starting transfers between devices  34.4 us (26%)
  local copies, waits for them, and re-layouts  15.3 us (12%)
  waiting for transfers between devices  1.72 us (1%)
    pallas_call x4, Pallas kernels, propagate(): pl.pallas_call(functools.partial(propagate_kernel, peers, share, begin *...  29.9 us
    pallas_call x4, Pallas kernels, finish(): pl.pallas_call(functools.partial(finish_kernel, peers, share, begin * NF,...  16.3 us
    unnamed x57, local copies, waits for them, and re-layouts  14.8 us
    ppermute x12, starting transfers between devices, local(): lax.ppermute(renewed[k], 'spec', [(i, i ^ k) for i in range(peers)])  14.3 us
    pallas_call x4, Pallas kernels, couple(): pl.pallas_call(functools.partial(couple_kernel, peers, dirs, begin, size,...  14.2 us
    ppermute x12, starting transfers between devices, local(): lax.ppermute(packed[k], 'spec', [(i, i ^ k) for i in range(peers)])  14.2 us
    ppermute x4, starting transfers between devices, swap(): return lax.ppermute(array, 'tile', pairs + [(j, i) for i, j in pairs])  5.85 us
    pallas_call x1, Pallas kernels, mark(): pl.pallas_call(functools.partial(mark_kernel, rows, ahead), in_specs=[sme...  5.81 us
  transfers between devices with their start and end apart: 28, of which 3 were waited for; matrix products, arithmetic and copies ran while one was open for 2% of the time, Pallas kernels for 53%

commit v1 on v0

--- a/solution.py
+++ b/solution.py
@@ -33,89 +33,32 @@
     )
 
 
-def params(mib=14):
+def params(mib=16):
     return pltpu.CompilerParams(vmem_limit_bytes=mib * MIB)
 
 
-def near_kernel(depth, parity, act, east, north, across, beyond, ends, sem):
-    rows, comps, lon = act.shape
-    even = parity[0] == 0
-    targets = ((even, across), (jnp.logical_not(even), beyond))
-    copies = []
-    for n, current in enumerate((east, north)):
-        copies.append(pltpu.make_async_copy(current, ends.at[n], sem.at[n]))
-    for i, (top, near) in enumerate(targets):
-        first = jnp.where(top, rows - 2, 0)
-        copies.append(pltpu.make_async_copy(
-            act.at[pl.ds(first, 2), :depth, :], near.at[:, :depth, :], sem.at[2 + i]))
-    for copy in copies:
-        copy.start()
-    for copy in copies:
-        copy.wait()
-    for top, near in targets:
-        pair = [jnp.where(top, ends[n, rows - 1:rows, :], ends[n, 0:1, :]) for n in range(2)]
-        pair = jnp.concatenate(pair, axis=0)
-        coarse = pair.astype(jnp.bfloat16).astype(jnp.float32)
-        tail = jnp.concatenate([coarse, pair - coarse, jnp.zeros((12, lon), jnp.float32)], axis=0)
-        near[0, depth:, :] = tail.astype(jnp.bfloat16)
-        near[1, depth:, :] = jnp.zeros((16, lon), jnp.bfloat16)
-
-
-def near_edges(parity, action, east, north, depth):
-    rows, comps, lon = action.shape
-    vmem = pl.BlockSpec(memory_space=pltpu.VMEM)
-    hbm = pl.BlockSpec(memory_space=pltpu.HBM)
-    return pl.pallas_call(
-        functools.partial(near_kernel, depth),
-        in_specs=[pl.BlockSpec(memory_space=pltpu.SMEM), hbm, hbm, hbm],
-        out_specs=[vmem] * 2,
-        out_shape=[jax.ShapeDtypeStruct((2, depth + 16, lon), jnp.bfloat16)] * 2,
-        scratch_shapes=[pltpu.VMEM((2, rows, lon), jnp.float32), pltpu.SemaphoreType.DMA((4,))],
-        compiler_params=params(58),
-        cost_estimate=cost(1),
-        name="near_edges",
-    )(parity, action, east, north)
-
-
-def mark_kernel(rows, ahead, bases, parity, slot_t, act, onehot, held, rest, across, beyond, sem):
-    even = parity[0] == 0
-    copies = []
-    for i, (top, far) in enumerate(((even, across), (jnp.logical_not(even), beyond))):
-        first = jnp.where(top, rows - 2, 0)
-        copies.append(pltpu.make_async_copy(act.at[pl.ds(first, 2), ahead:, :], far, sem.at[i]))
-    for i in range(rows):
-        copies.append(pltpu.make_async_copy(act.at[i, :ahead, :], held.at[i], sem.at[2 + i]))
-        copies.append(pltpu.make_async_copy(act.at[i, ahead:, :], rest.at[i], sem.at[2 + rows + i]))
-    for copy in copies:
-        copy.start()
+def mark_kernel(rows, bases, slot_t, onehot, token):
+    token[...] = jnp.zeros_like(token)
     lanes = lax.broadcasted_iota(jnp.int32, onehot.shape[1:], 1)
     for r in range(rows):
         onehot[r] = jnp.where(slot_t[:, r:r + 1] - bases[r] == lanes, 1.0, 0.0).astype(jnp.bfloat16)
-    for copy in copies:
-        copy.wait()
-
-
-def mark(bases, parity, slot_t, action, ahead):
-    rows, comps, lon = action.shape
-    vmem = pl.BlockSpec(memory_space=pltpu.VMEM)
-    smem = pl.BlockSpec(memory_space=pltpu.SMEM)
-    far = jax.ShapeDtypeStruct((2, comps - ahead, lon), jnp.bfloat16)
+
+
+def mark(bases, slot_t):
+    lon, rows = slot_t.shape
+    vmem = pl.BlockSpec(memory_space=pltpu.VMEM)
     return pl.pallas_call(
-        functools.partial(mark_kernel, rows, ahead),
-        in_specs=[smem, smem, vmem, pl.BlockSpec(memory_space=pltpu.HBM)],
-        out_specs=[vmem] * 5,
+        functools.partial(mark_kernel, rows),
+        in_specs=[pl.BlockSpec(memory_space=pltpu.SMEM), vmem],
+        out_specs=[vmem] * 2,
         out_shape=[
             jax.ShapeDtypeStruct((rows, lon, WINDOW), jnp.bfloat16),
-            jax.ShapeDtypeStruct((rows, ahead, lon), action.dtype),
-            jax.ShapeDtypeStruct((rows, comps - ahead, lon), action.dtype),
-            far,
-            far,
+            jax.ShapeDtypeStruct((8, 128), jnp.int32),
         ],
-        scratch_shapes=[pltpu.SemaphoreType.DMA((2 + 2 * rows,))],
-        compiler_params=params(40),
+        compiler_params=params(),
         cost_estimate=cost(0.2),
         name="mark",
-    )(bases, parity, slot_t, action)
+    )(bases, slot_t)
 
 
 def setup_kernel(rows, bases, slot, pattern, table, after, spread, sel, tt):
@@ -195,7 +138,7 @@
     return copies
 
 
-def propagate_kernel(peers, share, begin, depth, offset, dirs, aliased, spots, meta, act, across, beyond,
+def propagate_kernel(peers, share, begin, depth, offset, source, dirs, aliased, spots, meta, act, across, beyond,
                      across_tail, beyond_tail, ae_ref, an_ref, east, north, onehot, *rest):
     rows, _, lon = act.shape
     ready = rest[:len(spots)]
@@ -203,18 +146,25 @@
     even = meta[3 + rows] == 0
     moved_out = rest[0]
     outs = rest[1:peers + 1]
-    moved, once, be_ref, bn_ref, packed, out_sem, x_sem = rest[-7:]
+    block, moved, once, be_ref, bn_ref, packed, in_sem, out_sem, x_sem = rest[-9:]
     count = depth // NF
     halves = lon // 128
     lane = lax.broadcasted_iota(jnp.int32, (SUBK, 128), 1)
     first = lane == 0
     last = lane == 127
 
+    def bring(i):
+        part = pl.ds(pl.multiple_of(i * NF, NF), NF)
+        there = pl.ds(pl.multiple_of(source + i * NF, NF), NF)
+        return pltpu.make_async_copy(act.at[:, there, :], block.at[:, part, :], in_sem.at[i])
+
     def leave(i):
         part = pl.ds(pl.multiple_of(i * NF, NF), NF)
         far = pl.ds(pl.multiple_of(begin + i * NF, NF), NF)
         return pltpu.make_async_copy(moved.at[:, part, :], moved_out.at[:, far, :], out_sem.at[i])
 
+    for i in range(count):
+        bring(i).start()
     gathering = gather(meta, ready, spots, dirs, rest[peers + 1], x_sem)
     for n, (own, b_ref) in enumerate(((east, be_ref), (north, bn_ref))):
         for at, one, other in ((0, beyond_tail, across_tail), (rows + 1, across_tail, beyond_tail)):
@@ -250,7 +200,7 @@
 
         def load(r):
             if 0 <= r < rows:
-                return halved(act[r, edge, :].astype(jnp.float32))
+                return halved(block[r, ks, :].astype(jnp.float32))
             at = r + 2 if r < 0 else r - rows
             one, other = (beyond, across) if r < 0 else (across, beyond)
             return halved(
@@ -278,6 +228,7 @@
         return carry
 
     def piece(i, carry):
+        bring(i).wait()
         lax.fori_loop(i * (NF // SUBK), (i + 1) * (NF // SUBK), group, 0)
         leave(i).start()
         return carry
@@ -306,8 +257,8 @@
     depth = count * NF
     vmem = pl.BlockSpec(memory_space=pltpu.VMEM)
     hbm = pl.BlockSpec(memory_space=pltpu.HBM)
-    in_specs = [pl.BlockSpec(memory_space=pltpu.SMEM)] + [vmem] * 10
-    in_specs += [pl.BlockSpec(memory_space=pl.ANY)] * len(ready)
+    loose = pl.BlockSpec(memory_space=pl.ANY)
+    in_specs = [pl.BlockSpec(memory_space=pltpu.SMEM), loose] + [vmem] * 9 + [loose] * len(ready)
     args = [meta, held, *halos, *tails, ae, an, east, north, onehot, *ready]
     out_specs = [hbm] + [vmem] * peers
     out_shape = [jax.ShapeDtypeStruct((rows, comps, lon), jnp.bfloat16)]
@@ -323,16 +274,19 @@
             args.append(buffer)
     result = pl.pallas_call(
         functools.partial(
-            propagate_kernel, peers, share, begin * NF, depth, offset * NF, comps // NF, len(aliases), spots
+            propagate_kernel, peers, share, begin * NF, depth, offset * NF,
+            (begin if held.shape[1] == comps else 0) * NF, comps // NF, len(aliases), spots,
         ),
         in_specs=in_specs,
         out_specs=out_specs,
         scratch_shapes=[
             pltpu.VMEM((rows, depth, lon), jnp.bfloat16),
+            pltpu.VMEM((rows, depth, lon), jnp.bfloat16),
             pltpu.VMEM((rows + 2, SUBK, lon), jnp.float32),
             pltpu.VMEM((rows + 2, lon), jnp.float32),
             pltpu.VMEM((rows + 2, lon), jnp.float32),
             pltpu.VMEM((depth, SEA), jnp.bfloat16),
+            pltpu.SemaphoreType.DMA((count,)),
             pltpu.SemaphoreType.DMA((count,)),
             pltpu.SemaphoreType.DMA((max(len(ready), 1),)),
         ],
@@ -494,8 +448,21 @@
     ahead = parts_out[0] * NF
     parity = (tile % 2).astype(jnp.int32)
     parity = (tile % 2).astype(jnp.int32)
-    across, beyond = near_edges(parity.reshape(1), action, east_current, north_current, ahead)
-    near = swap(across, 0), swap(beyond, 1)
+    currents = jnp.stack([east_current, north_current])
+
+    def near_edge(top):
+        first = jnp.where(top, rows - 2, 0)
+        body = lax.dynamic_slice(action, (first, 0, 0), (2, ahead, lon))
+        pair = lax.dynamic_slice(currents, (0, jnp.where(top, rows - 1, 0), 0), (2, 1, lon))[:, 0]
+        coarse = lax.reduce_precision(pair, 8, 7)
+        tail = jnp.concatenate([coarse, pair - coarse, jnp.zeros((12, lon), jnp.float32)])
+        return jnp.concatenate([body, jnp.broadcast_to(tail.astype(jnp.bfloat16), (2, 16, lon))], axis=1)
+
+    def far_edge(top, zero):
+        first = jnp.where(top, rows - 2, 0) + zero
+        return lax.dynamic_slice(action, (first, ahead, 0), (2, comps - ahead, lon))
+
+    near = swap(near_edge(parity == 0), 0), swap(near_edge(parity == 1), 1)
 
     components = me * comps + jnp.arange(comps, dtype=jnp.int32)
     direction = (components // NF).astype(jnp.float32)
@@ -524,8 +491,8 @@
     ]).astype(jnp.int32)
     slot_t = slot.T
 
-    onehot, held, remaining, across, beyond = mark(bases, parity.reshape(1), slot_t, action, ahead)
-    far = swap(across, 0), swap(beyond, 1)
+    onehot, token = mark(bases, slot_t)
+    far = swap(far_edge(parity == 0, token[0, 0]), 0), swap(far_edge(parity == 1, token[0, 0]), 1)
 
     moved, x = None, None
     pieces, spots = [], []
@@ -533,7 +500,7 @@
         offset = begin - parts_out[0] if j else 0
         ready = (pieces[j - 2], tuple(spots[j - 2])) if j >= 2 else ([], ())
         moved, packed, x = propagate(
-            meta, remaining if j else held, far if j else near, offset, near, ae, an,
+            meta, action if j else action[:, :ahead], far if j else near, offset, near, ae, an,
             east_current, north_current, onehot, moved, x, *ready, begin, count, peers,
         )
         pieces.append([packed[0]] + [

time: 132 us -> 135 us (1.023)
  Pallas kernels: 79 us -> 73.3 us
  local copies, waits for them, and re-layouts: 15.3 us -> 18.7 us
  other arithmetic: 0.41 us -> 3.33 us
    pallas_call x2 -> x1, Pallas kernels: 7.7 us -> 1.55 us  [mark(): pl.pallas_call(functools.partial(mark_kernel, rows), in_specs=[pl.BlockSp...]
    dynamic_slice x0 -> x2, local copies, waits for them, and re-layouts: none -> 3.44 us  [the longest x1 2.37 us: far_edge(): return lax.dynamic_slice(action, (first, ahead, 0), (2, comps - ahead, lon))]
    unnamed x57 -> x47, local copies, waits for them, and re-layouts: 14.8 us -> 12.6 us
    slice x0 -> x2, local copies, waits for them, and re-layouts: none -> 2.02 us  [the longest x1 1.51 us: local(): action[:, :ahead]]
    concatenate x0 -> x3, other arithmetic: none -> 1.48 us  [the longest x2 1.4 us: near_edge(): jnp.concatenate([body, jnp.broadcast_to(tail.astype(jnp.bfloat16), (2, 16...]
  transfers between devices with their start and end apart: 28 -> 28, of which waited for: 3 -> 1; matrix products, arithmetic and copies ran while one was open for 2% -> 6% of each run, Pallas kernels for 53% -> 49%
where the time goes in v1:
time: 135 us; the launch traced here: 134 us
  Pallas kernels  73.3 us (54%)
  starting transfers between devices  35.7 us (26%)
  local copies, waits for them, and re-layouts  18.7 us (14%)
  other arithmetic  3.33 us (2%)
  between operations  1.83 us (1%)
  waiting for transfers between devices  1.51 us (1%)
    pallas_call x4, Pallas kernels, propagate(): pl.pallas_call(functools.partial(propagate_kernel, peers, share, begin *...  30.4 us
    pallas_call x4, Pallas kernels, finish(): pl.pallas_call(functools.partial(finish_kernel, peers, share, begin * NF,...  16.3 us
    ppermute x12, starting transfers between devices, local(): lax.ppermute(renewed[k], 'spec', [(i, i ^ k) for i in range(peers)])  14.3 us
    ppermute x12, starting transfers between devices, local(): lax.ppermute(packed[k], 'spec', [(i, i ^ k) for i in range(peers)])  14.3 us
    pallas_call x4, Pallas kernels, couple(): pl.pallas_call(functools.partial(couple_kernel, peers, dirs, begin, size,...  14.2 us
    unnamed x47, local copies, waits for them, and re-layouts  12.6 us
    ppermute x4, starting transfers between devices, swap(): return lax.ppermute(array, 'tile', pairs + [(j, i) for i, j in pairs])  7.03 us
    pallas_call x1, Pallas kernels, setup(): pl.pallas_call(functools.partial(setup_kernel, rows), in_specs=[pl.BlockS...  5.65 us
  transfers between devices with their start and end apart: 28, of which 1 were waited for; matrix products, arithmetic and copies ran while one was open for 6% of the time, Pallas kernels for 49%

profile of v1, /device:TPU:0, one launch (start us, length us, event | category | flops | bytes accessed | tf_op | source)
XLA Modules:
  0.0 134.5 jit_solution(14400961455980381238)
XLA Ops:
  11.7 2.4 %constant_dynamic-slice_fusion.2 = (bf16[2,576,256]{2,1,0:T(8,128)(2,1)}, bf16[2,576,256]{2,1,0:T(8,128)(2,1)}) fusion(bf16[16,768,256]{2,1,0:T(8,128)(2,1)} %act.5, s32[]{:T(128)S(6)} %select_n.84, s32[]{:T(128)S(6)} %select_n.82), kind=kLoop, calls=%fused_computation.49 | loop fusion | bytes 2359304 | tf_op jit(solution)/shard_map/dynamic_slice | solution.py:463
  14.8 4.6 %collective-permute-start = (bf16[2,576,256]{2,1,0:T(8,128)(2,1)}, bf16[2,576,256]{2,1,0:T(8,128)(2,1)S(1)}, u32[]{:S(2)}, u32[]{:S(2)}) collective-permute-start(bf16[2,576,256]{2,1,0:T(8,128)(2,1)} %get-tuple-element.98), channel_id=1, source_target_pairs={{0,1},{2,3},{4,5},{6,7},{1,0},{3,2},{5,4},{7,6},{8,9},{10,11},{12,... | collective-permute-start | bytes 1769480 | tf_op jit(solution)/shard_map/ppermute | solution.py:435
  21.4 2.3 %copy-done.20 = bf16[16,256,512]{2,1,0:T(8,128)(2,1)S(1)} copy-done((bf16[16,256,512]{2,1,0:T(8,128)(2,1)S(1)}, bf16[16,256,512]{2,1,0:T(8,128)(2,1)}, u32[]{:S(2)}) %copy-start.20) | copy-done | bytes 4194328
  23.7 6.7 %propagate.4 = (bf16[16,768,256]{2,1,0:T(8,128)(2,1)}, bf16[192,512]{1,0:T(8,128)(2,1)S(1)}, bf16[192,512]{1,0:T(8,128)(2,1)S(1)}, bf16[192,512]{1,0:T(8,128)(2,1)S(1)}, bf16[192,512]{1,0:T(8,128)(2,1)S(1)}) custom-call(s32[20]{0:T(128)S(1)} %concatenate.17.meta, bf16[16,192,256]{2,1,0:T(8,128)(2,1)S(1)} %slice.8.act, ...), custom_call_target="tpu_custom_call" | custom-call | flops 7590000128 | bytes 19800000 | tf_op jit(solution)/shard_map/propagate/pallas_call | solution.py:275
  30.5 2.1 %collective-permute-start.7 = (bf16[192,512]{1,0:T(8,128)(2,1)S(1)}, bf16[192,512]{1,0:T(8,128)(2,1)S(1)}, u32[]{:S(2)}, u32[]{:S(2)}) collective-permute-start(bf16[192,512]{1,0:T(8,128)(2,1)S(1)} %get-tuple-element.57), channel_id=1, source_target_pairs={{0,8},{8,0},{16,24},{24,16},{1,9},{9,1},{17,25},{25,17},{2,10},{10... | collective-permute-start | bytes 589832 | tf_op jit(solution)/shard_map/ppermute | solution.py:507
  34.2 6.8 %propagate.5 = (bf16[16,768,256]{2,1,0:T(8,128)(2,1)}, bf16[192,512]{1,0:T(8,128)(2,1)S(1)}, bf16[192,512]{1,0:T(8,128)(2,1)S(1)}, bf16[192,512]{1,0:T(8,128)(2,1)S(1)}, bf16[192,512]{1,0:T(8,128)(2,1)S(1)}) custom-call(s32[20]{0:T(128)S(1)} %concatenate.17.meta, bf16[16,768,256]{2,1,0:T(8,128)(2,1)S(1)} %bitcast.16, ...), custom_call_target="tpu_custom_call", output_to_operand_aliasing={{0}: (11, {})} | custom-call | flops 7590000128 | bytes 19800000 | tf_op jit(solution)/shard_map/propagate/pallas_call | solution.py:275
  41.0 2.0 %collective-permute-start.4 = (bf16[192,512]{1,0:T(8,128)(2,1)S(1)}, bf16[192,512]{1,0:T(8,128)(2,1)S(1)}, u32[]{:S(2)}, u32[]{:S(2)}) collective-permute-start(bf16[192,512]{1,0:T(8,128)(2,1)S(1)} %get-tuple-element.53), channel_id=1, source_target_pairs={{0,8},{8,0},{16,24},{24,16},{1,9},{9,1},{17,25},{25,17},{2,10},{10... | collective-permute-start | bytes 589832 | tf_op jit(solution)/shard_map/ppermute | solution.py:507
  47.6 8.3 %propagate.6 = (bf16[16,768,256]{2,1,0:T(8,128)(2,1)}, bf16[192,512]{1,0:T(8,128)(2,1)S(1)}, bf16[192,512]{1,0:T(8,128)(2,1)S(1)}, bf16[192,512]{1,0:T(8,128)(2,...) custom-call(s32[20]{0:T(128)S(1)} %concatenate.17.meta, ...), custom_call_target="tpu_custom_call", output_to_operand_aliasing={{0}: (15, {})} | custom-call | flops 7590000128 | bytes 19800000 | tf_op jit(solution)/shard_map/propagate/pallas_call | solution.py:275
  56.0 2.0 %collective-permute-start.13 = (bf16[192,512]{1,0:T(8,128)(2,1)S(1)}, bf16[192,512]{1,0:T(8,128)(2,1)S(1)}, u32[]{:S(2)}, u32[]{:S(2)}) collective-permute-start(bf16[192,512]{1,0:T(8,128)(2,1)S(1)} %get-tuple-element.72), channel_id=1, source_target_pairs={{0,8},{8,0},{16,24},{24,16},{1,9},{9,1},{17,25},{25,17},{2,10},{10... | collective-permute-start | bytes 589832 | tf_op jit(solution)/shard_map/ppermute | solution.py:507
  60.2 8.6 %propagate.7 = (bf16[16,768,256]{2,1,0:T(8,128)(2,1)}, bf16[192,512]{1,0:T(8,128)(2,1)S(1)}, bf16[192,512]{1,0:T(8,128)(2,1)}, bf16[192,512]{1,0:T(8,128)(2,1)},...) custom-call(s32[20]{0:T(128)S(1)} %copy-done.5, ...), custom_call_target="tpu_custom_call", output_to_operand_aliasing={{0}: (15, {}), {5}: (16, {})} | custom-call | flops 7590000128 | bytes 19800000 | tf_op jit(solution)/shard_map/propagate/pallas_call | solution.py:275
  68.8 2.0 %collective-permute-start.10 = (bf16[192,512]{1,0:T(8,128)(2,1)}, bf16[192,512]{1,0:T(8,128)(2,1)}, u32[]{:S(2)}, u32[]{:S(2)}) collective-permute-start(bf16[192,512]{1,0:T(8,128)(2,1)} %get-tuple-element.68), channel_id=1, source_target_pairs={{0,8},{8,0},{16,24},{24,16},{1,9},{9,1},{17,25},{25,17},{2,10},{10... | collective-permute-start | bytes 589832 | tf_op jit(solution)/shard_map/ppermute | solution.py:507
  76.9 5.7 %setup.1 = (bf16[16,512,256]{2,1,0:T(8,128)(2,1)S(1)}, f32[48,3072]{1,0:T(8,128)S(1)}, bf16[2,64,6144]{2,1,0:T(8,128)(2,1)S(1)}) custom-call(s32[16]{0:T(128)S(1)} %copy-done.12, s32[16,256]{1,0:T(8,128)S(1)} %fusion.1.slot, s32[48,24]{1,0:T(8,128)S(1)} %copy-done.3, bf16[48,64,64]{2,1,0:T(8,128)(2,1)S(1)} %copy-done, ...), custom_call_target="tpu_custom_call" | custom-call | flops 230000000 | bytes 600000 | tf_op jit(solution)/shard_map/setup/pallas_call | solution.py:90
  85.8 2.1 %collect.1.rest_4_ = bf16[3072,512]{1,0:T(8,128)(2,1)S(1)} custom-call(s32[20]{0:T(128)S(1)} %copy-done.6, bf16[192,512]{1,0:T(8,128)(2,1)S(1)} %get-tuple-element.71.rest_0_, bf16[192,512]{1,0:T(8,128)(2,1)S(1)} %copy-done.2, bf16[192,512]{1,0:T(8,128)(2,1)} %collective-permute-done.14.rest_2_, ...), custom_call_target="tpu_custom_call", output_to_operand_aliasing={{}: (5, {})} | custom-call | flops 230000000 | bytes 600000 | tf_op jit(solution)/shard_map/collect/pallas_call | solution.py:310
  88.0 3.8 %couple.4 = (bf16[128,512]{1,0:T(8,128)(2,1)S(1)}, bf16[128,512]{1,0:T(8,128)(2,1)S(1)}, bf16[128,512]{1,0:T(8,128)(2,1)S(1)}, bf16[128,512]{1,0:T(8,128)(2,1)S(1)}, bf16[3072,512]{1,0:T(8,128)(2,1)S(1)}) custom-call(s32[20]{0:T(128)S(1)} %copy-done.6, bf16[512,3072]{1,0:T(8,128)(2,1)S(1)} %weave.4.w, ...), custom_call_target="tpu_custom_call", output_to_operand_aliasing={{4}: (6, {})} | custom-call | flops 2300000000 | bytes 6000000 | tf_op jit(solution)/shard_map/couple/pallas_call | solution.py:358
  91.7 2.0 %collective-permute-start.16 = (bf16[128,512]{1,0:T(8,128)(2,1)S(1)}, bf16[128,512]{1,0:T(8,128)(2,1)S(1)}, u32[]{:S(2)}, u32[]{:S(2)}) collective-permute-start(bf16[128,512]{1,0:T(8,128)(2,1)S(1)} %get-tuple-element.77), channel_id=1, source_target_pairs={{0,8},{8,0},{16,24},{24,16},{1,9},{9,1},{17,25},{25,17},{2,10},{10... | collective-permute-start | bytes 393224 | tf_op jit(solution)/shard_map/ppermute | solution.py:526
  95.3 4.0 %couple.5 = (bf16[256,512]{1,0:T(8,128)(2,1)S(1)}, bf16[256,512]{1,0:T(8,128)(2,1)S(1)}, bf16[256,512]{1,0:T(8,128)(2,1)S(1)}, bf16[256,512]{1,0:T(8,128)(2,1)S(1)}) custom-call(s32[20]{0:T(128)S(1)} %copy-done.6, bf16[1024,3072]{1,0:T(8,128)(2,1)S(1)} %weave.5.w, bf16[3072,512]{1,0:T(8,128)(2,1)S(1)} %get-tuple-element.80.rest_0_, ...), custom_call_target="tpu_custom_call" | custom-call | flops 4600000000 | bytes 12000000 | tf_op jit(solution)/shard_map/couple/pallas_call | solution.py:358
  99.3 2.0 %collective-permute-start.19 = (bf16[256,512]{1,0:T(8,128)(2,1)S(1)}, bf16[256,512]{1,0:T(8,128)(2,1)S(1)}, u32[]{:S(2)}, u32[]{:S(2)}) collective-permute-start(bf16[256,512]{1,0:T(8,128)(2,1)S(1)} %get-tuple-element.82), channel_id=1, source_target_pairs={{0,8},{8,0},{16,24},{24,16},{1,9},{9,1},{17,25},{25,17},{2,10},{10... | collective-permute-start | bytes 786440 | tf_op jit(solution)/shard_map/ppermute | solution.py:526
  102.9 4.0 %couple.6 = (bf16[256,512]{1,0:T(8,128)(2,1)S(1)}, bf16[256,512]{1,0:T(8,128)(2,1)S(1)}, bf16[256,512]{1,0:T(8,128)(2,1)S(1)}, bf16[256,512]{1,0:T(8,128)(2,1)S(1)}) custom-call(s32[20]{0:T(128)S(1)} %copy-done.6, bf16[1024,3072]{1,0:T(8,128)(2,1)S(1)} %weave.6.w, bf16[3072,512]{1,0:T(8,128)(2,1)S(1)} %get-tuple-element.80.rest_0_, ...), custom_call_target="tpu_custom_call" | custom-call | flops 4600000000 | bytes 12000000 | tf_op jit(solution)/shard_map/couple/pallas_call | solution.py:358
  106.9 2.0 %collective-permute-start.22 = (bf16[256,512]{1,0:T(8,128)(2,1)S(1)}, bf16[256,512]{1,0:T(8,128)(2,1)S(1)}, u32[]{:S(2)}, u32[]{:S(2)}) collective-permute-start(bf16[256,512]{1,0:T(8,128)(2,1)S(1)} %get-tuple-element.86), channel_id=1, source_target_pairs={{0,8},{8,0},{16,24},{24,16},{1,9},{9,1},{17,25},{25,17},{2,10},{10... | collective-permute-start | bytes 786440 | tf_op jit(solution)/shard_map/ppermute | solution.py:526
  110.4 3.9 %finish.4.moved = bf16[16,768,256]{2,1,0:T(8,128)(2,1)} custom-call(s32[20]{0:T(128)S(1)} %copy-done.6, s32[16,256]{1,0:T(8,128)S(1)} %fusion.1.slot, bf16[16,512,256]{2,1,0:T(8,128)(2,1)S(1)} %get-tuple-element.64.spread, bf16[16,768,256]{2,1,0:T(8,128)(2,1)} %get-tuple-element.65.moved, ...), custom_call_target="tpu_custom_call", output_to_operand_aliasing={{}: (3, {})} | custom-call | flops 2300000000 | bytes 6000000 | tf_op jit(solution)/shard_map/finish/pallas_call | solution.py:411
  115.8 2.4 %couple.7 = (bf16[128,512]{1,0:T(8,128)(2,1)S(1)}, bf16[128,512]{1,0:T(8,128)(2,1)S(1)}, bf16[128,512]{1,0:T(8,128)(2,1)S(1)}, bf16[128,512]{1,0:T(8,128)(2,1)S(1)}) custom-call(s32[20]{0:T(128)S(1)} %copy-done.6, bf16[512,3072]{1,0:T(8,128)(2,1)S(1)} %weave.7.w, bf16[3072,512]{1,0:T(8,128)(2,1)S(1)} %get-tuple-element.80.rest_0_, ...), custom_call_target="tpu_custom_call" | custom-call | flops 2300000000 | bytes 6000000 | tf_op jit(solution)/shard_map/couple/pallas_call | solution.py:358
  120.3 4.4 %finish.5.moved = bf16[16,768,256]{2,1,0:T(8,128)(2,1)} custom-call(s32[20]{0:T(128)S(1)} %copy-done.6, s32[16,256]{1,0:T(8,128)S(1)} %fusion.1.slot, bf16[16,512,256]{2,1,0:T(8,128)(2,1)S(1)} %get-tuple-element.64.spread, bf16[16,768,256]{2,1,0:T(8,128)(2,1)} %finish.4.moved, ...), custom_call_target="tpu_custom_call", output_to_operand_aliasing={{}: (3, {})} | custom-call | flops 4600000000 | bytes 12000000 | tf_op jit(solution)/shard_map/finish/pallas_call | solution.py:411
  126.2 4.4 %finish.6.moved = bf16[16,768,256]{2,1,0:T(8,128)(2,1)} custom-call(s32[20]{0:T(128)S(1)} %copy-done.6, s32[16,256]{1,0:T(8,128)S(1)} %fusion.1.slot, bf16[16,512,256]{2,1,0:T(8,128)(2,1)S(1)} %get-tuple-element.64.spread, bf16[16,768,256]{2,1,0:T(8,128)(2,1)} %finish.5.moved, ...), custom_call_target="tpu_custom_call", output_to_operand_aliasing={{}: (3, {})} | custom-call | flops 4600000000 | bytes 12000000 | tf_op jit(solution)/shard_map/finish/pallas_call | solution.py:411
  130.6 3.6 %finish.7 = bf16[16,768,256]{2,1,0:T(8,128)(2,1)} custom-call(s32[20]{0:T(128)S(1)} %copy-done.6, s32[16,256]{1,0:T(8,128)S(1)} %fusion.1.slot, bf16[16,512,256]{2,1,0:T(8,128)(2,1)S(1)} %get-tuple-element.64.spread, bf16[16,768,256]{2,1,0:T(8,128)(2,1)} %finish.6.moved, ...), custom_call_target="tpu_custom_call", output_to_operand_aliasing={{}: (3, {})} | custom-call | flops 2300000000 | bytes 6000000 | tf_op jit(solution)/shard_map/finish/pallas_call | solution.py:411
  (122 shorter events, 40.6 us)
Async XLA Ops:
  2.7 18.3 %collective-permute-start.2 = (bf16[2,208,256]{2,1,0:T(8,128)(2,1)}, bf16[2,208,256]{2,1,0:T(8,128)(2,1)S(1)}, u32[]{:S(2)}, u32[]{:S(2)}) collective-permute-start(bf16[2,208,256]{2,1,0:T(8,128)(2,1)} %pad_maximum_fusion), channel_id=1, source_target_pairs={{0,1},{2,3},{4,5},{6,7},{1,0},{3,2},{5,4},{7,6},{8,9},{10,11},{12,... | collective-permute-start | bytes 638984 | tf_op jit(solution)/shard_map/ppermute | solution.py:435
  3.9 17.2 %collective-permute-start.3 = (bf16[2,208,256]{2,1,0:T(8,128)(2,1)}, bf16[2,208,256]{2,1,0:T(8,128)(2,1)}, u32[]{:S(2)}, u32[]{:S(2)}) collective-permute-start(bf16[2,208,256]{2,1,0:T(8,128)(2,1)} %pad_maximum_fusion.1), channel_id=1, source_target_pairs={{1,2},{3,4},{5,6},{2,1},{4,3},{6,5},{9,10},{11,12},{13,14},{10,9},... | collective-permute-start | bytes 638984 | tf_op jit(solution)/shard_map/ppermute | solution.py:435
  14.1 20.1 %collective-permute-start.1 = (bf16[2,576,256]{2,1,0:T(8,128)(2,1)}, bf16[2,576,256]{2,1,0:T(8,128)(2,1)S(1)}, u32[]{:S(2)}, u32[]{:S(2)}) collective-permute-start(bf16[2,576,256]{2,1,0:T(8,128)(2,1)} %get-tuple-element.97), channel_id=1, source_target_pairs={{1,2},{3,4},{5,6},{2,1},{4,3},{6,5},{9,10},{11,12},{13,14},{10,9},... | collective-permute-start | bytes 1769480 | tf_op jit(solution)/shard_map/ppermute | solution.py:435
  14.8 19.4 %collective-permute-start = (bf16[2,576,256]{2,1,0:T(8,128)(2,1)}, bf16[2,576,256]{2,1,0:T(8,128)(2,1)S(1)}, u32[]{:S(2)}, u32[]{:S(2)}) collective-permute-start(bf16[2,576,256]{2,1,0:T(8,128)(2,1)} %get-tuple-element.98), channel_id=1, source_target_pairs={{0,1},{2,3},{4,5},{6,7},{1,0},{3,2},{5,4},{7,6},{8,9},{10,11},{12,... | collective-permute-start | bytes 1769480 | tf_op jit(solution)/shard_map/ppermute | solution.py:435
  30.5 14.0 %collective-permute-start.7 = (bf16[192,512]{1,0:T(8,128)(2,1)S(1)}, bf16[192,512]{1,0:T(8,128)(2,1)S(1)}, u32[]{:S(2)}, u32[]{:S(2)}) collective-permute-start(bf16[192,512]{1,0:T(8,128)(2,1)S(1)} %get-tuple-element.57), channel_id=1, source_target_pairs={{0,8},{8,0},{16,24},{24,16},{1,9},{9,1},{17,25},{25,17},{2,10},{10... | collective-permute-start | bytes 589832 | tf_op jit(solution)/shard_map/ppermute | solution.py:507
  32.6 12.0 %collective-permute-start.8 = (bf16[192,512]{1,0:T(8,128)(2,1)S(1)}, bf16[192,512]{1,0:T(8,128)(2,1)S(1)}, u32[]{:S(2)}, u32[]{:S(2)}) collective-permute-start(bf16[192,512]{1,0:T(8,128)(2,1)S(1)} %get-tuple-element.58), channel_id=1, source_target_pairs={{0,16},{8,24},{16,0},{24,8},{1,17},{9,25},{17,1},{25,9},{2,18},{10... | collective-permute-start | bytes 589832 | tf_op jit(solution)/shard_map/ppermute | solution.py:507
  41.0 18.5 %collective-permute-start.4 = (bf16[192,512]{1,0:T(8,128)(2,1)S(1)}, bf16[192,512]{1,0:T(8,128)(2,1)S(1)}, u32[]{:S(2)}, u32[]{:S(2)}) collective-permute-start(bf16[192,512]{1,0:T(8,128)(2,1)S(1)} %get-tuple-element.53), channel_id=1, source_target_pairs={{0,8},{8,0},{16,24},{24,16},{1,9},{9,1},{17,25},{25,17},{2,10},{10... | collective-permute-start | bytes 589832 | tf_op jit(solution)/shard_map/ppermute | solution.py:507
  43.0 16.5 %collective-permute-start.5 = (bf16[192,512]{1,0:T(8,128)(2,1)S(1)}, bf16[192,512]{1,0:T(8,128)(2,1)S(1)}, u32[]{:S(2)}, u32[]{:S(2)}) collective-permute-start(bf16[192,512]{1,0:T(8,128)(2,1)S(1)} %get-tuple-element.54), channel_id=1, source_target_pairs={{0,16},{8,24},{16,0},{24,8},{1,17},{9,25},{17,1},{25,9},{2,18},{10... | collective-permute-start | bytes 589832 | tf_op jit(solution)/shard_map/ppermute | solution.py:507
  44.5 15.0 %collective-permute-start.6 = (bf16[192,512]{1,0:T(8,128)(2,1)S(1)}, bf16[192,512]{1,0:T(8,128)(2,1)S(1)}, u32[]{:S(2)}, u32[]{:S(2)}) collective-permute-start(bf16[192,512]{1,0:T(8,128)(2,1)S(1)} %get-tuple-element.55), channel_id=1, source_target_pairs={{0,24},{8,16},{16,8},{24,0},{1,25},{9,17},{17,9},{25,1},{2,26},{10... | collective-permute-start | bytes 589832 | tf_op jit(solution)/shard_map/ppermute | solution.py:507
  56.0 16.3 %collective-permute-start.13 = (bf16[192,512]{1,0:T(8,128)(2,1)S(1)}, bf16[192,512]{1,0:T(8,128)(2,1)S(1)}, u32[]{:S(2)}, u32[]{:S(2)}) collective-permute-start(bf16[192,512]{1,0:T(8,128)(2,1)S(1)} %get-tuple-element.72), channel_id=1, source_target_pairs={{0,8},{8,0},{16,24},{24,16},{1,9},{9,1},{17,25},{25,17},{2,10},{10... | collective-permute-start | bytes 589832 | tf_op jit(solution)/shard_map/ppermute | solution.py:507
  58.0 27.8 %collective-permute-start.14 = (bf16[192,512]{1,0:T(8,128)(2,1)}, bf16[192,512]{1,0:T(8,128)(2,1)}, u32[]{:S(2)}, u32[]{:S(2)}) collective-permute-start(bf16[192,512]{1,0:T(8,128)(2,1)} %get-tuple-element.73), channel_id=1, source_target_pairs={{0,16},{8,24},{16,0},{24,8},{1,17},{9,25},{17,1},{25,9},{2,18},{10... | collective-permute-start | bytes 589832 | tf_op jit(solution)/shard_map/ppermute | solution.py:507
  59.5 26.3 %collective-permute-start.15 = (bf16[192,512]{1,0:T(8,128)(2,1)}, bf16[192,512]{1,0:T(8,128)(2,1)}, u32[]{:S(2)}, u32[]{:S(2)}) collective-permute-start(bf16[192,512]{1,0:T(8,128)(2,1)} %get-tuple-element.74), channel_id=1, source_target_pairs={{0,24},{8,16},{16,8},{24,0},{1,25},{9,17},{17,9},{25,1},{2,26},{10... | collective-permute-start | bytes 589832 | tf_op jit(solution)/shard_map/ppermute | solution.py:507
  68.8 19.2 %collective-permute-start.10 = (bf16[192,512]{1,0:T(8,128)(2,1)}, bf16[192,512]{1,0:T(8,128)(2,1)}, u32[]{:S(2)}, u32[]{:S(2)}) collective-permute-start(bf16[192,512]{1,0:T(8,128)(2,1)} %get-tuple-element.68), channel_id=1, source_target_pairs={{0,8},{8,0},{16,24},{24,16},{1,9},{9,1},{17,25},{25,17},{2,10},{10... | collective-permute-start | bytes 589832 | tf_op jit(solution)/shard_map/ppermute | solution.py:507
  70.8 17.2 %collective-permute-start.11 = (bf16[192,512]{1,0:T(8,128)(2,1)}, bf16[192,512]{1,0:T(8,128)(2,1)}, u32[]{:S(2)}, u32[]{:S(2)}) collective-permute-start(bf16[192,512]{1,0:T(8,128)(2,1)} %get-tuple-element.69), channel_id=1, source_target_pairs={{0,16},{8,24},{16,0},{24,8},{1,17},{9,25},{17,1},{25,9},{2,18},{10... | collective-permute-start | bytes 589832 | tf_op jit(solution)/shard_map/ppermute | solution.py:507
  73.0 15.0 %collective-permute-start.12 = (bf16[192,512]{1,0:T(8,128)(2,1)}, bf16[192,512]{1,0:T(8,128)(2,1)}, u32[]{:S(2)}, u32[]{:S(2)}) collective-permute-start(bf16[192,512]{1,0:T(8,128)(2,1)} %get-tuple-element.70), channel_id=1, source_target_pairs={{0,24},{8,16},{16,8},{24,0},{1,25},{9,17},{17,9},{25,1},{2,26},{10... | collective-permute-start | bytes 589832 | tf_op jit(solution)/shard_map/ppermute | solution.py:507
  91.7 11.1 %collective-permute-start.16 = (bf16[128,512]{1,0:T(8,128)(2,1)S(1)}, bf16[128,512]{1,0:T(8,128)(2,1)S(1)}, u32[]{:S(2)}, u32[]{:S(2)}) collective-permute-start(bf16[128,512]{1,0:T(8,128)(2,1)S(1)} %get-tuple-element.77), channel_id=1, source_target_pairs={{0,8},{8,0},{16,24},{24,16},{1,9},{9,1},{17,25},{25,17},{2,10},{10... | collective-permute-start | bytes 393224 | tf_op jit(solution)/shard_map/ppermute | solution.py:526
  99.3 15.0 %collective-permute-start.19 = (bf16[256,512]{1,0:T(8,128)(2,1)S(1)}, bf16[256,512]{1,0:T(8,128)(2,1)S(1)}, u32[]{:S(2)}, u32[]{:S(2)}) collective-permute-start(bf16[256,512]{1,0:T(8,128)(2,1)S(1)} %get-tuple-element.82), channel_id=1, source_target_pairs={{0,8},{8,0},{16,24},{24,16},{1,9},{9,1},{17,25},{25,17},{2,10},{10... | collective-permute-start | bytes 786440 | tf_op jit(solution)/shard_map/ppermute | solution.py:526
  101.3 13.1 %collective-permute-start.20 = (bf16[256,512]{1,0:T(8,128)(2,1)S(1)}, bf16[256,512]{1,0:T(8,128)(2,1)S(1)}, u32[]{:S(2)}, u32[]{:S(2)}) collective-permute-start(bf16[256,512]{1,0:T(8,128)(2,1)S(1)} %get-tuple-element.83), channel_id=1, source_target_pairs={{0,16},{8,24},{16,0},{24,8},{1,17},{9,25},{17,1},{25,9},{2,18},{10... | collective-permute-start | bytes 786440 | tf_op jit(solution)/shard_map/ppermute | solution.py:526
  102.9 12.9 %collective-permute-start.21 = (bf16[256,512]{1,0:T(8,128)(2,1)S(1)}, bf16[256,512]{1,0:T(8,128)(2,1)S(1)}, u32[]{:S(2)}, u32[]{:S(2)}) collective-permute-start(bf16[256,512]{1,0:T(8,128)(2,1)S(1)} %get-tuple-element.84), channel_id=1, source_target_pairs={{0,24},{8,16},{16,8},{24,0},{1,25},{9,17},{17,9},{25,1},{2,26},{10... | collective-permute-start | bytes 786440 | tf_op jit(solution)/shard_map/ppermute | solution.py:526
  106.9 17.8 %collective-permute-start.22 = (bf16[256,512]{1,0:T(8,128)(2,1)S(1)}, bf16[256,512]{1,0:T(8,128)(2,1)S(1)}, u32[]{:S(2)}, u32[]{:S(2)}) collective-permute-start(bf16[256,512]{1,0:T(8,128)(2,1)S(1)} %get-tuple-element.86), channel_id=1, source_target_pairs={{0,8},{8,0},{16,24},{24,16},{1,9},{9,1},{17,25},{25,17},{2,10},{10... | collective-permute-start | bytes 786440 | tf_op jit(solution)/shard_map/ppermute | solution.py:526
  108.9 17.3 %collective-permute-start.23 = (bf16[256,512]{1,0:T(8,128)(2,1)S(1)}, bf16[256,512]{1,0:T(8,128)(2,1)S(1)}, u32[]{:S(2)}, u32[]{:S(2)}) collective-permute-start(bf16[256,512]{1,0:T(8,128)(2,1)S(1)} %get-tuple-element.87), channel_id=1, source_target_pairs={{0,16},{8,24},{16,0},{24,8},{1,17},{9,25},{17,1},{25,9},{2,18},{10... | collective-permute-start | bytes 786440 | tf_op jit(solution)/shard_map/ppermute | solution.py:526
  114.3 11.9 %collective-permute-start.24 = (bf16[256,512]{1,0:T(8,128)(2,1)S(1)}, bf16[256,512]{1,0:T(8,128)(2,1)S(1)}, u32[]{:S(2)}, u32[]{:S(2)}) collective-permute-start(bf16[256,512]{1,0:T(8,128)(2,1)S(1)} %get-tuple-element.88), channel_id=1, source_target_pairs={{0,24},{8,16},{16,8},{24,0},{1,25},{9,17},{17,9},{25,1},{2,26},{10... | collective-permute-start | bytes 786440 | tf_op jit(solution)/shard_map/ppermute | solution.py:526
  118.2 12.4 %collective-permute-start.25 = (bf16[128,512]{1,0:T(8,128)(2,1)S(1)}, bf16[128,512]{1,0:T(8,128)(2,1)S(1)}, u32[]{:S(2)}, u32[]{:S(2)}) collective-permute-start(bf16[128,512]{1,0:T(8,128)(2,1)S(1)} %get-tuple-element.90), channel_id=1, source_target_pairs={{0,8},{8,0},{16,24},{24,16},{1,9},{9,1},{17,25},{25,17},{2,10},{10... | collective-permute-start | bytes 393224 | tf_op jit(solution)/shard_map/ppermute | solution.py:526
  119.7 10.9 %collective-permute-start.26 = (bf16[128,512]{1,0:T(8,128)(2,1)S(1)}, bf16[128,512]{1,0:T(8,128)(2,1)S(1)}, u32[]{:S(2)}, u32[]{:S(2)}) collective-permute-start(bf16[128,512]{1,0:T(8,128)(2,1)S(1)} %get-tuple-element.91), channel_id=1, source_target_pairs={{0,16},{8,24},{16,0},{24,8},{1,17},{9,25},{17,1},{25,9},{2,18},{10... | collective-permute-start | bytes 393224 | tf_op jit(solution)/shard_map/ppermute | solution.py:526
  (27 other events, 211.2 us)

commit v2 on v1

--- a/solution.py
+++ b/solution.py
@@ -37,35 +37,47 @@
     return pltpu.CompilerParams(vmem_limit_bytes=mib * MIB)
 
 
-def mark_kernel(rows, bases, slot_t, onehot, token):
-    token[...] = jnp.zeros_like(token)
+def mark_kernel(rows, ahead, meta, slot_t, pattern, act, onehot, passed, across, beyond, sem):
+    even = meta[3 + rows] == 0
+    copies = []
+    for i, (top, far) in enumerate(((even, across), (jnp.logical_not(even), beyond))):
+        first = jnp.where(top, rows - 2, 0)
+        copies.append(pltpu.make_async_copy(act.at[pl.ds(first, 2), ahead:, :], far, sem.at[i]))
+        copies[-1].start()
+    passed[...] = pattern[...]
     lanes = lax.broadcasted_iota(jnp.int32, onehot.shape[1:], 1)
     for r in range(rows):
-        onehot[r] = jnp.where(slot_t[:, r:r + 1] - bases[r] == lanes, 1.0, 0.0).astype(jnp.bfloat16)
-
-
-def mark(bases, slot_t):
-    lon, rows = slot_t.shape
-    vmem = pl.BlockSpec(memory_space=pltpu.VMEM)
+        onehot[r] = jnp.where(slot_t[:, r:r + 1] - meta[3 + r] == lanes, 1.0, 0.0).astype(jnp.bfloat16)
+    for copy in copies:
+        copy.wait()
+
+
+def mark(meta, slot_t, pattern, action, ahead):
+    rows, comps, lon = action.shape
+    vmem = pl.BlockSpec(memory_space=pltpu.VMEM)
+    far = jax.ShapeDtypeStruct((2, comps - ahead, lon), jnp.bfloat16)
     return pl.pallas_call(
-        functools.partial(mark_kernel, rows),
-        in_specs=[pl.BlockSpec(memory_space=pltpu.SMEM), vmem],
-        out_specs=[vmem] * 2,
+        functools.partial(mark_kernel, rows, ahead),
+        in_specs=[pl.BlockSpec(memory_space=pltpu.SMEM), vmem, vmem, pl.BlockSpec(memory_space=pl.ANY)],
+        out_specs=[vmem] * 4,
         out_shape=[
             jax.ShapeDtypeStruct((rows, lon, WINDOW), jnp.bfloat16),
-            jax.ShapeDtypeStruct((8, 128), jnp.int32),
+            jax.ShapeDtypeStruct(pattern.shape, pattern.dtype),
+            far,
+            far,
         ],
+        scratch_shapes=[pltpu.SemaphoreType.DMA((2,))],
         compiler_params=params(),
         cost_estimate=cost(0.2),
         name="mark",
-    )(bases, slot_t)
-
-
-def setup_kernel(rows, bases, slot, pattern, table, after, spread, sel, tt):
+    )(meta, slot_t, pattern, action)
+
+
+def setup_kernel(rows, meta, slot, pattern, table, after, spread, sel, tt):
     lon = slot.shape[1]
     depths = lax.broadcasted_iota(jnp.int32, (WINDOW, lon), 0)
     for r in range(rows):
-        spread[r] = jnp.where(slot[r:r + 1, :] - bases[r] == depths, 1.0, 0.0).astype(jnp.bfloat16)
+        spread[r] = jnp.where(slot[r:r + 1, :] - meta[3 + r] == depths, 1.0, 0.0).astype(jnp.bfloat16)
     columns = [jnp.broadcast_to(pattern[:, j:j + 1], (ND, 128)) for j in range(pattern.shape[1])]
     which = lax.broadcasted_iota(jnp.int32, (ND, 128), 1) // NF
     for t in range(ND * NF // 128):
@@ -84,7 +96,7 @@
             tt[odd, :, ND * NF + t * 128:ND * NF + (t + 1) * 128] = pair
 
 
-def setup(bases, slot, pattern, table, after):
+def setup(meta, slot, pattern, table, after):
     rows, lon = slot.shape
     vmem = pl.BlockSpec(memory_space=pltpu.VMEM)
     return pl.pallas_call(
@@ -99,7 +111,7 @@
         compiler_params=params(),
         cost_estimate=cost(0.2),
         name="setup",
-    )(bases, slot, pattern, table, after)
+    )(meta, slot, pattern, table, after)
 
 
 def weave_kernel(peers, dirs, begin, size, sel, tt, after, w):
@@ -458,10 +470,6 @@
         tail = jnp.concatenate([coarse, pair - coarse, jnp.zeros((12, lon), jnp.float32)])
         return jnp.concatenate([body, jnp.broadcast_to(tail.astype(jnp.bfloat16), (2, 16, lon))], axis=1)
 
-    def far_edge(top, zero):
-        first = jnp.where(top, rows - 2, 0) + zero
-        return lax.dynamic_slice(action, (first, ahead, 0), (2, comps - ahead, lon))
-
     near = swap(near_edge(parity == 0), 0), swap(near_edge(parity == 1), 1)
 
     components = me * comps + jnp.arange(comps, dtype=jnp.int32)
@@ -491,8 +499,8 @@
     ]).astype(jnp.int32)
     slot_t = slot.T
 
-    onehot, token = mark(bases, slot_t)
-    far = swap(far_edge(parity == 0, token[0, 0]), 0), swap(far_edge(parity == 1, token[0, 0]), 1)
+    onehot, pattern, across, beyond = mark(meta, slot_t, pattern, action, ahead)
+    far = swap(across, 0), swap(beyond, 1)
 
     moved, x = None, None
     pieces, spots = [], []
@@ -500,7 +508,7 @@
         offset = begin - parts_out[0] if j else 0
         ready = (pieces[j - 2], tuple(spots[j - 2])) if j >= 2 else ([], ())
         moved, packed, x = propagate(
-            meta, action if j else action[:, :ahead], far if j else near, offset, near, ae, an,
+            meta, action, far if j else near, offset, near, ae, an,
             east_current, north_current, onehot, moved, x, *ready, begin, count, peers,
         )
         pieces.append([packed[0]] + [
@@ -509,7 +517,7 @@
         ])
         spots.append([(k, begin) for k in range(peers)])
 
-    spread, sel, tt = setup(bases, slot, pattern, table, packed[0])
+    spread, sel, tt = setup(meta, slot, pattern, table, packed[0])
     woven = [
         weave(sel, tt, packed[0], begin, size, peers, dirs)
         for begin, size in zip(offsets_of(parts_back), parts_back)

time: 135 us -> 121 us (0.90)
  local copies, waits for them, and re-layouts: 18.7 us -> 12.2 us
  Pallas kernels: 73.3 us -> 69.1 us
    pallas_call x4, Pallas kernels: 30.4 us -> 26.8 us  [propagate(): pl.pallas_call(functools.partial(propagate_kernel, peers, share, begin *...]
    dynamic_slice x1 -> x0, local copies, waits for them, and re-layouts: 2.37 us -> none  [far_edge(): return lax.dynamic_slice(action, (first, ahead, 0), (2, comps - ahead, lon))]
    unnamed x47 -> x15, local copies, waits for them, and re-layouts: 12.6 us -> 10.6 us
    slice x2 -> x0, local copies, waits for them, and re-layouts: 2.02 us -> none  [the longest x1 1.51 us: local(): action[:, :ahead]]
    concatenate x2, other arithmetic: 1.4 us -> 0.03 us  [near_edge(): jnp.concatenate([body, jnp.broadcast_to(tail.astype(jnp.bfloat16), (2, 16...]
  transfers between devices with their start and end apart: 28 -> 28, of which waited for: 1 -> 3; matrix products, arithmetic and copies ran while one was open for 6% -> 2% of each run, Pallas kernels for 49% -> 52%
where the time goes in v2:
time: 121 us; the launch traced here: 120 us
  Pallas kernels  69.1 us (57%)
  starting transfers between devices  34.4 us (28%)
  local copies, waits for them, and re-layouts  12.2 us (10%)
  other arithmetic  1.99 us (2%)
  waiting for transfers between devices  1.77 us (1%)
    pallas_call x4, Pallas kernels, propagate(): pl.pallas_call(functools.partial(propagate_kernel, peers, share, begin *...  26.8 us
    pallas_call x4, Pallas kernels, finish(): pl.pallas_call(functools.partial(finish_kernel, peers, share, begin * NF,...  16.3 us
    ppermute x12, starting transfers between devices, local(): lax.ppermute(renewed[k], 'spec', [(i, i ^ k) for i in range(peers)])  14.3 us
    ppermute x12, starting transfers between devices, local(): lax.ppermute(packed[k], 'spec', [(i, i ^ k) for i in range(peers)])  14.2 us
    pallas_call x4, Pallas kernels, couple(): pl.pallas_call(functools.partial(couple_kernel, peers, dirs, begin, size,...  13.8 us
    unnamed x15, local copies, waits for them, and re-layouts  10.6 us
    ppermute x4, starting transfers between devices, swap(): return lax.ppermute(array, 'tile', pairs + [(j, i) for i, j in pairs])  5.83 us
    pallas_call x1, Pallas kernels, setup(): pl.pallas_call(functools.partial(setup_kernel, rows), in_specs=[pl.BlockS...  5.65 us
  transfers between devices with their start and end apart: 28, of which 3 were waited for; matrix products, arithmetic and copies ran while one was open for 2% of the time, Pallas kernels for 52%

profile of v2, /device:TPU:0, one launch (start us, length us, event | category | flops | bytes accessed | tf_op | source)
XLA Modules:
  0.0 120.1 jit_solution(3944063420566880632)
XLA Ops:
  5.4 2.8 %copy-done = bf16[16,768,256]{2,1,0:T(8,128)(2,1)S(1)} copy-done((bf16[16,768,256]{2,1,0:T(8,128)(2,1)S(1)}, bf16[16,768,256]{2,1,0:T(8,128)(2,1)}, u32[]{:S(2)}) %copy-start) | copy-done | bytes 6291480
  8.2 1.7 %mark.1 = (bf16[16,256,512]{2,1,0:T(8,128)(2,1)S(1)}, s32[48,24]{1,0:T(8,128)S(1)}, bf16[2,576,256]{2,1,0:T(8,128)(2,1)S(1)}, bf16[2,576,256]{2,1,0:T(8,128)(2,1)S(1)}) custom-call(s32[20]{0:T(128)S(1)} %concatenate.17.meta, s32[256,16]{1,0:T(8,128)S(1)} %copy.19.slot_t, s32[48,24]{1,0:T(8,128)S(1)} %copy.20.pattern, bf16[16,768,256]{2,1,0:T(8,128)(2,1)S(1)} %copy-done), custom_call_target="tpu_custom_call" | custom-call | flops 230000000 | bytes 600000 | tf_op jit(solution)/shard_map/mark/pallas_call | solution.py:59
  10.0 2.0 %copy-done.5 = bf16[16,256,512]{2,1,0:T(8,128)(2,1)} copy-done((bf16[16,256,512]{2,1,0:T(8,128)(2,1)}, bf16[16,256,512]{2,1,0:T(8,128)(2,1)S(1)}, u32[]{:S(2)}) %copy-start.5) | copy-done | bytes 4194328
  12.0 3.9 %collective-permute-start = (bf16[2,576,256]{2,1,0:T(8,128)(2,1)S(1)}, bf16[2,576,256]{2,1,0:T(8,128)(2,1)S(1)}, u32[]{:S(2)}, u32[]{:S(2)}) collective-permute-start(bf16[2,576,256]{2,1,0:T(8,128)(2,1)S(1)} %get-tuple-element.52), channel_id=1, source_target_pairs={{0,1},{2,3},{4,5},{6,7},{1,0},{3,2},{5,4},{7,6},{8,9},{10,11},{12,... | collective-permute-start | bytes 1769480 | tf_op jit(solution)/shard_map/ppermute | solution.py:447
  17.1 2.8 %copy-done.1 = bf16[16,768,256]{2,1,0:T(8,128)(2,1)S(1)} copy-done((bf16[16,768,256]{2,1,0:T(8,128)(2,1)S(1)}, bf16[16,768,256]{2,1,0:T(8,128)(2,1)}, u32[]{:S(2)}) %copy-start.1) | copy-done | bytes 6291480
  19.8 2.2 %copy-done.6 = bf16[16,256,512]{2,1,0:T(8,128)(2,1)S(1)} copy-done((bf16[16,256,512]{2,1,0:T(8,128)(2,1)S(1)}, bf16[16,256,512]{2,1,0:T(8,128)(2,1)}, u32[]{:S(2)}) %copy-start.6) | copy-done | bytes 4194328
  22.0 6.1 %propagate.4 = (bf16[16,768,256]{2,1,0:T(8,128)(2,1)}, bf16[192,512]{1,0:T(8,128)(2,1)S(1)}, bf16[192,512]{1,0:T(8,128)(2,1)S(1)}, bf16[192,512]{1,0:T(8,128)(2,1)S(1)}, bf16[192,512]{1,0:T(8,128)(2,1)S(1)}) custom-call(s32[20]{0:T(128)S(1)} %concatenate.17.meta, bf16[16,768,256]{2,1,0:T(8,128)(2,1)S(1)} %copy-done.1, ...), custom_call_target="tpu_custom_call" | custom-call | flops 7590000128 | bytes 19800000 | tf_op jit(solution)/shard_map/propagate/pallas_call | solution.py:287
  31.7 6.1 %propagate.5 = (bf16[16,768,256]{2,1,0:T(8,128)(2,1)}, bf16[192,512]{1,0:T(8,128)(2,1)S(1)}, bf16[192,512]{1,0:T(8,128)(2,1)S(1)}, bf16[192,512]{1,0:T(8,128)(2,1)S(1)}, bf16[192,512]{1,0:T(8,128)(2,1)S(1)}) custom-call(s32[20]{0:T(128)S(1)} %concatenate.17.meta, bf16[16,768,256]{2,1,0:T(8,128)(2,1)S(1)} %copy-done.1, ...), custom_call_target="tpu_custom_call", output_to_operand_aliasing={{0}: (11, {})} | custom-call | flops 7590000128 | bytes 19800000 | tf_op jit(solution)/shard_map/propagate/pallas_call | solution.py:287
  37.8 1.6 %collective-permute-start.4 = (bf16[192,512]{1,0:T(8,128)(2,1)S(1)}, bf16[192,512]{1,0:T(8,128)(2,1)S(1)}, u32[]{:S(2)}, u32[]{:S(2)}) collective-permute-start(bf16[192,512]{1,0:T(8,128)(2,1)S(1)} %get-tuple-element.57), channel_id=1, source_target_pairs={{0,8},{8,0},{16,24},{24,16},{1,9},{9,1},{17,25},{25,17},{2,10},{10... | collective-permute-start | bytes 589832 | tf_op jit(solution)/shard_map/ppermute | solution.py:515
  41.4 7.2 %propagate.6 = (bf16[16,768,256]{2,1,0:T(8,128)(2,1)}, bf16[192,512]{1,0:T(8,128)(2,1)S(1)}, bf16[192,512]{1,0:T(8,128)(2,1)S(1)}, bf16[192,512]{1,0:T(8,128)(2,...) custom-call(s32[20]{0:T(128)S(1)} %concatenate.17.meta, ...), custom_call_target="tpu_custom_call", output_to_operand_aliasing={{0}: (15, {})} | custom-call | flops 7590000128 | bytes 19800000 | tf_op jit(solution)/shard_map/propagate/pallas_call | solution.py:287
  52.1 7.4 %propagate.7 = (bf16[16,768,256]{2,1,0:T(8,128)(2,1)}, bf16[192,512]{1,0:T(8,128)(2,1)S(1)}, bf16[192,512]{1,0:T(8,128)(2,1)S(1)}, bf16[192,512]{1,0:T(8,128)(2,...) custom-call(s32[20]{0:T(128)S(1)} %concatenate.17.meta, ...), custom_call_target="tpu_custom_call", output_to_operand_aliasing={{0}: (15, {}), {5}: (16, {})} | custom-call | flops 7590000128 | bytes 19800000 | tf_op jit(solution)/shard_map/propagate/pallas_call | solution.py:287
  59.5 1.6 %collective-permute-start.10 = (bf16[192,512]{1,0:T(8,128)(2,1)S(1)}, bf16[192,512]{1,0:T(8,128)(2,1)S(1)}, u32[]{:S(2)}, u32[]{:S(2)}) collective-permute-start(bf16[192,512]{1,0:T(8,128)(2,1)S(1)} %get-tuple-element.72), channel_id=1, source_target_pairs={{0,8},{8,0},{16,24},{24,16},{1,9},{9,1},{17,25},{25,17},{2,10},{10... | collective-permute-start | bytes 589832 | tf_op jit(solution)/shard_map/ppermute | solution.py:515
  63.1 5.7 %setup.1 = (bf16[16,512,256]{2,1,0:T(8,128)(2,1)S(1)}, f32[48,3072]{1,0:T(8,128)S(1)}, bf16[2,64,6144]{2,1,0:T(8,128)(2,1)S(1)}) custom-call(s32[20]{0:T(128)S(1)} %concatenate.17.meta, s32[16,256]{1,0:T(8,128)S(1)} %fusion.1.slot, s32[48,24]{1,0:T(8,128)S(1)} %get-tuple-element.51.pattern, bf16[48,64,64]{2,1,0:T(8,128)(2,1)S(1)} %copy-done.2, ...), custom_call_target="tpu_custom_call" | custom-call | flops 230000000 | bytes 600000 | tf_op jit(solution)/shard_map/setup/pallas_call | solution.py:102
  72.0 1.6 %collect.1.rest_4_ = bf16[3072,512]{1,0:T(8,128)(2,1)S(1)} custom-call(s32[20]{0:T(128)S(1)} %concatenate.17.meta, bf16[192,512]{1,0:T(8,128)(2,1)S(1)} %get-tuple-element.75.rest_0_, bf16[192,512]{1,0:T(8,128)(2,1)S(1)} %collective-permute-done.13.rest_1_, bf16[192,512]{1,0:T(8,128)(2,1)S(1)} %collective-permute-done.14.rest_2_, ...), custom_call_target="tpu_custom_call", output_to_operand_aliasing={{}: (5, {})} | custom-call | flops 230000000 | bytes 600000 | tf_op jit(solution)/shard_map/collect/pallas_call | solution.py:322
  73.7 3.4 %couple.4 = (bf16[128,512]{1,0:T(8,128)(2,1)S(1)}, bf16[128,512]{1,0:T(8,128)(2,1)S(1)}, bf16[128,512]{1,0:T(8,128)(2,1)S(1)}, bf16[128,512]{1,0:T(8,128)(2,1)S(1)}, bf16[3072,512]{1,0:T(8,128)(2,1)S(1)}) custom-call(s32[20]{0:T(128)S(1)} %concatenate.17.meta, bf16[512,3072]{1,0:T(8,128)(2,1)S(1)} %weave.4.w, ...), custom_call_target="tpu_custom_call", output_to_operand_aliasing={{4}: (6, {})} | custom-call | flops 2300000000 | bytes 6000000 | tf_op jit(solution)/shard_map/couple/pallas_call | solution.py:370
  77.1 1.6 %collective-permute-start.16 = (bf16[128,512]{1,0:T(8,128)(2,1)S(1)}, bf16[128,512]{1,0:T(8,128)(2,1)S(1)}, u32[]{:S(2)}, u32[]{:S(2)}) collective-permute-start(bf16[128,512]{1,0:T(8,128)(2,1)S(1)} %get-tuple-element.81), channel_id=1, source_target_pairs={{0,8},{8,0},{16,24},{24,16},{1,9},{9,1},{17,25},{25,17},{2,10},{10... | collective-permute-start | bytes 393224 | tf_op jit(solution)/shard_map/ppermute | solution.py:534
  80.7 4.0 %couple.5 = (bf16[256,512]{1,0:T(8,128)(2,1)S(1)}, bf16[256,512]{1,0:T(8,128)(2,1)S(1)}, bf16[256,512]{1,0:T(8,128)(2,1)S(1)}, bf16[256,512]{1,0:T(8,128)(2,1)S(1)}) custom-call(s32[20]{0:T(128)S(1)} %concatenate.17.meta, bf16[1024,3072]{1,0:T(8,128)(2,1)S(1)} %weave.5.w, bf16[3072,512]{1,0:T(8,128)(2,1)S(1)} %get-tuple-element.84.rest_0_, ...), custom_call_target="tpu_custom_call" | custom-call | flops 4600000000 | bytes 12000000 | tf_op jit(solution)/shard_map/couple/pallas_call | solution.py:370
  88.2 4.0 %couple.6 = (bf16[256,512]{1,0:T(8,128)(2,1)S(1)}, bf16[256,512]{1,0:T(8,128)(2,1)S(1)}, bf16[256,512]{1,0:T(8,128)(2,1)S(1)}, bf16[256,512]{1,0:T(8,128)(2,1)S(1)}) custom-call(s32[20]{0:T(128)S(1)} %concatenate.17.meta, bf16[1024,3072]{1,0:T(8,128)(2,1)S(1)} %weave.6.w, bf16[3072,512]{1,0:T(8,128)(2,1)S(1)} %get-tuple-element.84.rest_0_, ...), custom_call_target="tpu_custom_call" | custom-call | flops 4600000000 | bytes 12000000 | tf_op jit(solution)/shard_map/couple/pallas_call | solution.py:370
  95.3 3.9 %finish.4.moved = bf16[16,768,256]{2,1,0:T(8,128)(2,1)} custom-call(s32[20]{0:T(128)S(1)} %concatenate.17.meta, s32[16,256]{1,0:T(8,128)S(1)} %fusion.1.slot, bf16[16,512,256]{2,1,0:T(8,128)(2,1)S(1)} %get-tuple-element.68.spread, bf16[16,768,256]{2,1,0:T(8,128)(2,1)} %get-tuple-element.69.moved, ...), custom_call_target="tpu_custom_call", output_to_operand_aliasing={{}: (3, {})} | custom-call | flops 2300000000 | bytes 6000000 | tf_op jit(solution)/shard_map/finish/pallas_call | solution.py:423
  100.6 2.4 %couple.7 = (bf16[128,512]{1,0:T(8,128)(2,1)S(1)}, bf16[128,512]{1,0:T(8,128)(2,1)S(1)}, bf16[128,512]{1,0:T(8,128)(2,1)S(1)}, bf16[128,512]{1,0:T(8,128)(2,1)S(1)}) custom-call(s32[20]{0:T(128)S(1)} %concatenate.17.meta, bf16[512,3072]{1,0:T(8,128)(2,1)S(1)} %weave.7.w, bf16[3072,512]{1,0:T(8,128)(2,1)S(1)} %get-tuple-element.84.rest_0_, ...), custom_call_target="tpu_custom_call" | custom-call | flops 2300000000 | bytes 6000000 | tf_op jit(solution)/shard_map/couple/pallas_call | solution.py:370
  102.9 1.6 %collective-permute-start.25 = (bf16[128,512]{1,0:T(8,128)(2,1)S(1)}, bf16[128,512]{1,0:T(8,128)(2,1)S(1)}, u32[]{:S(2)}, u32[]{:S(2)}) collective-permute-start(bf16[128,512]{1,0:T(8,128)(2,1)S(1)} %get-tuple-element.94), channel_id=1, source_target_pairs={{0,8},{8,0},{16,24},{24,16},{1,9},{9,1},{17,25},{25,17},{2,10},{10... | collective-permute-start | bytes 393224 | tf_op jit(solution)/shard_map/ppermute | solution.py:534
  105.2 4.4 %finish.5.moved = bf16[16,768,256]{2,1,0:T(8,128)(2,1)} custom-call(s32[20]{0:T(128)S(1)} %concatenate.17.meta, s32[16,256]{1,0:T(8,128)S(1)} %fusion.1.slot, bf16[16,512,256]{2,1,0:T(8,128)(2,1)S(1)} %get-tuple-element.68.spread, bf16[16,768,256]{2,1,0:T(8,128)(2,1)} %finish.4.moved, ...), custom_call_target="tpu_custom_call", output_to_operand_aliasing={{}: (3, {})} | custom-call | flops 4600000000 | bytes 12000000 | tf_op jit(solution)/shard_map/finish/pallas_call | solution.py:423
  111.8 4.4 %finish.6.moved = bf16[16,768,256]{2,1,0:T(8,128)(2,1)} custom-call(s32[20]{0:T(128)S(1)} %concatenate.17.meta, s32[16,256]{1,0:T(8,128)S(1)} %fusion.1.slot, bf16[16,512,256]{2,1,0:T(8,128)(2,1)S(1)} %get-tuple-element.68.spread, bf16[16,768,256]{2,1,0:T(8,128)(2,1)} %finish.5.moved, ...), custom_call_target="tpu_custom_call", output_to_operand_aliasing={{}: (3, {})} | custom-call | flops 4600000000 | bytes 12000000 | tf_op jit(solution)/shard_map/finish/pallas_call | solution.py:423
  116.3 3.7 %finish.7 = bf16[16,768,256]{2,1,0:T(8,128)(2,1)} custom-call(s32[20]{0:T(128)S(1)} %concatenate.17.meta, s32[16,256]{1,0:T(8,128)S(1)} %fusion.1.slot, bf16[16,512,256]{2,1,0:T(8,128)(2,1)S(1)} %get-tuple-element.68.spread, bf16[16,768,256]{2,1,0:T(8,128)(2,1)} %finish.6.moved, ...), custom_call_target="tpu_custom_call", output_to_operand_aliasing={{}: (3, {})} | custom-call | flops 2300000000 | bytes 6000000 | tf_op jit(solution)/shard_map/finish/pallas_call | solution.py:423
  (86 shorter events, 33.7 us)
Async XLA Ops:
  2.0 14.7 %collective-permute-start.2 = (bf16[2,208,256]{2,1,0:T(8,128)(2,1)S(1)}, bf16[2,208,256]{2,1,0:T(8,128)(2,1)S(1)}, u32[]{:S(2)}, u32[]{:S(2)}) collective-permute-start(bf16[2,208,256]{2,1,0:T(8,128)(2,1)S(1)} %pad_maximum_fusion), channel_id=1, source_target_pairs={{0,1},{2,3},{4,5},{6,7},{1,0},{3,2},{5,4},{7,6},{8,9},{10,11},{12,... | collective-permute-start | bytes 638984 | tf_op jit(solution)/shard_map/ppermute | solution.py:447
  2.6 14.1 %collective-permute-start.3 = (bf16[2,208,256]{2,1,0:T(8,128)(2,1)S(1)}, bf16[2,208,256]{2,1,0:T(8,128)(2,1)S(1)}, u32[]{:S(2)}, u32[]{:S(2)}) collective-permute-start(bf16[2,208,256]{2,1,0:T(8,128)(2,1)S(1)} %pad_maximum_fusion.1), channel_id=1, source_target_pairs={{1,2},{3,4},{5,6},{2,1},{4,3},{6,5},{9,10},{11,12},{13,14},{10,9},... | collective-permute-start | bytes 638984 | tf_op jit(solution)/shard_map/ppermute | solution.py:447
  12.0 19.7 %collective-permute-start = (bf16[2,576,256]{2,1,0:T(8,128)(2,1)S(1)}, bf16[2,576,256]{2,1,0:T(8,128)(2,1)S(1)}, u32[]{:S(2)}, u32[]{:S(2)}) collective-permute-start(bf16[2,576,256]{2,1,0:T(8,128)(2,1)S(1)} %get-tuple-element.52), channel_id=1, source_target_pairs={{0,1},{2,3},{4,5},{6,7},{1,0},{3,2},{5,4},{7,6},{8,9},{10,11},{12,... | collective-permute-start | bytes 1769480 | tf_op jit(solution)/shard_map/ppermute | solution.py:447
  15.9 15.8 %collective-permute-start.1 = (bf16[2,576,256]{2,1,0:T(8,128)(2,1)S(1)}, bf16[2,576,256]{2,1,0:T(8,128)(2,1)S(1)}, u32[]{:S(2)}, u32[]{:S(2)}) collective-permute-start(bf16[2,576,256]{2,1,0:T(8,128)(2,1)S(1)} %get-tuple-element.53), channel_id=1, source_target_pairs={{1,2},{3,4},{5,6},{2,1},{4,3},{6,5},{9,10},{11,12},{13,14},{10,9},... | collective-permute-start | bytes 1769480 | tf_op jit(solution)/shard_map/ppermute | solution.py:447
  28.1 12.8 %collective-permute-start.7 = (bf16[192,512]{1,0:T(8,128)(2,1)S(1)}, bf16[192,512]{1,0:T(8,128)(2,1)S(1)}, u32[]{:S(2)}, u32[]{:S(2)}) collective-permute-start(bf16[192,512]{1,0:T(8,128)(2,1)S(1)} %get-tuple-element.61), channel_id=1, source_target_pairs={{0,8},{8,0},{16,24},{24,16},{1,9},{9,1},{17,25},{25,17},{2,10},{10... | collective-permute-start | bytes 589832 | tf_op jit(solution)/shard_map/ppermute | solution.py:515
  29.7 11.7 %collective-permute-start.8 = (bf16[192,512]{1,0:T(8,128)(2,1)S(1)}, bf16[192,512]{1,0:T(8,128)(2,1)S(1)}, u32[]{:S(2)}, u32[]{:S(2)}) collective-permute-start(bf16[192,512]{1,0:T(8,128)(2,1)S(1)} %get-tuple-element.62), channel_id=1, source_target_pairs={{0,16},{8,24},{16,0},{24,8},{1,17},{9,25},{17,1},{25,9},{2,18},{10... | collective-permute-start | bytes 589832 | tf_op jit(solution)/shard_map/ppermute | solution.py:515
  37.8 13.8 %collective-permute-start.4 = (bf16[192,512]{1,0:T(8,128)(2,1)S(1)}, bf16[192,512]{1,0:T(8,128)(2,1)S(1)}, u32[]{:S(2)}, u32[]{:S(2)}) collective-permute-start(bf16[192,512]{1,0:T(8,128)(2,1)S(1)} %get-tuple-element.57), channel_id=1, source_target_pairs={{0,8},{8,0},{16,24},{24,16},{1,9},{9,1},{17,25},{25,17},{2,10},{10... | collective-permute-start | bytes 589832 | tf_op jit(solution)/shard_map/ppermute | solution.py:515
  39.4 12.8 %collective-permute-start.5 = (bf16[192,512]{1,0:T(8,128)(2,1)S(1)}, bf16[192,512]{1,0:T(8,128)(2,1)S(1)}, u32[]{:S(2)}, u32[]{:S(2)}) collective-permute-start(bf16[192,512]{1,0:T(8,128)(2,1)S(1)} %get-tuple-element.58), channel_id=1, source_target_pairs={{0,16},{8,24},{16,0},{24,8},{1,17},{9,25},{17,1},{25,9},{2,18},{10... | collective-permute-start | bytes 589832 | tf_op jit(solution)/shard_map/ppermute | solution.py:515
  40.9 11.2 %collective-permute-start.6 = (bf16[192,512]{1,0:T(8,128)(2,1)S(1)}, bf16[192,512]{1,0:T(8,128)(2,1)S(1)}, u32[]{:S(2)}, u32[]{:S(2)}) collective-permute-start(bf16[192,512]{1,0:T(8,128)(2,1)S(1)} %get-tuple-element.59), channel_id=1, source_target_pairs={{0,24},{8,16},{16,8},{24,0},{1,25},{9,17},{17,9},{25,1},{2,26},{10... | collective-permute-start | bytes 589832 | tf_op jit(solution)/shard_map/ppermute | solution.py:515
  48.6 14.0 %collective-permute-start.13 = (bf16[192,512]{1,0:T(8,128)(2,1)S(1)}, bf16[192,512]{1,0:T(8,128)(2,1)S(1)}, u32[]{:S(2)}, u32[]{:S(2)}) collective-permute-start(bf16[192,512]{1,0:T(8,128)(2,1)S(1)} %get-tuple-element.76), channel_id=1, source_target_pairs={{0,8},{8,0},{16,24},{24,16},{1,9},{9,1},{17,25},{25,17},{2,10},{10... | collective-permute-start | bytes 589832 | tf_op jit(solution)/shard_map/ppermute | solution.py:515
  50.1 21.8 %collective-permute-start.14 = (bf16[192,512]{1,0:T(8,128)(2,1)S(1)}, bf16[192,512]{1,0:T(8,128)(2,1)S(1)}, u32[]{:S(2)}, u32[]{:S(2)}) collective-permute-start(bf16[192,512]{1,0:T(8,128)(2,1)S(1)} %get-tuple-element.77), channel_id=1, source_target_pairs={{0,16},{8,24},{16,0},{24,8},{1,17},{9,25},{17,1},{25,9},{2,18},{10... | collective-permute-start | bytes 589832 | tf_op jit(solution)/shard_map/ppermute | solution.py:515
  51.7 20.3 %collective-permute-start.15 = (bf16[192,512]{1,0:T(8,128)(2,1)S(1)}, bf16[192,512]{1,0:T(8,128)(2,1)S(1)}, u32[]{:S(2)}, u32[]{:S(2)}) collective-permute-start(bf16[192,512]{1,0:T(8,128)(2,1)S(1)} %get-tuple-element.78), channel_id=1, source_target_pairs={{0,24},{8,16},{16,8},{24,0},{1,25},{9,17},{17,9},{25,1},{2,26},{10... | collective-permute-start | bytes 589832 | tf_op jit(solution)/shard_map/ppermute | solution.py:515
  59.5 14.1 %collective-permute-start.10 = (bf16[192,512]{1,0:T(8,128)(2,1)S(1)}, bf16[192,512]{1,0:T(8,128)(2,1)S(1)}, u32[]{:S(2)}, u32[]{:S(2)}) collective-permute-start(bf16[192,512]{1,0:T(8,128)(2,1)S(1)} %get-tuple-element.72), channel_id=1, source_target_pairs={{0,8},{8,0},{16,24},{24,16},{1,9},{9,1},{17,25},{25,17},{2,10},{10... | collective-permute-start | bytes 589832 | tf_op jit(solution)/shard_map/ppermute | solution.py:515
  61.1 12.5 %collective-permute-start.11 = (bf16[192,512]{1,0:T(8,128)(2,1)S(1)}, bf16[192,512]{1,0:T(8,128)(2,1)S(1)}, u32[]{:S(2)}, u32[]{:S(2)}) collective-permute-start(bf16[192,512]{1,0:T(8,128)(2,1)S(1)} %get-tuple-element.73), channel_id=1, source_target_pairs={{0,16},{8,24},{16,0},{24,8},{1,17},{9,25},{17,1},{25,9},{2,18},{10... | collective-permute-start | bytes 589832 | tf_op jit(solution)/shard_map/ppermute | solution.py:515
  62.6 11.0 %collective-permute-start.12 = (bf16[192,512]{1,0:T(8,128)(2,1)S(1)}, bf16[192,512]{1,0:T(8,128)(2,1)S(1)}, u32[]{:S(2)}, u32[]{:S(2)}) collective-permute-start(bf16[192,512]{1,0:T(8,128)(2,1)S(1)} %get-tuple-element.74), channel_id=1, source_target_pairs={{0,24},{8,16},{16,8},{24,0},{1,25},{9,17},{17,9},{25,1},{2,26},{10... | collective-permute-start | bytes 589832 | tf_op jit(solution)/shard_map/ppermute | solution.py:515
  77.1 10.7 %collective-permute-start.16 = (bf16[128,512]{1,0:T(8,128)(2,1)S(1)}, bf16[128,512]{1,0:T(8,128)(2,1)S(1)}, u32[]{:S(2)}, u32[]{:S(2)}) collective-permute-start(bf16[128,512]{1,0:T(8,128)(2,1)S(1)} %get-tuple-element.81), channel_id=1, source_target_pairs={{0,8},{8,0},{16,24},{24,16},{1,9},{9,1},{17,25},{25,17},{2,10},{10... | collective-permute-start | bytes 393224 | tf_op jit(solution)/shard_map/ppermute | solution.py:534
  84.7 14.5 %collective-permute-start.19 = (bf16[256,512]{1,0:T(8,128)(2,1)S(1)}, bf16[256,512]{1,0:T(8,128)(2,1)S(1)}, u32[]{:S(2)}, u32[]{:S(2)}) collective-permute-start(bf16[256,512]{1,0:T(8,128)(2,1)S(1)} %get-tuple-element.86), channel_id=1, source_target_pairs={{0,8},{8,0},{16,24},{24,16},{1,9},{9,1},{17,25},{25,17},{2,10},{10... | collective-permute-start | bytes 786440 | tf_op jit(solution)/shard_map/ppermute | solution.py:534
  86.2 13.5 %collective-permute-start.20 = (bf16[256,512]{1,0:T(8,128)(2,1)S(1)}, bf16[256,512]{1,0:T(8,128)(2,1)S(1)}, u32[]{:S(2)}, u32[]{:S(2)}) collective-permute-start(bf16[256,512]{1,0:T(8,128)(2,1)S(1)} %get-tuple-element.87), channel_id=1, source_target_pairs={{0,16},{8,24},{16,0},{24,8},{1,17},{9,25},{17,1},{25,9},{2,18},{10... | collective-permute-start | bytes 786440 | tf_op jit(solution)/shard_map/ppermute | solution.py:534
  87.8 12.8 %collective-permute-start.21 = (bf16[256,512]{1,0:T(8,128)(2,1)S(1)}, bf16[256,512]{1,0:T(8,128)(2,1)S(1)}, u32[]{:S(2)}, u32[]{:S(2)}) collective-permute-start(bf16[256,512]{1,0:T(8,128)(2,1)S(1)} %get-tuple-element.88), channel_id=1, source_target_pairs={{0,24},{8,16},{16,8},{24,0},{1,25},{9,17},{17,9},{25,1},{2,26},{10... | collective-permute-start | bytes 786440 | tf_op jit(solution)/shard_map/ppermute | solution.py:534
  92.2 17.4 %collective-permute-start.22 = (bf16[256,512]{1,0:T(8,128)(2,1)S(1)}, bf16[256,512]{1,0:T(8,128)(2,1)S(1)}, u32[]{:S(2)}, u32[]{:S(2)}) collective-permute-start(bf16[256,512]{1,0:T(8,128)(2,1)S(1)} %get-tuple-element.90), channel_id=1, source_target_pairs={{0,8},{8,0},{16,24},{24,16},{1,9},{9,1},{17,25},{25,17},{2,10},{10... | collective-permute-start | bytes 786440 | tf_op jit(solution)/shard_map/ppermute | solution.py:534
  93.8 17.4 %collective-permute-start.23 = (bf16[256,512]{1,0:T(8,128)(2,1)S(1)}, bf16[256,512]{1,0:T(8,128)(2,1)S(1)}, u32[]{:S(2)}, u32[]{:S(2)}) collective-permute-start(bf16[256,512]{1,0:T(8,128)(2,1)S(1)} %get-tuple-element.91), channel_id=1, source_target_pairs={{0,16},{8,24},{16,0},{24,8},{1,17},{9,25},{17,1},{25,9},{2,18},{10... | collective-permute-start | bytes 786440 | tf_op jit(solution)/shard_map/ppermute | solution.py:534
  99.2 12.6 %collective-permute-start.24 = (bf16[256,512]{1,0:T(8,128)(2,1)S(1)}, bf16[256,512]{1,0:T(8,128)(2,1)S(1)}, u32[]{:S(2)}, u32[]{:S(2)}) collective-permute-start(bf16[256,512]{1,0:T(8,128)(2,1)S(1)} %get-tuple-element.92), channel_id=1, source_target_pairs={{0,24},{8,16},{16,8},{24,0},{1,25},{9,17},{17,9},{25,1},{2,26},{10... | collective-permute-start | bytes 786440 | tf_op jit(solution)/shard_map/ppermute | solution.py:534
  102.9 13.3 %collective-permute-start.25 = (bf16[128,512]{1,0:T(8,128)(2,1)S(1)}, bf16[128,512]{1,0:T(8,128)(2,1)S(1)}, u32[]{:S(2)}, u32[]{:S(2)}) collective-permute-start(bf16[128,512]{1,0:T(8,128)(2,1)S(1)} %get-tuple-element.94), channel_id=1, source_target_pairs={{0,8},{8,0},{16,24},{24,16},{1,9},{9,1},{17,25},{25,17},{2,10},{10... | collective-permute-start | bytes 393224 | tf_op jit(solution)/shard_map/ppermute | solution.py:534
  104.5 11.8 %collective-permute-start.26 = (bf16[128,512]{1,0:T(8,128)(2,1)S(1)}, bf16[128,512]{1,0:T(8,128)(2,1)S(1)}, u32[]{:S(2)}, u32[]{:S(2)}) collective-permute-start(bf16[128,512]{1,0:T(8,128)(2,1)S(1)} %get-tuple-element.95), channel_id=1, source_target_pairs={{0,16},{8,24},{16,0},{24,8},{1,17},{9,25},{17,1},{25,9},{2,18},{10... | collective-permute-start | bytes 393224 | tf_op jit(solution)/shard_map/ppermute | solution.py:534
  (11 other events, 89.2 us)

commit v3 on v2

--- a/solution.py
+++ b/solution.py
@@ -37,40 +37,46 @@
     return pltpu.CompilerParams(vmem_limit_bytes=mib * MIB)
 
 
-def mark_kernel(rows, ahead, meta, slot_t, pattern, act, onehot, passed, across, beyond, sem):
+def mark_kernel(rows, meta, slot_t, pattern, ae, an, top, bottom, onehot, passed, ae_out, an_out, across, beyond):
     even = meta[3 + rows] == 0
-    copies = []
-    for i, (top, far) in enumerate(((even, across), (jnp.logical_not(even), beyond))):
-        first = jnp.where(top, rows - 2, 0)
-        copies.append(pltpu.make_async_copy(act.at[pl.ds(first, 2), ahead:, :], far, sem.at[i]))
-        copies[-1].start()
+
+    @pl.when(even)
+    def rising():
+        across[...] = top[...]
+        beyond[...] = bottom[...]
+
+    @pl.when(jnp.logical_not(even))
+    def falling():
+        across[...] = bottom[...]
+        beyond[...] = top[...]
+
     passed[...] = pattern[...]
+    ae_out[...] = jnp.broadcast_to(ae[...], ae_out.shape)
+    an_out[...] = jnp.broadcast_to(an[...], an_out.shape)
     lanes = lax.broadcasted_iota(jnp.int32, onehot.shape[1:], 1)
     for r in range(rows):
         onehot[r] = jnp.where(slot_t[:, r:r + 1] - meta[3 + r] == lanes, 1.0, 0.0).astype(jnp.bfloat16)
-    for copy in copies:
-        copy.wait()
-
-
-def mark(meta, slot_t, pattern, action, ahead):
-    rows, comps, lon = action.shape
-    vmem = pl.BlockSpec(memory_space=pltpu.VMEM)
-    far = jax.ShapeDtypeStruct((2, comps - ahead, lon), jnp.bfloat16)
+
+
+def mark(meta, slot_t, pattern, ae, an, top, bottom):
+    lon, rows = slot_t.shape
+    vmem = pl.BlockSpec(memory_space=pltpu.VMEM)
     return pl.pallas_call(
-        functools.partial(mark_kernel, rows, ahead),
-        in_specs=[pl.BlockSpec(memory_space=pltpu.SMEM), vmem, vmem, pl.BlockSpec(memory_space=pl.ANY)],
-        out_specs=[vmem] * 4,
+        functools.partial(mark_kernel, rows),
+        in_specs=[pl.BlockSpec(memory_space=pltpu.SMEM)] + [vmem] * 6,
+        out_specs=[vmem] * 6,
         out_shape=[
             jax.ShapeDtypeStruct((rows, lon, WINDOW), jnp.bfloat16),
             jax.ShapeDtypeStruct(pattern.shape, pattern.dtype),
-            far,
-            far,
+            jax.ShapeDtypeStruct(ae.shape, ae.dtype),
+            jax.ShapeDtypeStruct(an.shape, an.dtype),
+            jax.ShapeDtypeStruct(top.shape, top.dtype),
+            jax.ShapeDtypeStruct(top.shape, top.dtype),
         ],
-        scratch_shapes=[pltpu.SemaphoreType.DMA((2,))],
         compiler_params=params(),
         cost_estimate=cost(0.2),
         name="mark",
-    )(meta, slot_t, pattern, action)
+    )(meta, slot_t, pattern, ae, an, top, bottom)
 
 
 def setup_kernel(rows, meta, slot, pattern, table, after, spread, sel, tt):
@@ -78,14 +84,15 @@
     depths = lax.broadcasted_iota(jnp.int32, (WINDOW, lon), 0)
     for r in range(rows):
         spread[r] = jnp.where(slot[r:r + 1, :] - meta[3 + r] == depths, 1.0, 0.0).astype(jnp.bfloat16)
-    columns = [jnp.broadcast_to(pattern[:, j:j + 1], (ND, 128)) for j in range(pattern.shape[1])]
-    which = lax.broadcasted_iota(jnp.int32, (ND, 128), 1) // NF
-    for t in range(ND * NF // 128):
-        target = which + t * (128 // NF)
-        hit = columns[0] == target
-        for column in columns[1:]:
-            hit = hit | (column == target)
-        sel[:, t * 128:(t + 1) * 128] = jnp.where(hit, 1.0, 0.0)
+    target = lax.broadcasted_iota(jnp.int32, (ND, 128), 1)
+    hit = pattern[:, 0:1] == target
+    for j in range(1, pattern.shape[1]):
+        hit = hit | (pattern[:, j:j + 1] == target)
+    chosen = jnp.where(hit, 1.0, 0.0).astype(jnp.bfloat16)
+    block = lax.broadcasted_iota(jnp.int32, (128, ND * NF), 1) // NF
+    owner = lax.broadcasted_iota(jnp.int32, (128, ND * NF), 0)
+    widen = jnp.where(block == owner, 1.0, 0.0).astype(jnp.bfloat16)
+    sel[...] = jnp.dot(chosen, widen, preferred_element_type=jnp.float32)
     for odd in range(2):
         for t in range(ND // 2):
             pair = jnp.concatenate(
@@ -499,7 +506,9 @@
     ]).astype(jnp.int32)
     slot_t = slot.T
 
-    onehot, pattern, across, beyond = mark(meta, slot_t, pattern, action, ahead)
+    onehot, pattern, ae, an, across, beyond = mark(
+        meta, slot_t, pattern, ae, an, action[rows - 2:, ahead:], action[:2, ahead:]
+    )
     far = swap(across, 0), swap(beyond, 1)
 
     moved, x = None, None

time: 121 us -> 113 us (0.934)
  local copies, waits for them, and re-layouts: 12.2 us -> 6.6 us
  Pallas kernels: 69.1 us -> 65.6 us
  waiting for transfers between devices: 1.77 us -> 3.59 us
    unnamed x15 -> x13, local copies, waits for them, and re-layouts: 10.6 us -> 3.62 us
    pallas_call x1, Pallas kernels: 5.65 us -> 2.57 us  [setup(): pl.pallas_call(functools.partial(setup_kernel, rows), in_specs=[pl.BlockS...]
    ppermute x12, waiting for transfers between devices: 0.03 us -> 1.67 us  [local(): lax.ppermute(packed[k], 'spec', [(i, i ^ k) for i in range(peers)])]
    slice x0 -> x1, local copies, waits for them, and re-layouts: none -> 1.33 us  [local(): action[:2, ahead:]]
  transfers between devices with their start and end apart: 28 -> 28, of which waited for: 3 -> 3; matrix products, arithmetic and copies ran while one was open for 2% -> 3% of each run, Pallas kernels for 52% -> 52%
where the time goes in v3:
time: 113 us
  Pallas kernels  65.6 us (58%)
  starting transfers between devices  34.5 us (31%)
  local copies, waits for them, and re-layouts  6.6 us (6%)
  waiting for transfers between devices  3.59 us (3%)
  other arithmetic  1.96 us (2%)
    pallas_call x4, Pallas kernels, propagate(): pl.pallas_call(functools.partial(propagate_kernel, peers, share, begin *...  26.5 us
    pallas_call x4, Pallas kernels, finish(): pl.pallas_call(functools.partial(finish_kernel, peers, share, begin * NF,...  16.1 us
    ppermute x12, starting transfers between devices, local(): lax.ppermute(renewed[k], 'spec', [(i, i ^ k) for i in range(peers)])  14.4 us
    ppermute x12, starting transfers between devices, local(): lax.ppermute(packed[k], 'spec', [(i, i ^ k) for i in range(peers)])  14.2 us
    pallas_call x4, Pallas kernels, couple(): pl.pallas_call(functools.partial(couple_kernel, peers, dirs, begin, size,...  14 us
    ppermute x4, starting transfers between devices, swap(): return lax.ppermute(array, 'tile', pairs + [(j, i) for i, j in pairs])  5.89 us
    unnamed x13, local copies, waits for them, and re-layouts  3.62 us
    pallas_call x4, Pallas kernels, weave(): pl.pallas_call(functools.partial(weave_kernel, peers, dirs, begin, size),...  3.19 us
  transfers between devices with their start and end apart: 28, of which 3 were waited for; matrix products, arithmetic and copies ran while one was open for 3% of the time, Pallas kernels for 52%

profile of v3, /device:TPU:0, one launch (start us, length us, event | category | flops | bytes accessed | tf_op | source)
XLA Modules:
  0.0 112.9 jit_solution(8421815413882933764)
XLA Ops:
  7.1 1.6 %mark.1 = (bf16[16,256,512]{2,1,0:T(8,128)(2,1)S(1)}, s32[48,24]{1,0:T(8,128)S(1)}, f32[768,128]{1,0:T(8,128)S(1)}, f32[768,128]{1,0:T(8,128)S(1)}, bf16[2,576,2...) custom-call(s32[20]{0:T(128)S(1)} %concatenate.17.meta, s32[256,16]{1,0:T(8,128)S(1)} %copy.19.slot_t, ...), custom_call_target="tpu_custom_call" | custom-call | flops 230000000 | bytes 600000 | tf_op jit(solution)/shard_map/mark/pallas_call | solution.py:64
  8.8 4.0 %collective-permute-start = (bf16[2,576,256]{2,1,0:T(8,128)(2,1)S(1)}, bf16[2,576,256]{2,1,0:T(8,128)(2,1)S(1)}, u32[]{:S(2)}, u32[]{:S(2)}) collective-permute-start(bf16[2,576,256]{2,1,0:T(8,128)(2,1)S(1)} %get-tuple-element.54), channel_id=1, source_target_pairs={{0,1},{2,3},{4,5},{6,7},{1,0},{3,2},{5,4},{7,6},{8,9},{10,11},{12,... | collective-permute-start | bytes 1769480 | tf_op jit(solution)/shard_map/ppermute | solution.py:454
  13.6 2.8 %copy-done.1 = bf16[16,768,256]{2,1,0:T(8,128)(2,1)S(1)} copy-done((bf16[16,768,256]{2,1,0:T(8,128)(2,1)S(1)}, bf16[16,768,256]{2,1,0:T(8,128)(2,1)}, u32[]{:S(2)}) %copy-start.1) | copy-done | bytes 6291480
  16.3 6.1 %propagate.4 = (bf16[16,768,256]{2,1,0:T(8,128)(2,1)}, bf16[192,512]{1,0:T(8,128)(2,1)S(1)}, bf16[192,512]{1,0:T(8,128)(2,1)S(1)}, bf16[192,512]{1,0:T(8,128)(2,1)S(1)}, bf16[192,512]{1,0:T(8,128)(2,1)S(1)}) custom-call(s32[20]{0:T(128)S(1)} %concatenate.17.meta, bf16[16,768,256]{2,1,0:T(8,128)(2,1)S(1)} %copy-done.1, ...), custom_call_target="tpu_custom_call" | custom-call | flops 7590000128 | bytes 19800000 | tf_op jit(solution)/shard_map/propagate/pallas_call | solution.py:294
  22.4 1.6 %collective-permute-start.7 = (bf16[192,512]{1,0:T(8,128)(2,1)S(1)}, bf16[192,512]{1,0:T(8,128)(2,1)S(1)}, u32[]{:S(2)}, u32[]{:S(2)}) collective-permute-start(bf16[192,512]{1,0:T(8,128)(2,1)S(1)} %get-tuple-element.65), channel_id=1, source_target_pairs={{0,8},{8,0},{16,24},{24,16},{1,9},{9,1},{17,25},{25,17},{2,10},{10... | collective-permute-start | bytes 589832 | tf_op jit(solution)/shard_map/ppermute | solution.py:524
  26.0 6.1 %propagate.5 = (bf16[16,768,256]{2,1,0:T(8,128)(2,1)}, bf16[192,512]{1,0:T(8,128)(2,1)S(1)}, bf16[192,512]{1,0:T(8,128)(2,1)S(1)}, bf16[192,512]{1,0:T(8,128)(2,1)S(1)}, bf16[192,512]{1,0:T(8,128)(2,1)S(1)}) custom-call(s32[20]{0:T(128)S(1)} %concatenate.17.meta, bf16[16,768,256]{2,1,0:T(8,128)(2,1)S(1)} %copy-done.1, ...), custom_call_target="tpu_custom_call", output_to_operand_aliasing={{0}: (11, {})} | custom-call | flops 7590000128 | bytes 19800000 | tf_op jit(solution)/shard_map/propagate/pallas_call | solution.py:294
  32.1 1.6 %collective-permute-start.4 = (bf16[192,512]{1,0:T(8,128)(2,1)S(1)}, bf16[192,512]{1,0:T(8,128)(2,1)S(1)}, u32[]{:S(2)}, u32[]{:S(2)}) collective-permute-start(bf16[192,512]{1,0:T(8,128)(2,1)S(1)} %get-tuple-element.61), channel_id=1, source_target_pairs={{0,8},{8,0},{16,24},{24,16},{1,9},{9,1},{17,25},{25,17},{2,10},{10... | collective-permute-start | bytes 589832 | tf_op jit(solution)/shard_map/ppermute | solution.py:524
  35.7 7.2 %propagate.6 = (bf16[16,768,256]{2,1,0:T(8,128)(2,1)}, bf16[192,512]{1,0:T(8,128)(2,1)S(1)}, bf16[192,512]{1,0:T(8,128)(2,1)S(1)}, bf16[192,512]{1,0:T(8,128)(2,...) custom-call(s32[20]{0:T(128)S(1)} %concatenate.17.meta, ...), custom_call_target="tpu_custom_call", output_to_operand_aliasing={{0}: (15, {})} | custom-call | flops 7590000128 | bytes 19800000 | tf_op jit(solution)/shard_map/propagate/pallas_call | solution.py:294
  42.9 1.5 %collective-permute-start.13 = (bf16[192,512]{1,0:T(8,128)(2,1)S(1)}, bf16[192,512]{1,0:T(8,128)(2,1)S(1)}, u32[]{:S(2)}, u32[]{:S(2)}) collective-permute-start(bf16[192,512]{1,0:T(8,128)(2,1)S(1)} %get-tuple-element.80), channel_id=1, source_target_pairs={{0,8},{8,0},{16,24},{24,16},{1,9},{9,1},{17,25},{25,17},{2,10},{10... | collective-permute-start | bytes 589832 | tf_op jit(solution)/shard_map/ppermute | solution.py:524
  44.4 1.5 %collective-permute-start.14 = (bf16[192,512]{1,0:T(8,128)(2,1)S(1)}, bf16[192,512]{1,0:T(8,128)(2,1)S(1)}, u32[]{:S(2)}, u32[]{:S(2)}) collective-permute-start(bf16[192,512]{1,0:T(8,128)(2,1)S(1)} %get-tuple-element.81), channel_id=1, source_target_pairs={{0,16},{8,24},{16,0},{24,8},{1,17},{9,25},{17,1},{25,9},{2,18},{10... | collective-permute-start | bytes 589832 | tf_op jit(solution)/shard_map/ppermute | solution.py:524
  46.4 7.2 %propagate.7 = (bf16[16,768,256]{2,1,0:T(8,128)(2,1)}, bf16[192,512]{1,0:T(8,128)(2,1)S(1)}, bf16[192,512]{1,0:T(8,128)(2,1)S(1)}, bf16[192,512]{1,0:T(8,128)(2,...) custom-call(s32[20]{0:T(128)S(1)} %concatenate.17.meta, ...), custom_call_target="tpu_custom_call", output_to_operand_aliasing={{0}: (15, {}), {5}: (16, {})} | custom-call | flops 7590000128 | bytes 19800000 | tf_op jit(solution)/shard_map/propagate/pallas_call | solution.py:294
  53.6 1.6 %collective-permute-start.10 = (bf16[192,512]{1,0:T(8,128)(2,1)S(1)}, bf16[192,512]{1,0:T(8,128)(2,1)S(1)}, u32[]{:S(2)}, u32[]{:S(2)}) collective-permute-start(bf16[192,512]{1,0:T(8,128)(2,1)S(1)} %get-tuple-element.76), channel_id=1, source_target_pairs={{0,8},{8,0},{16,24},{24,16},{1,9},{9,1},{17,25},{25,17},{2,10},{10... | collective-permute-start | bytes 589832 | tf_op jit(solution)/shard_map/ppermute | solution.py:524
  57.2 2.6 %setup.1 = (bf16[16,512,256]{2,1,0:T(8,128)(2,1)S(1)}, f32[48,3072]{1,0:T(8,128)S(1)}, bf16[2,64,6144]{2,1,0:T(8,128)(2,1)S(1)}) custom-call(s32[20]{0:T(128)S(1)} %concatenate.17.meta, s32[16,256]{1,0:T(8,128)S(1)} %fusion.1.slot, s32[48,24]{1,0:T(8,128)S(1)} %get-tuple-element.53.pattern, bf16[48,64,64]{2,1,0:T(8,128)(2,1)S(1)} %copy-done, ...), custom_call_target="tpu_custom_call" | custom-call | flops 230000000 | bytes 600000 | tf_op jit(solution)/shard_map/setup/pallas_call | solution.py:109
  63.0 1.6 %collect.1.rest_4_ = bf16[3072,512]{1,0:T(8,128)(2,1)S(1)} custom-call(s32[20]{0:T(128)S(1)} %concatenate.17.meta, bf16[192,512]{1,0:T(8,128)(2,1)S(1)} %get-tuple-element.79.rest_0_, bf16[192,512]{1,0:T(8,128)(2,1)S(1)} %collective-permute-done.13.rest_1_, bf16[192,512]{1,0:T(8,128)(2,1)S(1)} %collective-permute-done.14.rest_2_, ...), custom_call_target="tpu_custom_call", output_to_operand_aliasing={{}: (5, {})} | custom-call | flops 230000000 | bytes 600000 | tf_op jit(solution)/shard_map/collect/pallas_call | solution.py:329
  64.7 1.6 %collective-permute-done.11.rest_2_ = bf16[192,512]{1,0:T(8,128)(2,1)S(1)} collective-permute-done((bf16[192,512]{1,0:T(8,128)(2,1)S(1)}, bf16[192,512]{1,0:T(8,128)(2,1)S(1)}, u32[]{:S(2)}, u32[]{:S(2)}) %collective-permute-start.11) | collective-permute-done | bytes 196640 | tf_op jit(solution)/shard_map/ppermute | solution.py:524
  66.3 3.6 %couple.4 = (bf16[128,512]{1,0:T(8,128)(2,1)S(1)}, bf16[128,512]{1,0:T(8,128)(2,1)S(1)}, bf16[128,512]{1,0:T(8,128)(2,1)S(1)}, bf16[128,512]{1,0:T(8,128)(2,1)S(1)}, bf16[3072,512]{1,0:T(8,128)(2,1)S(1)}) custom-call(s32[20]{0:T(128)S(1)} %concatenate.17.meta, bf16[512,3072]{1,0:T(8,128)(2,1)S(1)} %weave.4.w, ...), custom_call_target="tpu_custom_call", output_to_operand_aliasing={{4}: (6, {})} | custom-call | flops 2300000000 | bytes 6000000 | tf_op jit(solution)/shard_map/couple/pallas_call | solution.py:377
  73.5 4.0 %couple.5 = (bf16[256,512]{1,0:T(8,128)(2,1)S(1)}, bf16[256,512]{1,0:T(8,128)(2,1)S(1)}, bf16[256,512]{1,0:T(8,128)(2,1)S(1)}, bf16[256,512]{1,0:T(8,128)(2,1)S(1)}) custom-call(s32[20]{0:T(128)S(1)} %concatenate.17.meta, bf16[1024,3072]{1,0:T(8,128)(2,1)S(1)} %weave.5.w, bf16[3072,512]{1,0:T(8,128)(2,1)S(1)} %get-tuple-element.88.rest_0_, ...), custom_call_target="tpu_custom_call" | custom-call | flops 4600000000 | bytes 12000000 | tf_op jit(solution)/shard_map/couple/pallas_call | solution.py:377
  81.1 4.0 %couple.6 = (bf16[256,512]{1,0:T(8,128)(2,1)S(1)}, bf16[256,512]{1,0:T(8,128)(2,1)S(1)}, bf16[256,512]{1,0:T(8,128)(2,1)S(1)}, bf16[256,512]{1,0:T(8,128)(2,1)S(1)}) custom-call(s32[20]{0:T(128)S(1)} %concatenate.17.meta, bf16[1024,3072]{1,0:T(8,128)(2,1)S(1)} %weave.6.w, bf16[3072,512]{1,0:T(8,128)(2,1)S(1)} %get-tuple-element.88.rest_0_, ...), custom_call_target="tpu_custom_call" | custom-call | flops 4600000000 | bytes 12000000 | tf_op jit(solution)/shard_map/couple/pallas_call | solution.py:377
  87.2 3.6 %finish.4.moved = bf16[16,768,256]{2,1,0:T(8,128)(2,1)} custom-call(s32[20]{0:T(128)S(1)} %concatenate.17.meta, s32[16,256]{1,0:T(8,128)S(1)} %fusion.1.slot, bf16[16,512,256]{2,1,0:T(8,128)(2,1)S(1)} %get-tuple-element.72.spread, bf16[16,768,256]{2,1,0:T(8,128)(2,1)} %get-tuple-element.73.moved, ...), custom_call_target="tpu_custom_call", output_to_operand_aliasing={{}: (3, {})} | custom-call | flops 2300000000 | bytes 6000000 | tf_op jit(solution)/shard_map/finish/pallas_call | solution.py:430
  93.4 2.4 %couple.7 = (bf16[128,512]{1,0:T(8,128)(2,1)S(1)}, bf16[128,512]{1,0:T(8,128)(2,1)S(1)}, bf16[128,512]{1,0:T(8,128)(2,1)S(1)}, bf16[128,512]{1,0:T(8,128)(2,1)S(1)}) custom-call(s32[20]{0:T(128)S(1)} %concatenate.17.meta, bf16[512,3072]{1,0:T(8,128)(2,1)S(1)} %weave.7.w, bf16[3072,512]{1,0:T(8,128)(2,1)S(1)} %get-tuple-element.88.rest_0_, ...), custom_call_target="tpu_custom_call" | custom-call | flops 2300000000 | bytes 6000000 | tf_op jit(solution)/shard_map/couple/pallas_call | solution.py:377
  97.6 4.4 %finish.5.moved = bf16[16,768,256]{2,1,0:T(8,128)(2,1)} custom-call(s32[20]{0:T(128)S(1)} %concatenate.17.meta, s32[16,256]{1,0:T(8,128)S(1)} %fusion.1.slot, bf16[16,512,256]{2,1,0:T(8,128)(2,1)S(1)} %get-tuple-element.72.spread, bf16[16,768,256]{2,1,0:T(8,128)(2,1)} %finish.4.moved, ...), custom_call_target="tpu_custom_call", output_to_operand_aliasing={{}: (3, {})} | custom-call | flops 4600000000 | bytes 12000000 | tf_op jit(solution)/shard_map/finish/pallas_call | solution.py:430
  102.0 1.8 %collective-permute-start.27 = (bf16[128,512]{1,0:T(8,128)(2,1)S(1)}, bf16[128,512]{1,0:T(8,128)(2,1)S(1)}, u32[]{:S(2)}, u32[]{:S(2)}) collective-permute-start(bf16[128,512]{1,0:T(8,128)(2,1)S(1)} %get-tuple-element.100), channel_id=1, source_target_pairs={{0,24},{8,16},{16,8},{24,0},{1,25},{9,17},{17,9},{25,1},{2,26},{10... | collective-permute-start | bytes 393224 | tf_op jit(solution)/shard_map/ppermute | solution.py:543
  104.7 4.4 %finish.6.moved = bf16[16,768,256]{2,1,0:T(8,128)(2,1)} custom-call(s32[20]{0:T(128)S(1)} %concatenate.17.meta, s32[16,256]{1,0:T(8,128)S(1)} %fusion.1.slot, bf16[16,512,256]{2,1,0:T(8,128)(2,1)S(1)} %get-tuple-element.72.spread, bf16[16,768,256]{2,1,0:T(8,128)(2,1)} %finish.5.moved, ...), custom_call_target="tpu_custom_call", output_to_operand_aliasing={{}: (3, {})} | custom-call | flops 4600000000 | bytes 12000000 | tf_op jit(solution)/shard_map/finish/pallas_call | solution.py:430
  109.1 3.7 %finish.7 = bf16[16,768,256]{2,1,0:T(8,128)(2,1)} custom-call(s32[20]{0:T(128)S(1)} %concatenate.17.meta, s32[16,256]{1,0:T(8,128)S(1)} %fusion.1.slot, bf16[16,512,256]{2,1,0:T(8,128)(2,1)S(1)} %get-tuple-element.72.spread, bf16[16,768,256]{2,1,0:T(8,128)(2,1)} %finish.6.moved, ...), custom_call_target="tpu_custom_call", output_to_operand_aliasing={{}: (3, {})} | custom-call | flops 2300000000 | bytes 6000000 | tf_op jit(solution)/shard_map/finish/pallas_call | solution.py:430
  (86 shorter events, 32.0 us)
Async XLA Ops:
  2.0 11.5 %collective-permute-start.2 = (bf16[2,208,256]{2,1,0:T(8,128)(2,1)S(1)}, bf16[2,208,256]{2,1,0:T(8,128)(2,1)S(1)}, u32[]{:S(2)}, u32[]{:S(2)}) collective-permute-start(bf16[2,208,256]{2,1,0:T(8,128)(2,1)S(1)} %pad_maximum_fusion), channel_id=1, source_target_pairs={{0,1},{2,3},{4,5},{6,7},{1,0},{3,2},{5,4},{7,6},{8,9},{10,11},{12,... | collective-permute-start | bytes 638984 | tf_op jit(solution)/shard_map/ppermute | solution.py:454
  2.6 11.0 %collective-permute-start.3 = (bf16[2,208,256]{2,1,0:T(8,128)(2,1)S(1)}, bf16[2,208,256]{2,1,0:T(8,128)(2,1)S(1)}, u32[]{:S(2)}, u32[]{:S(2)}) collective-permute-start(bf16[2,208,256]{2,1,0:T(8,128)(2,1)S(1)} %pad_maximum_fusion.1), channel_id=1, source_target_pairs={{1,2},{3,4},{5,6},{2,1},{4,3},{6,5},{9,10},{11,12},{13,14},{10,9},... | collective-permute-start | bytes 638984 | tf_op jit(solution)/shard_map/ppermute | solution.py:454
  8.8 17.2 %collective-permute-start = (bf16[2,576,256]{2,1,0:T(8,128)(2,1)S(1)}, bf16[2,576,256]{2,1,0:T(8,128)(2,1)S(1)}, u32[]{:S(2)}, u32[]{:S(2)}) collective-permute-start(bf16[2,576,256]{2,1,0:T(8,128)(2,1)S(1)} %get-tuple-element.54), channel_id=1, source_target_pairs={{0,1},{2,3},{4,5},{6,7},{1,0},{3,2},{5,4},{7,6},{8,9},{10,11},{12,... | collective-permute-start | bytes 1769480 | tf_op jit(solution)/shard_map/ppermute | solution.py:454
  12.8 13.2 %collective-permute-start.1 = (bf16[2,576,256]{2,1,0:T(8,128)(2,1)S(1)}, bf16[2,576,256]{2,1,0:T(8,128)(2,1)S(1)}, u32[]{:S(2)}, u32[]{:S(2)}) collective-permute-start(bf16[2,576,256]{2,1,0:T(8,128)(2,1)S(1)} %get-tuple-element.55), channel_id=1, source_target_pairs={{1,2},{3,4},{5,6},{2,1},{4,3},{6,5},{9,10},{11,12},{13,14},{10,9},... | collective-permute-start | bytes 1769480 | tf_op jit(solution)/shard_map/ppermute | solution.py:454
  22.4 12.8 %collective-permute-start.7 = (bf16[192,512]{1,0:T(8,128)(2,1)S(1)}, bf16[192,512]{1,0:T(8,128)(2,1)S(1)}, u32[]{:S(2)}, u32[]{:S(2)}) collective-permute-start(bf16[192,512]{1,0:T(8,128)(2,1)S(1)} %get-tuple-element.65), channel_id=1, source_target_pairs={{0,8},{8,0},{16,24},{24,16},{1,9},{9,1},{17,25},{25,17},{2,10},{10... | collective-permute-start | bytes 589832 | tf_op jit(solution)/shard_map/ppermute | solution.py:524
  24.0 11.7 %collective-permute-start.8 = (bf16[192,512]{1,0:T(8,128)(2,1)S(1)}, bf16[192,512]{1,0:T(8,128)(2,1)S(1)}, u32[]{:S(2)}, u32[]{:S(2)}) collective-permute-start(bf16[192,512]{1,0:T(8,128)(2,1)S(1)} %get-tuple-element.66), channel_id=1, source_target_pairs={{0,16},{8,24},{16,0},{24,8},{1,17},{9,25},{17,1},{25,9},{2,18},{10... | collective-permute-start | bytes 589832 | tf_op jit(solution)/shard_map/ppermute | solution.py:524
  25.5 10.2 %collective-permute-start.9 = (bf16[192,512]{1,0:T(8,128)(2,1)S(1)}, bf16[192,512]{1,0:T(8,128)(2,1)S(1)}, u32[]{:S(2)}, u32[]{:S(2)}) collective-permute-start(bf16[192,512]{1,0:T(8,128)(2,1)S(1)} %get-tuple-element.67), channel_id=1, source_target_pairs={{0,24},{8,16},{16,8},{24,0},{1,25},{9,17},{17,9},{25,1},{2,26},{10... | collective-permute-start | bytes 589832 | tf_op jit(solution)/shard_map/ppermute | solution.py:524
  32.1 13.8 %collective-permute-start.4 = (bf16[192,512]{1,0:T(8,128)(2,1)S(1)}, bf16[192,512]{1,0:T(8,128)(2,1)S(1)}, u32[]{:S(2)}, u32[]{:S(2)}) collective-permute-start(bf16[192,512]{1,0:T(8,128)(2,1)S(1)} %get-tuple-element.61), channel_id=1, source_target_pairs={{0,8},{8,0},{16,24},{24,16},{1,9},{9,1},{17,25},{25,17},{2,10},{10... | collective-permute-start | bytes 589832 | tf_op jit(solution)/shard_map/ppermute | solution.py:524
  33.7 12.8 %collective-permute-start.5 = (bf16[192,512]{1,0:T(8,128)(2,1)S(1)}, bf16[192,512]{1,0:T(8,128)(2,1)S(1)}, u32[]{:S(2)}, u32[]{:S(2)}) collective-permute-start(bf16[192,512]{1,0:T(8,128)(2,1)S(1)} %get-tuple-element.62), channel_id=1, source_target_pairs={{0,16},{8,24},{16,0},{24,8},{1,17},{9,25},{17,1},{25,9},{2,18},{10... | collective-permute-start | bytes 589832 | tf_op jit(solution)/shard_map/ppermute | solution.py:524
  35.2 11.3 %collective-permute-start.6 = (bf16[192,512]{1,0:T(8,128)(2,1)S(1)}, bf16[192,512]{1,0:T(8,128)(2,1)S(1)}, u32[]{:S(2)}, u32[]{:S(2)}) collective-permute-start(bf16[192,512]{1,0:T(8,128)(2,1)S(1)} %get-tuple-element.63), channel_id=1, source_target_pairs={{0,24},{8,16},{16,8},{24,0},{1,25},{9,17},{17,9},{25,1},{2,26},{10... | collective-permute-start | bytes 589832 | tf_op jit(solution)/shard_map/ppermute | solution.py:524
  42.9 13.8 %collective-permute-start.13 = (bf16[192,512]{1,0:T(8,128)(2,1)S(1)}, bf16[192,512]{1,0:T(8,128)(2,1)S(1)}, u32[]{:S(2)}, u32[]{:S(2)}) collective-permute-start(bf16[192,512]{1,0:T(8,128)(2,1)S(1)} %get-tuple-element.80), channel_id=1, source_target_pairs={{0,8},{8,0},{16,24},{24,16},{1,9},{9,1},{17,25},{25,17},{2,10},{10... | collective-permute-start | bytes 589832 | tf_op jit(solution)/shard_map/ppermute | solution.py:524
  44.4 18.6 %collective-permute-start.14 = (bf16[192,512]{1,0:T(8,128)(2,1)S(1)}, bf16[192,512]{1,0:T(8,128)(2,1)S(1)}, u32[]{:S(2)}, u32[]{:S(2)}) collective-permute-start(bf16[192,512]{1,0:T(8,128)(2,1)S(1)} %get-tuple-element.81), channel_id=1, source_target_pairs={{0,16},{8,24},{16,0},{24,8},{1,17},{9,25},{17,1},{25,9},{2,18},{10... | collective-permute-start | bytes 589832 | tf_op jit(solution)/shard_map/ppermute | solution.py:524
  46.0 17.1 %collective-permute-start.15 = (bf16[192,512]{1,0:T(8,128)(2,1)S(1)}, bf16[192,512]{1,0:T(8,128)(2,1)S(1)}, u32[]{:S(2)}, u32[]{:S(2)}) collective-permute-start(bf16[192,512]{1,0:T(8,128)(2,1)S(1)} %get-tuple-element.82), channel_id=1, source_target_pairs={{0,24},{8,16},{16,8},{24,0},{1,25},{9,17},{17,9},{25,1},{2,26},{10... | collective-permute-start | bytes 589832 | tf_op jit(solution)/shard_map/ppermute | solution.py:524
  53.6 11.0 %collective-permute-start.10 = (bf16[192,512]{1,0:T(8,128)(2,1)S(1)}, bf16[192,512]{1,0:T(8,128)(2,1)S(1)}, u32[]{:S(2)}, u32[]{:S(2)}) collective-permute-start(bf16[192,512]{1,0:T(8,128)(2,1)S(1)} %get-tuple-element.76), channel_id=1, source_target_pairs={{0,8},{8,0},{16,24},{24,16},{1,9},{9,1},{17,25},{25,17},{2,10},{10... | collective-permute-start | bytes 589832 | tf_op jit(solution)/shard_map/ppermute | solution.py:524
  55.2 11.1 %collective-permute-start.11 = (bf16[192,512]{1,0:T(8,128)(2,1)S(1)}, bf16[192,512]{1,0:T(8,128)(2,1)S(1)}, u32[]{:S(2)}, u32[]{:S(2)}) collective-permute-start(bf16[192,512]{1,0:T(8,128)(2,1)S(1)} %get-tuple-element.77), channel_id=1, source_target_pairs={{0,16},{8,24},{16,0},{24,8},{1,17},{9,25},{17,1},{25,9},{2,18},{10... | collective-permute-start | bytes 589832 | tf_op jit(solution)/shard_map/ppermute | solution.py:524
  71.2 9.8 %collective-permute-start.17 = (bf16[128,512]{1,0:T(8,128)(2,1)S(1)}, bf16[128,512]{1,0:T(8,128)(2,1)S(1)}, u32[]{:S(2)}, u32[]{:S(2)}) collective-permute-start(bf16[128,512]{1,0:T(8,128)(2,1)S(1)} %get-tuple-element.86), channel_id=1, source_target_pairs={{0,16},{8,24},{16,0},{24,8},{1,17},{9,25},{17,1},{25,9},{2,18},{10... | collective-permute-start | bytes 393224 | tf_op jit(solution)/shard_map/ppermute | solution.py:543
  77.5 13.4 %collective-permute-start.19 = (bf16[256,512]{1,0:T(8,128)(2,1)S(1)}, bf16[256,512]{1,0:T(8,128)(2,1)S(1)}, u32[]{:S(2)}, u32[]{:S(2)}) collective-permute-start(bf16[256,512]{1,0:T(8,128)(2,1)S(1)} %get-tuple-element.90), channel_id=1, source_target_pairs={{0,8},{8,0},{16,24},{24,16},{1,9},{9,1},{17,25},{25,17},{2,10},{10... | collective-permute-start | bytes 786440 | tf_op jit(solution)/shard_map/ppermute | solution.py:543
  78.8 13.6 %collective-permute-start.20 = (bf16[256,512]{1,0:T(8,128)(2,1)S(1)}, bf16[256,512]{1,0:T(8,128)(2,1)S(1)}, u32[]{:S(2)}, u32[]{:S(2)}) collective-permute-start(bf16[256,512]{1,0:T(8,128)(2,1)S(1)} %get-tuple-element.91), channel_id=1, source_target_pairs={{0,16},{8,24},{16,0},{24,8},{1,17},{9,25},{17,1},{25,9},{2,18},{10... | collective-permute-start | bytes 786440 | tf_op jit(solution)/shard_map/ppermute | solution.py:543
  79.6 13.8 %collective-permute-start.21 = (bf16[256,512]{1,0:T(8,128)(2,1)S(1)}, bf16[256,512]{1,0:T(8,128)(2,1)S(1)}, u32[]{:S(2)}, u32[]{:S(2)}) collective-permute-start(bf16[256,512]{1,0:T(8,128)(2,1)S(1)} %get-tuple-element.92), channel_id=1, source_target_pairs={{0,24},{8,16},{16,8},{24,0},{1,25},{9,17},{17,9},{25,1},{2,26},{10... | collective-permute-start | bytes 786440 | tf_op jit(solution)/shard_map/ppermute | solution.py:543
  85.1 16.9 %collective-permute-start.22 = (bf16[256,512]{1,0:T(8,128)(2,1)S(1)}, bf16[256,512]{1,0:T(8,128)(2,1)S(1)}, u32[]{:S(2)}, u32[]{:S(2)}) collective-permute-start(bf16[256,512]{1,0:T(8,128)(2,1)S(1)} %get-tuple-element.94), channel_id=1, source_target_pairs={{0,8},{8,0},{16,24},{24,16},{1,9},{9,1},{17,25},{25,17},{2,10},{10... | collective-permute-start | bytes 786440 | tf_op jit(solution)/shard_map/ppermute | solution.py:543
  86.4 17.4 %collective-permute-start.23 = (bf16[256,512]{1,0:T(8,128)(2,1)S(1)}, bf16[256,512]{1,0:T(8,128)(2,1)S(1)}, u32[]{:S(2)}, u32[]{:S(2)}) collective-permute-start(bf16[256,512]{1,0:T(8,128)(2,1)S(1)} %get-tuple-element.95), channel_id=1, source_target_pairs={{0,16},{8,24},{16,0},{24,8},{1,17},{9,25},{17,1},{25,9},{2,18},{10... | collective-permute-start | bytes 786440 | tf_op jit(solution)/shard_map/ppermute | solution.py:543
  90.9 13.8 %collective-permute-start.24 = (bf16[256,512]{1,0:T(8,128)(2,1)S(1)}, bf16[256,512]{1,0:T(8,128)(2,1)S(1)}, u32[]{:S(2)}, u32[]{:S(2)}) collective-permute-start(bf16[256,512]{1,0:T(8,128)(2,1)S(1)} %get-tuple-element.96), channel_id=1, source_target_pairs={{0,24},{8,16},{16,8},{24,0},{1,25},{9,17},{17,9},{25,1},{2,26},{10... | collective-permute-start | bytes 786440 | tf_op jit(solution)/shard_map/ppermute | solution.py:543
  95.8 13.3 %collective-permute-start.25 = (bf16[128,512]{1,0:T(8,128)(2,1)S(1)}, bf16[128,512]{1,0:T(8,128)(2,1)S(1)}, u32[]{:S(2)}, u32[]{:S(2)}) collective-permute-start(bf16[128,512]{1,0:T(8,128)(2,1)S(1)} %get-tuple-element.98), channel_id=1, source_target_pairs={{0,8},{8,0},{16,24},{24,16},{1,9},{9,1},{17,25},{25,17},{2,10},{10... | collective-permute-start | bytes 393224 | tf_op jit(solution)/shard_map/ppermute | solution.py:543
  96.4 12.7 %collective-permute-start.26 = (bf16[128,512]{1,0:T(8,128)(2,1)S(1)}, bf16[128,512]{1,0:T(8,128)(2,1)S(1)}, u32[]{:S(2)}, u32[]{:S(2)}) collective-permute-start(bf16[128,512]{1,0:T(8,128)(2,1)S(1)} %get-tuple-element.99), channel_id=1, source_target_pairs={{0,16},{8,24},{16,0},{24,8},{1,17},{9,25},{17,1},{25,9},{2,18},{10... | collective-permute-start | bytes 393224 | tf_op jit(solution)/shard_map/ppermute | solution.py:543
  (10 other events, 105.0 us)

commit v4 on v3

--- a/solution.py
+++ b/solution.py
@@ -37,7 +37,7 @@
     return pltpu.CompilerParams(vmem_limit_bytes=mib * MIB)
 
 
-def mark_kernel(rows, meta, slot_t, pattern, ae, an, top, bottom, onehot, passed, ae_out, an_out, across, beyond):
+def mark_kernel(rows, meta, slot_t, ae, an, top, bottom, onehot, ae_out, an_out, across, beyond):
     even = meta[3 + rows] == 0
 
     @pl.when(even)
@@ -50,7 +50,6 @@
         across[...] = bottom[...]
         beyond[...] = top[...]
 
-    passed[...] = pattern[...]
     ae_out[...] = jnp.broadcast_to(ae[...], ae_out.shape)
     an_out[...] = jnp.broadcast_to(an[...], an_out.shape)
     lanes = lax.broadcasted_iota(jnp.int32, onehot.shape[1:], 1)
@@ -58,41 +57,42 @@
         onehot[r] = jnp.where(slot_t[:, r:r + 1] - meta[3 + r] == lanes, 1.0, 0.0).astype(jnp.bfloat16)
 
 
-def mark(meta, slot_t, pattern, ae, an, top, bottom):
+def mark(meta, slot_t, ae, an, top, bottom):
     lon, rows = slot_t.shape
     vmem = pl.BlockSpec(memory_space=pltpu.VMEM)
     return pl.pallas_call(
         functools.partial(mark_kernel, rows),
-        in_specs=[pl.BlockSpec(memory_space=pltpu.SMEM)] + [vmem] * 6,
-        out_specs=[vmem] * 6,
+        in_specs=[pl.BlockSpec(memory_space=pltpu.SMEM)] + [vmem] * 5,
+        out_specs=[vmem] * 5,
         out_shape=[
             jax.ShapeDtypeStruct((rows, lon, WINDOW), jnp.bfloat16),
-            jax.ShapeDtypeStruct(pattern.shape, pattern.dtype),
             jax.ShapeDtypeStruct(ae.shape, ae.dtype),
             jax.ShapeDtypeStruct(an.shape, an.dtype),
             jax.ShapeDtypeStruct(top.shape, top.dtype),
             jax.ShapeDtypeStruct(top.shape, top.dtype),
         ],
         compiler_params=params(),
-        cost_estimate=cost(0.2),
+        cost_estimate=cost(4),
         name="mark",
-    )(meta, slot_t, pattern, ae, an, top, bottom)
-
-
-def setup_kernel(rows, meta, slot, pattern, table, after, spread, sel, tt):
+    )(meta, slot_t, ae, an, top, bottom)
+
+
+def setup_kernel(rows, meta, slot, pattern_t, table, after, spread, sel, tt):
     lon = slot.shape[1]
     depths = lax.broadcasted_iota(jnp.int32, (WINDOW, lon), 0)
     for r in range(rows):
         spread[r] = jnp.where(slot[r:r + 1, :] - meta[3 + r] == depths, 1.0, 0.0).astype(jnp.bfloat16)
-    target = lax.broadcasted_iota(jnp.int32, (ND, 128), 1)
-    hit = pattern[:, 0:1] == target
-    for j in range(1, pattern.shape[1]):
-        hit = hit | (pattern[:, j:j + 1] == target)
+    target = lax.broadcasted_iota(jnp.int32, (128, ND), 0)
+    hit = pattern_t[0:1, :] == target
+    for j in range(1, pattern_t.shape[0]):
+        hit = hit | (pattern_t[j:j + 1, :] == target)
     chosen = jnp.where(hit, 1.0, 0.0).astype(jnp.bfloat16)
     block = lax.broadcasted_iota(jnp.int32, (128, ND * NF), 1) // NF
     owner = lax.broadcasted_iota(jnp.int32, (128, ND * NF), 0)
     widen = jnp.where(block == owner, 1.0, 0.0).astype(jnp.bfloat16)
-    sel[...] = jnp.dot(chosen, widen, preferred_element_type=jnp.float32)
+    sel[...] = lax.dot_general(
+        chosen, widen, (((0,), (0,)), ((), ())), preferred_element_type=jnp.float32
+    )
     for odd in range(2):
         for t in range(ND // 2):
             pair = jnp.concatenate(
@@ -103,7 +103,7 @@
             tt[odd, :, ND * NF + t * 128:ND * NF + (t + 1) * 128] = pair
 
 
-def setup(meta, slot, pattern, table, after):
+def setup(meta, slot, pattern_t, table, after):
     rows, lon = slot.shape
     vmem = pl.BlockSpec(memory_space=pltpu.VMEM)
     return pl.pallas_call(
@@ -118,7 +118,7 @@
         compiler_params=params(),
         cost_estimate=cost(0.2),
         name="setup",
-    )(meta, slot, pattern, table, after)
+    )(meta, slot, pattern_t, table, after)
 
 
 def weave_kernel(peers, dirs, begin, size, sel, tt, after, w):
@@ -461,8 +461,8 @@
     tile = lax.axis_index("tile")
     tiles = lax.axis_size("tile")
     dirs = comps // NF
-    parts_out = split_directions(dirs, (3, 3, 3, 3))
-    parts_back = split_directions(dirs, (2, 4, 4, 2))
+    parts_out = split_directions(dirs, (4, 4, 4))
+    parts_back = split_directions(dirs, (3, 6, 3))
 
     ahead = parts_out[0] * NF
     parity = (tile % 2).astype(jnp.int32)
@@ -506,8 +506,8 @@
     ]).astype(jnp.int32)
     slot_t = slot.T
 
-    onehot, pattern, ae, an, across, beyond = mark(
-        meta, slot_t, pattern, ae, an, action[rows - 2:, ahead:], action[:2, ahead:]
+    onehot, ae, an, across, beyond = mark(
+        meta, slot_t, ae, an, action[rows - 2:, ahead:], action[:2, ahead:]
     )
     far = swap(across, 0), swap(beyond, 1)
 
@@ -526,7 +526,7 @@
         ])
         spots.append([(k, begin) for k in range(peers)])
 
-    spread, sel, tt = setup(meta, slot, pattern, table, packed[0])
+    spread, sel, tt = setup(meta, slot, pattern.T, table, packed[0])
     woven = [
         weave(sel, tt, packed[0], begin, size, peers, dirs)
         for begin, size in zip(offsets_of(parts_back), parts_back)

time: 113 us -> 106 us (0.938)
  waiting for transfers between devices: 3.59 us -> 14.7 us
  Pallas kernels: 65.6 us -> 57.8 us
  starting transfers between devices: 34.5 us -> 27.3 us
  local copies, waits for them, and re-layouts: 6.6 us -> 3 us
    ppermute x12 -> x9, waiting for transfers between devices: 1.92 us -> 8.6 us  [local(): lax.ppermute(renewed[k], 'spec', [(i, i ^ k) for i in range(peers)])]
    ppermute x12 -> x9, waiting for transfers between devices: 1.67 us -> 6.09 us  [local(): lax.ppermute(packed[k], 'spec', [(i, i ^ k) for i in range(peers)])]
    ppermute x12 -> x9, starting transfers between devices: 14.4 us -> 10.7 us  [local(): lax.ppermute(renewed[k], 'spec', [(i, i ^ k) for i in range(peers)])]
    unnamed x13 -> x12, local copies, waits for them, and re-layouts: 3.62 us -> 0.04 us
    ppermute x12 -> x9, starting transfers between devices: 14.2 us -> 10.7 us  [local(): lax.ppermute(packed[k], 'spec', [(i, i ^ k) for i in range(peers)])]
    pallas_call x4 -> x3, Pallas kernels: 16.1 us -> 13.2 us  [finish(): pl.pallas_call(functools.partial(finish_kernel, peers, share, begin * NF,...]
    pallas_call x4 -> x3, Pallas kernels: 26.5 us -> 23.8 us  [propagate(): pl.pallas_call(functools.partial(propagate_kernel, peers, share, begin *...]
    pallas_call x4 -> x3, Pallas kernels: 14 us -> 12.5 us  [couple(): pl.pallas_call(functools.partial(couple_kernel, peers, dirs, begin, size,...]
  transfers between devices with their start and end apart: 28 -> 22, of which waited for: 3 -> 4; matrix products, arithmetic and copies ran while one was open for 3% -> 3% of each run, Pallas kernels for 52% -> 48%
where the time goes in v4:
time: 106 us; the launch traced here: 105 us
  Pallas kernels  57.8 us (55%)
  starting transfers between devices  27.3 us (26%)
  waiting for transfers between devices  14.7 us (14%)
  local copies, waits for them, and re-layouts  3 us (3%)
  other arithmetic  1.97 us (2%)
    pallas_call x3, Pallas kernels, propagate(): pl.pallas_call(functools.partial(propagate_kernel, peers, share, begin *...  23.8 us
    pallas_call x3, Pallas kernels, finish(): pl.pallas_call(functools.partial(finish_kernel, peers, share, begin * NF,...  13.2 us
    pallas_call x3, Pallas kernels, couple(): pl.pallas_call(functools.partial(couple_kernel, peers, dirs, begin, size,...  12.5 us
    ppermute x9, starting transfers between devices, local(): lax.ppermute(renewed[k], 'spec', [(i, i ^ k) for i in range(peers)])  10.7 us
    ppermute x9, starting transfers between devices, local(): lax.ppermute(packed[k], 'spec', [(i, i ^ k) for i in range(peers)])  10.7 us
    ppermute x9, waiting for transfers between devices, local(): lax.ppermute(renewed[k], 'spec', [(i, i ^ k) for i in range(peers)])  8.6 us
    ppermute x9, waiting for transfers between devices, local(): lax.ppermute(packed[k], 'spec', [(i, i ^ k) for i in range(peers)])  6.09 us
    ppermute x4, starting transfers between devices, swap(): return lax.ppermute(array, 'tile', pairs + [(j, i) for i, j in pairs])  5.89 us
  transfers between devices with their start and end apart: 22, of which 4 were waited for; matrix products, arithmetic and copies ran while one was open for 3% of the time, Pallas kernels for 48%

profile of v4, /device:TPU:0, one launch (start us, length us, event | category | flops | bytes accessed | tf_op | source)
XLA Modules:
  0.0 105.4 jit_solution(9733318886148514072)
XLA Ops:
  6.4 1.6 %mark.1 = (bf16[16,256,512]{2,1,0:T(8,128)(2,1)S(1)}, f32[768,128]{1,0:T(8,128)S(1)}, f32[768,128]{1,0:T(8,128)S(1)}, bf16[2,512,256]{2,1,0:T(8,128)(2,1)S(1)}, bf16[2,512,256]{2,1,0:T(8,128)(2,1)S(1)}) custom-call(s32[20]{0:T(128)S(1)} %concatenate.17.meta, s32[256,16]{1,0:T(8,128)S(1)} %copy.15.slot_t, f32[768,128]{1,0:T(8,128)S(1)} %broadcast_in_dim.51.ae, ...), custom_call_target="tpu_custom_call" | custom-call | flops 4600000000 | bytes 12000000 | tf_op jit(solution)/shard_map/mark/pallas_call | solution.py:63
  8.0 4.0 %collective-permute-start = (bf16[2,512,256]{2,1,0:T(8,128)(2,1)S(1)}, bf16[2,512,256]{2,1,0:T(8,128)(2,1)S(1)}, u32[]{:S(2)}, u32[]{:S(2)}) collective-permute-start(bf16[2,512,256]{2,1,0:T(8,128)(2,1)S(1)} %get-tuple-element.42), channel_id=1, source_target_pairs={{0,1},{2,3},{4,5},{6,7},{1,0},{3,2},{5,4},{7,6},{8,9},{10,11},{12,... | collective-permute-start | bytes 1572872 | tf_op jit(solution)/shard_map/ppermute | solution.py:454
  12.8 7.9 %propagate.3 = (bf16[16,768,256]{2,1,0:T(8,128)(2,1)}, bf16[256,512]{1,0:T(8,128)(2,1)S(1)}, bf16[256,512]{1,0:T(8,128)(2,1)S(1)}, bf16[256,512]{1,0:T(8,128)(2,1)S(1)}, bf16[256,512]{1,0:T(8,128)(2,1)S(1)}) custom-call(s32[20]{0:T(128)S(1)} %concatenate.17.meta, bf16[16,768,256]{2,1,0:T(8,128)(2,1)S(1)} %bitcast.16, ...), custom_call_target="tpu_custom_call" | custom-call | flops 10119999488 | bytes 26400000 | tf_op jit(solution)/shard_map/propagate/pallas_call | solution.py:294
  20.7 1.6 %collective-permute-start.4 = (bf16[256,512]{1,0:T(8,128)(2,1)S(1)}, bf16[256,512]{1,0:T(8,128)(2,1)S(1)}, u32[]{:S(2)}, u32[]{:S(2)}) collective-permute-start(bf16[256,512]{1,0:T(8,128)(2,1)S(1)} %get-tuple-element.48), channel_id=1, source_target_pairs={{0,8},{8,0},{16,24},{24,16},{1,9},{9,1},{17,25},{25,17},{2,10},{10... | collective-permute-start | bytes 786440 | tf_op jit(solution)/shard_map/ppermute | solution.py:524
  22.2 1.5 %collective-permute-start.5 = (bf16[256,512]{1,0:T(8,128)(2,1)S(1)}, bf16[256,512]{1,0:T(8,128)(2,1)S(1)}, u32[]{:S(2)}, u32[]{:S(2)}) collective-permute-start(bf16[256,512]{1,0:T(8,128)(2,1)S(1)} %get-tuple-element.49), channel_id=1, source_target_pairs={{0,16},{8,24},{16,0},{24,8},{1,17},{9,25},{17,1},{25,9},{2,18},{10... | collective-permute-start | bytes 786440 | tf_op jit(solution)/shard_map/ppermute | solution.py:524
  24.3 7.9 %propagate.4 = (bf16[16,768,256]{2,1,0:T(8,128)(2,1)}, bf16[256,512]{1,0:T(8,128)(2,1)S(1)}, bf16[256,512]{1,0:T(8,128)(2,1)S(1)}, bf16[256,512]{1,0:T(8,128)(2,1)S(1)}, bf16[256,512]{1,0:T(8,128)(2,1)S(1)}) custom-call(s32[20]{0:T(128)S(1)} %concatenate.17.meta, bf16[16,768,256]{2,1,0:T(8,128)(2,1)S(1)} %bitcast.16, ...), custom_call_target="tpu_custom_call", output_to_operand_aliasing={{0}: (11, {})} | custom-call | flops 10119999488 | bytes 26400000 | tf_op jit(solution)/shard_map/propagate/pallas_call | solution.py:294
  32.1 1.6 %collective-permute-start.10 = (bf16[256,512]{1,0:T(8,128)(2,1)S(1)}, bf16[256,512]{1,0:T(8,128)(2,1)S(1)}, u32[]{:S(2)}, u32[]{:S(2)}) collective-permute-start(bf16[256,512]{1,0:T(8,128)(2,1)S(1)} %get-tuple-element.62), channel_id=1, source_target_pairs={{0,8},{8,0},{16,24},{24,16},{1,9},{9,1},{17,25},{25,17},{2,10},{10... | collective-permute-start | bytes 786440 | tf_op jit(solution)/shard_map/ppermute | solution.py:524
  33.7 1.5 %collective-permute-start.11 = (bf16[256,512]{1,0:T(8,128)(2,1)S(1)}, bf16[256,512]{1,0:T(8,128)(2,1)S(1)}, u32[]{:S(2)}, u32[]{:S(2)}) collective-permute-start(bf16[256,512]{1,0:T(8,128)(2,1)S(1)} %get-tuple-element.63), channel_id=1, source_target_pairs={{0,16},{8,24},{16,0},{24,8},{1,17},{9,25},{17,1},{25,9},{2,18},{10... | collective-permute-start | bytes 786440 | tf_op jit(solution)/shard_map/ppermute | solution.py:524
  35.7 8.0 %propagate.5 = (bf16[16,768,256]{2,1,0:T(8,128)(2,1)}, bf16[256,512]{1,0:T(8,128)(2,1)S(1)}, bf16[256,512]{1,0:T(8,128)(2,1)S(1)}, bf16[256,512]{1,0:T(8,128)(2,...) custom-call(s32[20]{0:T(128)S(1)} %concatenate.17.meta, ...), custom_call_target="tpu_custom_call", output_to_operand_aliasing={{0}: (15, {})} | custom-call | flops 10119999488 | bytes 26400000 | tf_op jit(solution)/shard_map/propagate/pallas_call | solution.py:294
  43.8 1.6 %collective-permute-start.7 = (bf16[256,512]{1,0:T(8,128)(2,1)S(1)}, bf16[256,512]{1,0:T(8,128)(2,1)S(1)}, u32[]{:S(2)}, u32[]{:S(2)}) collective-permute-start(bf16[256,512]{1,0:T(8,128)(2,1)S(1)} %get-tuple-element.58), channel_id=1, source_target_pairs={{0,8},{8,0},{16,24},{24,16},{1,9},{9,1},{17,25},{25,17},{2,10},{10... | collective-permute-start | bytes 786440 | tf_op jit(solution)/shard_map/ppermute | solution.py:524
  45.3 1.5 %collective-permute-start.8 = (bf16[256,512]{1,0:T(8,128)(2,1)S(1)}, bf16[256,512]{1,0:T(8,128)(2,1)S(1)}, u32[]{:S(2)}, u32[]{:S(2)}) collective-permute-start(bf16[256,512]{1,0:T(8,128)(2,1)S(1)} %get-tuple-element.59), channel_id=1, source_target_pairs={{0,16},{8,24},{16,0},{24,8},{1,17},{9,25},{17,1},{25,9},{2,18},{10... | collective-permute-start | bytes 786440 | tf_op jit(solution)/shard_map/ppermute | solution.py:524
  47.3 2.6 %setup.1 = (bf16[16,512,256]{2,1,0:T(8,128)(2,1)S(1)}, f32[48,3072]{1,0:T(8,128)S(1)}, bf16[2,64,6144]{2,1,0:T(8,128)(2,1)S(1)}) custom-call(s32[20]{0:T(128)S(1)} %concatenate.17.meta, s32[16,256]{1,0:T(8,128)S(1)} %fusion.1.slot, s32[24,48]{1,0:T(8,128)S(1)} %bitcast.20, bf16[48,64,64]{2,1,0:T(8,128)(2,1)S(1)} %copy-done, ...), custom_call_target="tpu_custom_call" | custom-call | flops 230000000 | bytes 600000 | tf_op jit(solution)/shard_map/setup/pallas_call | solution.py:109
  50.7 1.7 %weave.4.w = bf16[1536,3072]{1,0:T(8,128)(2,1)S(1)} custom-call(f32[48,3072]{1,0:T(8,128)S(1)} %get-tuple-element.56.sel, bf16[2,64,6144]{2,1,0:T(8,128)(2,1)S(1)} %get-tuple-element.57.tt, bf16[256,512]{1,0:T(8,128)(2,1)S(1)} %get-tuple-element.53.after.rest_0_), custom_call_target="tpu_custom_call" | custom-call | flops 115000000 | bytes 300000 | tf_op jit(solution)/shard_map/weave/pallas_call | solution.py:139
  54.0 6.1 %collective-permute-done.8.rest_2_ = bf16[256,512]{1,0:T(8,128)(2,1)S(1)} collective-permute-done((bf16[256,512]{1,0:T(8,128)(2,1)S(1)}, bf16[256,512]{1,0:T(8,128)(2,1)S(1)}, u32[]{:S(2)}, u32[]{:S(2)}) %collective-permute-start.8) | collective-permute-done | bytes 262176 | tf_op jit(solution)/shard_map/ppermute | solution.py:524
  60.1 3.5 %couple.3 = (bf16[192,512]{1,0:T(8,128)(2,1)S(1)}, bf16[192,512]{1,0:T(8,128)(2,1)S(1)}, bf16[192,512]{1,0:T(8,128)(2,1)S(1)}, bf16[192,512]{1,0:T(8,128)(2,1)S(1)}, bf16[3072,512]{1,0:T(8,128)(2,1)S(1)}) custom-call(s32[20]{0:T(128)S(1)} %concatenate.17.meta, bf16[768,3072]{1,0:T(8,128)(2,1)S(1)} %weave.3.w, ...), custom_call_target="tpu_custom_call", output_to_operand_aliasing={{4}: (6, {})} | custom-call | flops 3449999872 | bytes 9000000 | tf_op jit(solution)/shard_map/couple/pallas_call | solution.py:377
  65.6 1.6 %collective-permute-start.15 = (bf16[192,512]{1,0:T(8,128)(2,1)S(1)}, bf16[192,512]{1,0:T(8,128)(2,1)S(1)}, u32[]{:S(2)}, u32[]{:S(2)}) collective-permute-start(bf16[192,512]{1,0:T(8,128)(2,1)S(1)} %get-tuple-element.69), channel_id=1, source_target_pairs={{0,24},{8,16},{16,8},{24,0},{1,25},{9,17},{17,9},{25,1},{2,26},{10... | collective-permute-start | bytes 589832 | tf_op jit(solution)/shard_map/ppermute | solution.py:543
  67.2 5.8 %couple.4 = (bf16[384,512]{1,0:T(8,128)(2,1)S(1)}, bf16[384,512]{1,0:T(8,128)(2,1)S(1)}, bf16[384,512]{1,0:T(8,128)(2,1)S(1)}, bf16[384,512]{1,0:T(8,128)(2,1)S(1)}) custom-call(s32[20]{0:T(128)S(1)} %concatenate.17.meta, bf16[1536,3072]{1,0:T(8,128)(2,1)S(1)} %weave.4.w, bf16[3072,512]{1,0:T(8,128)(2,1)S(1)} %get-tuple-element.70.rest_0_, ...), custom_call_target="tpu_custom_call" | custom-call | flops 6899999744 | bytes 18000000 | tf_op jit(solution)/shard_map/couple/pallas_call | solution.py:377
  75.0 1.6 %collective-permute-start.18 = (bf16[384,512]{1,0:T(8,128)(2,1)S(1)}, bf16[384,512]{1,0:T(8,128)(2,1)S(1)}, u32[]{:S(2)}, u32[]{:S(2)}) collective-permute-start(bf16[384,512]{1,0:T(8,128)(2,1)S(1)} %get-tuple-element.74), channel_id=1, source_target_pairs={{0,24},{8,16},{16,8},{24,0},{1,25},{9,17},{17,9},{25,1},{2,26},{10... | collective-permute-start | bytes 1179656 | tf_op jit(solution)/shard_map/ppermute | solution.py:543
  76.6 3.2 %couple.5 = (bf16[192,512]{1,0:T(8,128)(2,1)S(1)}, bf16[192,512]{1,0:T(8,128)(2,1)S(1)}, bf16[192,512]{1,0:T(8,128)(2,1)S(1)}, bf16[192,512]{1,0:T(8,128)(2,1)S(1)}) custom-call(s32[20]{0:T(128)S(1)} %concatenate.17.meta, bf16[768,3072]{1,0:T(8,128)(2,1)S(1)} %weave.5.w, bf16[3072,512]{1,0:T(8,128)(2,1)S(1)} %get-tuple-element.70.rest_0_, ...), custom_call_target="tpu_custom_call" | custom-call | flops 3449999872 | bytes 9000000 | tf_op jit(solution)/shard_map/couple/pallas_call | solution.py:377
  81.7 4.0 %finish.3.moved = bf16[16,768,256]{2,1,0:T(8,128)(2,1)} custom-call(s32[20]{0:T(128)S(1)} %concatenate.17.meta, s32[16,256]{1,0:T(8,128)S(1)} %fusion.1.slot, bf16[16,512,256]{2,1,0:T(8,128)(2,1)S(1)} %get-tuple-element.54.spread, bf16[16,768,256]{2,1,0:T(8,128)(2,1)} %get-tuple-element.55.moved, ...), custom_call_target="tpu_custom_call", output_to_operand_aliasing={{}: (3, {})} | custom-call | flops 3449999872 | bytes 9000000 | tf_op jit(solution)/shard_map/finish/pallas_call | solution.py:430
  85.8 1.7 %collective-permute-start.21 = (bf16[192,512]{1,0:T(8,128)(2,1)S(1)}, bf16[192,512]{1,0:T(8,128)(2,1)S(1)}, u32[]{:S(2)}, u32[]{:S(2)}) collective-permute-start(bf16[192,512]{1,0:T(8,128)(2,1)S(1)} %get-tuple-element.78), channel_id=1, source_target_pairs={{0,24},{8,16},{16,8},{24,0},{1,25},{9,17},{17,9},{25,1},{2,26},{10... | collective-permute-start | bytes 589832 | tf_op jit(solution)/shard_map/ppermute | solution.py:543
  87.4 6.6 %collective-permute-done.17.rest_2_ = bf16[384,512]{1,0:T(8,128)(2,1)S(1)} collective-permute-done((bf16[384,512]{1,0:T(8,128)(2,1)S(1)}, bf16[384,512]{1,0:T(8,128)(2,1)S(1)}, u32[]{:S(2)}, u32[]{:S(2)}) %collective-permute-start.17) | collective-permute-done | bytes 393248 | tf_op jit(solution)/shard_map/ppermute | solution.py:543
  94.5 5.1 %finish.4.moved = bf16[16,768,256]{2,1,0:T(8,128)(2,1)} custom-call(s32[20]{0:T(128)S(1)} %concatenate.17.meta, s32[16,256]{1,0:T(8,128)S(1)} %fusion.1.slot, bf16[16,512,256]{2,1,0:T(8,128)(2,1)S(1)} %get-tuple-element.54.spread, bf16[16,768,256]{2,1,0:T(8,128)(2,1)} %finish.3.moved, ...), custom_call_target="tpu_custom_call", output_to_operand_aliasing={{}: (3, {})} | custom-call | flops 6899999744 | bytes 18000000 | tf_op jit(solution)/shard_map/finish/pallas_call | solution.py:430
  101.2 4.0 %finish.5 = bf16[16,768,256]{2,1,0:T(8,128)(2,1)} custom-call(s32[20]{0:T(128)S(1)} %concatenate.17.meta, s32[16,256]{1,0:T(8,128)S(1)} %fusion.1.slot, bf16[16,512,256]{2,1,0:T(8,128)(2,1)S(1)} %get-tuple-element.54.spread, bf16[16,768,256]{2,1,0:T(8,128)(2,1)} %finish.4.moved, ...), custom_call_target="tpu_custom_call", output_to_operand_aliasing={{}: (3, {})} | custom-call | flops 3449999872 | bytes 9000000 | tf_op jit(solution)/shard_map/finish/pallas_call | solution.py:430
  (69 shorter events, 18.7 us)
Async XLA Ops:
  2.0 10.7 %collective-permute-start.2 = (bf16[2,272,256]{2,1,0:T(8,128)(2,1)S(1)}, bf16[2,272,256]{2,1,0:T(8,128)(2,1)S(1)}, u32[]{:S(2)}, u32[]{:S(2)}) collective-permute-start(bf16[2,272,256]{2,1,0:T(8,128)(2,1)S(1)} %pad_maximum_fusion), channel_id=1, source_target_pairs={{0,1},{2,3},{4,5},{6,7},{1,0},{3,2},{5,4},{7,6},{8,9},{10,11},{12,... | collective-permute-start | bytes 835592 | tf_op jit(solution)/shard_map/ppermute | solution.py:454
  2.6 10.2 %collective-permute-start.3 = (bf16[2,272,256]{2,1,0:T(8,128)(2,1)S(1)}, bf16[2,272,256]{2,1,0:T(8,128)(2,1)S(1)}, u32[]{:S(2)}, u32[]{:S(2)}) collective-permute-start(bf16[2,272,256]{2,1,0:T(8,128)(2,1)S(1)} %pad_maximum_fusion.1), channel_id=1, source_target_pairs={{1,2},{3,4},{5,6},{2,1},{4,3},{6,5},{9,10},{11,12},{13,14},{10,9},... | collective-permute-start | bytes 835592 | tf_op jit(solution)/shard_map/ppermute | solution.py:454
  8.0 16.2 %collective-permute-start = (bf16[2,512,256]{2,1,0:T(8,128)(2,1)S(1)}, bf16[2,512,256]{2,1,0:T(8,128)(2,1)S(1)}, u32[]{:S(2)}, u32[]{:S(2)}) collective-permute-start(bf16[2,512,256]{2,1,0:T(8,128)(2,1)S(1)} %get-tuple-element.42), channel_id=1, source_target_pairs={{0,1},{2,3},{4,5},{6,7},{1,0},{3,2},{5,4},{7,6},{8,9},{10,11},{12,... | collective-permute-start | bytes 1572872 | tf_op jit(solution)/shard_map/ppermute | solution.py:454
  12.0 12.2 %collective-permute-start.1 = (bf16[2,512,256]{2,1,0:T(8,128)(2,1)S(1)}, bf16[2,512,256]{2,1,0:T(8,128)(2,1)S(1)}, u32[]{:S(2)}, u32[]{:S(2)}) collective-permute-start(bf16[2,512,256]{2,1,0:T(8,128)(2,1)S(1)} %get-tuple-element.43), channel_id=1, source_target_pairs={{1,2},{3,4},{5,6},{2,1},{4,3},{6,5},{9,10},{11,12},{13,14},{10,9},... | collective-permute-start | bytes 1572872 | tf_op jit(solution)/shard_map/ppermute | solution.py:454
  20.7 14.5 %collective-permute-start.4 = (bf16[256,512]{1,0:T(8,128)(2,1)S(1)}, bf16[256,512]{1,0:T(8,128)(2,1)S(1)}, u32[]{:S(2)}, u32[]{:S(2)}) collective-permute-start(bf16[256,512]{1,0:T(8,128)(2,1)S(1)} %get-tuple-element.48), channel_id=1, source_target_pairs={{0,8},{8,0},{16,24},{24,16},{1,9},{9,1},{17,25},{25,17},{2,10},{10... | collective-permute-start | bytes 786440 | tf_op jit(solution)/shard_map/ppermute | solution.py:524
  22.2 13.5 %collective-permute-start.5 = (bf16[256,512]{1,0:T(8,128)(2,1)S(1)}, bf16[256,512]{1,0:T(8,128)(2,1)S(1)}, u32[]{:S(2)}, u32[]{:S(2)}) collective-permute-start(bf16[256,512]{1,0:T(8,128)(2,1)S(1)} %get-tuple-element.49), channel_id=1, source_target_pairs={{0,16},{8,24},{16,0},{24,8},{1,17},{9,25},{17,1},{25,9},{2,18},{10... | collective-permute-start | bytes 786440 | tf_op jit(solution)/shard_map/ppermute | solution.py:524
  23.8 11.9 %collective-permute-start.6 = (bf16[256,512]{1,0:T(8,128)(2,1)S(1)}, bf16[256,512]{1,0:T(8,128)(2,1)S(1)}, u32[]{:S(2)}, u32[]{:S(2)}) collective-permute-start(bf16[256,512]{1,0:T(8,128)(2,1)S(1)} %get-tuple-element.50), channel_id=1, source_target_pairs={{0,24},{8,16},{16,8},{24,0},{1,25},{9,17},{17,9},{25,1},{2,26},{10... | collective-permute-start | bytes 786440 | tf_op jit(solution)/shard_map/ppermute | solution.py:524
  32.1 14.7 %collective-permute-start.10 = (bf16[256,512]{1,0:T(8,128)(2,1)S(1)}, bf16[256,512]{1,0:T(8,128)(2,1)S(1)}, u32[]{:S(2)}, u32[]{:S(2)}) collective-permute-start(bf16[256,512]{1,0:T(8,128)(2,1)S(1)} %get-tuple-element.62), channel_id=1, source_target_pairs={{0,8},{8,0},{16,24},{24,16},{1,9},{9,1},{17,25},{25,17},{2,10},{10... | collective-permute-start | bytes 786440 | tf_op jit(solution)/shard_map/ppermute | solution.py:524
  33.7 19.6 %collective-permute-start.11 = (bf16[256,512]{1,0:T(8,128)(2,1)S(1)}, bf16[256,512]{1,0:T(8,128)(2,1)S(1)}, u32[]{:S(2)}, u32[]{:S(2)}) collective-permute-start(bf16[256,512]{1,0:T(8,128)(2,1)S(1)} %get-tuple-element.63), channel_id=1, source_target_pairs={{0,16},{8,24},{16,0},{24,8},{1,17},{9,25},{17,1},{25,9},{2,18},{10... | collective-permute-start | bytes 786440 | tf_op jit(solution)/shard_map/ppermute | solution.py:524
  35.2 18.1 %collective-permute-start.12 = (bf16[256,512]{1,0:T(8,128)(2,1)S(1)}, bf16[256,512]{1,0:T(8,128)(2,1)S(1)}, u32[]{:S(2)}, u32[]{:S(2)}) collective-permute-start(bf16[256,512]{1,0:T(8,128)(2,1)S(1)} %get-tuple-element.64), channel_id=1, source_target_pairs={{0,24},{8,16},{16,8},{24,0},{1,25},{9,17},{17,9},{25,1},{2,26},{10... | collective-permute-start | bytes 786440 | tf_op jit(solution)/shard_map/ppermute | solution.py:524
  35.7 11.6 %copy-start = (bf16[48,64,64]{2,1,0:T(8,128)(2,1)S(1)}, bf16[48,64,64]{2,1,0:T(8,128)(2,1)}, u32[]{:S(2)}) copy-start(bf16[48,64,64]{2,1,0:T(8,128)(2,1)} %table.1) | copy-start | bytes 1179652
  35.7 11.6 %copy-start.3 = (s32[48,24]{0,1:T(8,128)S(1)}, s32[48,24]{0,1:T(8,128)}, u32[]{:S(2)}) copy-start(s32[48,24]{0,1:T(8,128)} %param.10) | copy-start | bytes 13828
  43.8 10.3 %collective-permute-start.7 = (bf16[256,512]{1,0:T(8,128)(2,1)S(1)}, bf16[256,512]{1,0:T(8,128)(2,1)S(1)}, u32[]{:S(2)}, u32[]{:S(2)}) collective-permute-start(bf16[256,512]{1,0:T(8,128)(2,1)S(1)} %get-tuple-element.58), channel_id=1, source_target_pairs={{0,8},{8,0},{16,24},{24,16},{1,9},{9,1},{17,25},{25,17},{2,10},{10... | collective-permute-start | bytes 786440 | tf_op jit(solution)/shard_map/ppermute | solution.py:524
  45.3 14.8 %collective-permute-start.8 = (bf16[256,512]{1,0:T(8,128)(2,1)S(1)}, bf16[256,512]{1,0:T(8,128)(2,1)S(1)}, u32[]{:S(2)}, u32[]{:S(2)}) collective-permute-start(bf16[256,512]{1,0:T(8,128)(2,1)S(1)} %get-tuple-element.59), channel_id=1, source_target_pairs={{0,16},{8,24},{16,0},{24,8},{1,17},{9,25},{17,1},{25,9},{2,18},{10... | collective-permute-start | bytes 786440 | tf_op jit(solution)/shard_map/ppermute | solution.py:524
  46.8 13.2 %collective-permute-start.9 = (bf16[256,512]{1,0:T(8,128)(2,1)S(1)}, bf16[256,512]{1,0:T(8,128)(2,1)S(1)}, u32[]{:S(2)}, u32[]{:S(2)}) collective-permute-start(bf16[256,512]{1,0:T(8,128)(2,1)S(1)} %get-tuple-element.60), channel_id=1, source_target_pairs={{0,24},{8,16},{16,8},{24,0},{1,25},{9,17},{17,9},{25,1},{2,26},{10... | collective-permute-start | bytes 786440 | tf_op jit(solution)/shard_map/ppermute | solution.py:524
  63.6 11.3 %collective-permute-start.13 = (bf16[192,512]{1,0:T(8,128)(2,1)S(1)}, bf16[192,512]{1,0:T(8,128)(2,1)S(1)}, u32[]{:S(2)}, u32[]{:S(2)}) collective-permute-start(bf16[192,512]{1,0:T(8,128)(2,1)S(1)} %get-tuple-element.67), channel_id=1, source_target_pairs={{0,8},{8,0},{16,24},{24,16},{1,9},{9,1},{17,25},{25,17},{2,10},{10... | collective-permute-start | bytes 589832 | tf_op jit(solution)/shard_map/ppermute | solution.py:543
  64.4 12.2 %collective-permute-start.14 = (bf16[192,512]{1,0:T(8,128)(2,1)S(1)}, bf16[192,512]{1,0:T(8,128)(2,1)S(1)}, u32[]{:S(2)}, u32[]{:S(2)}) collective-permute-start(bf16[192,512]{1,0:T(8,128)(2,1)S(1)} %get-tuple-element.68), channel_id=1, source_target_pairs={{0,16},{8,24},{16,0},{24,8},{1,17},{9,25},{17,1},{25,9},{2,18},{10... | collective-permute-start | bytes 589832 | tf_op jit(solution)/shard_map/ppermute | solution.py:543
  65.6 11.0 %collective-permute-start.15 = (bf16[192,512]{1,0:T(8,128)(2,1)S(1)}, bf16[192,512]{1,0:T(8,128)(2,1)S(1)}, u32[]{:S(2)}, u32[]{:S(2)}) collective-permute-start(bf16[192,512]{1,0:T(8,128)(2,1)S(1)} %get-tuple-element.69), channel_id=1, source_target_pairs={{0,24},{8,16},{16,8},{24,0},{1,25},{9,17},{17,9},{25,1},{2,26},{10... | collective-permute-start | bytes 589832 | tf_op jit(solution)/shard_map/ppermute | solution.py:543
  73.0 12.8 %collective-permute-start.16 = (bf16[384,512]{1,0:T(8,128)(2,1)S(1)}, bf16[384,512]{1,0:T(8,128)(2,1)S(1)}, u32[]{:S(2)}, u32[]{:S(2)}) collective-permute-start(bf16[384,512]{1,0:T(8,128)(2,1)S(1)} %get-tuple-element.72), channel_id=1, source_target_pairs={{0,8},{8,0},{16,24},{24,16},{1,9},{9,1},{17,25},{25,17},{2,10},{10... | collective-permute-start | bytes 1179656 | tf_op jit(solution)/shard_map/ppermute | solution.py:543
  73.8 20.2 %collective-permute-start.17 = (bf16[384,512]{1,0:T(8,128)(2,1)S(1)}, bf16[384,512]{1,0:T(8,128)(2,1)S(1)}, u32[]{:S(2)}, u32[]{:S(2)}) collective-permute-start(bf16[384,512]{1,0:T(8,128)(2,1)S(1)} %get-tuple-element.73), channel_id=1, source_target_pairs={{0,16},{8,24},{16,0},{24,8},{1,17},{9,25},{17,1},{25,9},{2,18},{10... | collective-permute-start | bytes 1179656 | tf_op jit(solution)/shard_map/ppermute | solution.py:543
  75.0 19.6 %collective-permute-start.18 = (bf16[384,512]{1,0:T(8,128)(2,1)S(1)}, bf16[384,512]{1,0:T(8,128)(2,1)S(1)}, u32[]{:S(2)}, u32[]{:S(2)}) collective-permute-start(bf16[384,512]{1,0:T(8,128)(2,1)S(1)} %get-tuple-element.74), channel_id=1, source_target_pairs={{0,24},{8,16},{16,8},{24,0},{1,25},{9,17},{17,9},{25,1},{2,26},{10... | collective-permute-start | bytes 1179656 | tf_op jit(solution)/shard_map/ppermute | solution.py:543
  79.8 19.9 %collective-permute-start.19 = (bf16[192,512]{1,0:T(8,128)(2,1)S(1)}, bf16[192,512]{1,0:T(8,128)(2,1)S(1)}, u32[]{:S(2)}, u32[]{:S(2)}) collective-permute-start(bf16[192,512]{1,0:T(8,128)(2,1)S(1)} %get-tuple-element.76), channel_id=1, source_target_pairs={{0,8},{8,0},{16,24},{24,16},{1,9},{9,1},{17,25},{25,17},{2,10},{10... | collective-permute-start | bytes 589832 | tf_op jit(solution)/shard_map/ppermute | solution.py:543
  80.6 19.1 %collective-permute-start.20 = (bf16[192,512]{1,0:T(8,128)(2,1)S(1)}, bf16[192,512]{1,0:T(8,128)(2,1)S(1)}, u32[]{:S(2)}, u32[]{:S(2)}) collective-permute-start(bf16[192,512]{1,0:T(8,128)(2,1)S(1)} %get-tuple-element.77), channel_id=1, source_target_pairs={{0,16},{8,24},{16,0},{24,8},{1,17},{9,25},{17,1},{25,9},{2,18},{10... | collective-permute-start | bytes 589832 | tf_op jit(solution)/shard_map/ppermute | solution.py:543
  85.8 15.4 %collective-permute-start.21 = (bf16[192,512]{1,0:T(8,128)(2,1)S(1)}, bf16[192,512]{1,0:T(8,128)(2,1)S(1)}, u32[]{:S(2)}, u32[]{:S(2)}) collective-permute-start(bf16[192,512]{1,0:T(8,128)(2,1)S(1)} %get-tuple-element.78), channel_id=1, source_target_pairs={{0,24},{8,16},{16,8},{24,0},{1,25},{9,17},{17,9},{25,1},{2,26},{10... | collective-permute-start | bytes 589832 | tf_op jit(solution)/shard_map/ppermute | solution.py:543
  (4 other events, 25.8 us)

commit v5 on v4

--- a/solution.py
+++ b/solution.py
@@ -324,21 +324,21 @@
         copy.wait()
 
 
-def collect(meta, x, pieces, spots, dirs):
+def collect(meta, x, pieces, spots, dirs, after=()):
     vmem = pl.BlockSpec(memory_space=pltpu.VMEM)
     return pl.pallas_call(
         functools.partial(collect_kernel, spots, dirs),
         in_specs=[pl.BlockSpec(memory_space=pltpu.SMEM)]
-        + [pl.BlockSpec(memory_space=pl.ANY)] * len(pieces)
+        + [pl.BlockSpec(memory_space=pl.ANY)] * (len(pieces) + len(after))
         + [vmem],
         out_specs=vmem,
         out_shape=jax.ShapeDtypeStruct(x.shape, x.dtype),
         scratch_shapes=[pltpu.SemaphoreType.DMA((len(pieces),))],
-        input_output_aliases={1 + len(pieces): 0},
+        input_output_aliases={1 + len(pieces) + len(after): 0},
         compiler_params=params(),
         cost_estimate=cost(0.2),
         name="collect",
-    )(meta, *pieces, x)
+    )(meta, *pieces, *after, x)
 
 
 def couple_kernel(peers, dirs, begin, size, spots, meta, w, *rest):
@@ -386,6 +386,67 @@
         name="couple",
     )(meta, w, *args)
     return result[:peers], result[peers] if after is None else x
+
+
+def columns_of(meta, k, first, depth, dirs):
+    return pl.ds(pl.multiple_of(((meta[0] ^ k) * dirs + first) * NF, 128), depth)
+
+
+def begin_kernel(dirs, spots, meta, w, *rest):
+    total = rest[-1]
+    for i, (k, first) in enumerate(spots):
+        piece = rest[i]
+        part = jnp.dot(
+            w[:, columns_of(meta, k, first, piece.shape[0], dirs)], piece[...],
+            preferred_element_type=jnp.float32,
+        )
+        if i:
+            total[...] += part
+        else:
+            total[...] = part
+
+
+def begin_couple(meta, w, pieces, spots, dirs):
+    vmem = pl.BlockSpec(memory_space=pltpu.VMEM)
+    return pl.pallas_call(
+        functools.partial(begin_kernel, dirs, spots),
+        in_specs=[pl.BlockSpec(memory_space=pltpu.SMEM)] + [vmem] * (1 + len(pieces)),
+        out_specs=vmem,
+        out_shape=jax.ShapeDtypeStruct((w.shape[0], pieces[0].shape[1]), jnp.float32),
+        compiler_params=params(),
+        cost_estimate=cost(0.2),
+        name="begin_couple",
+    )(meta, w, *pieces)
+
+
+def end_kernel(peers, dirs, size, spots, meta, w, partial, *rest):
+    owns, pieces, outs, total = rest[:peers], rest[peers:2 * peers], rest[2 * peers:-1], rest[-1]
+    coupled = partial[...]
+    for i, (k, first) in enumerate(spots):
+        coupled += jnp.dot(
+            w[:, columns_of(meta, k, first, pieces[i].shape[0], dirs)], pieces[i][...],
+            preferred_element_type=jnp.float32,
+        )
+    for p in range(peers):
+        total[p] = coupled[p * size * NF:(p + 1) * size * NF]
+    for k in range(peers):
+        own = owns[k][:size * NF, :].astype(jnp.float32)
+        outs[k][...] = (own + own * total[meta[0] ^ k]).astype(jnp.bfloat16)
+
+
+def end_couple(meta, w, partial, owns, pieces, spots, size, peers, dirs):
+    vmem = pl.BlockSpec(memory_space=pltpu.VMEM)
+    share = SEA // peers
+    return pl.pallas_call(
+        functools.partial(end_kernel, peers, dirs, size, spots),
+        in_specs=[pl.BlockSpec(memory_space=pltpu.SMEM)] + [vmem] * (2 + 2 * peers),
+        out_specs=[vmem] * peers,
+        out_shape=[jax.ShapeDtypeStruct((size * NF, share), jnp.bfloat16)] * peers,
+        scratch_shapes=[pltpu.VMEM((peers, size * NF, share), jnp.float32)],
+        compiler_params=params(),
+        cost_estimate=cost(2),
+        name="end_couple",
+    )(meta, w, partial, *owns, *pieces)
 
 
 def finish_kernel(peers, share, begin, group, meta, slot, spread, moved, *rest):
@@ -532,13 +593,25 @@
         for begin, size in zip(offsets_of(parts_back), parts_back)
     ]
     x = collect(meta, x, pieces[-2], tuple(spots[-2]), dirs)
+    early = comps % 128 == 0 and parts_back[0] <= parts_out[0]
+    early = early and all(size * NF % 128 == 0 for size in parts_out)
+    if early:
+        ahead_pieces = [piece for part in pieces[:-1] for piece in part]
+        ahead_spots = tuple(spot for part in spots[:-1] for spot in part)
+        partial = begin_couple(meta, woven[0], ahead_pieces, ahead_spots, dirs)
     result = moved
     backs = []
     for g, (begin, size) in enumerate(zip(offsets_of(parts_back), parts_back)):
         after = backs[g - 2][1:] if g >= 2 else renewed[:1] if g else None
-        renewed, x = couple(
-            meta, woven[g], x, pieces[-1], after, tuple(spots[-1]), begin, size, peers, dirs
-        )
+        if early and g == 0:
+            renewed = end_couple(
+                meta, woven[0], partial, pieces[0], pieces[-1], tuple(spots[-1]), size, peers, dirs
+            )
+            x = collect(meta, x, pieces[-1], tuple(spots[-1]), dirs, tuple(renewed[:1]))
+        else:
+            renewed, x = couple(
+                meta, woven[g], x, pieces[-1], after, tuple(spots[-1]), begin, size, peers, dirs
+            )
         back = [renewed[0]] + [
             lax.ppermute(renewed[k], "spec", [(i, i ^ k) for i in range(peers)])
             for k in range(1, peers)

time: 106 us -> 105 us (level)
  waiting for transfers between devices: 14.7 us -> 12.3 us
  Pallas kernels: 57.8 us -> 59.4 us
    pallas_call x0 -> x2, Pallas kernels: none -> 4.18 us  [the longest x1 2.33 us: begin_couple(): pl.pallas_call(functools.partial(begin_kernel, dirs, spots), in_specs=[pl...]
    pallas_call x3 -> x2, Pallas kernels: 12.5 us -> 9.02 us  [couple(): pl.pallas_call(functools.partial(couple_kernel, peers, dirs, begin, size,...]
    ppermute x9, waiting for transfers between devices: 6.09 us -> 3.73 us  [local(): lax.ppermute(packed[k], 'spec', [(i, i ^ k) for i in range(peers)])]
  transfers between devices with their start and end apart: 22 -> 22, of which waited for: 4 -> 4; matrix products, arithmetic and copies ran while one was open for 3% -> 3% of each run, Pallas kernels for 48% -> 51%
where the time goes in v5:
time: 105 us
  Pallas kernels  59.4 us (57%)
  starting transfers between devices  27.4 us (26%)
  waiting for transfers between devices  12.3 us (12%)
  local copies, waits for them, and re-layouts  3.02 us (3%)
  other arithmetic  1.97 us (2%)
    pallas_call x3, Pallas kernels, propagate(): pl.pallas_call(functools.partial(propagate_kernel, peers, share, begin *...  23.8 us
    pallas_call x3, Pallas kernels, finish(): pl.pallas_call(functools.partial(finish_kernel, peers, share, begin * NF,...  13.2 us
    ppermute x9, starting transfers between devices, local(): lax.ppermute(renewed[k], 'spec', [(i, i ^ k) for i in range(peers)])  10.7 us
    ppermute x9, starting transfers between devices, local(): lax.ppermute(packed[k], 'spec', [(i, i ^ k) for i in range(peers)])  10.7 us
    pallas_call x2, Pallas kernels, couple(): pl.pallas_call(functools.partial(couple_kernel, peers, dirs, begin, size,...  9.02 us
    ppermute x9, waiting for transfers between devices, local(): lax.ppermute(renewed[k], 'spec', [(i, i ^ k) for i in range(peers)])  8.59 us
    ppermute x4, starting transfers between devices, swap(): return lax.ppermute(array, 'tile', pairs + [(j, i) for i, j in pairs])  6.07 us
    ppermute x9, waiting for transfers between devices, local(): lax.ppermute(packed[k], 'spec', [(i, i ^ k) for i in range(peers)])  3.73 us
  transfers between devices with their start and end apart: 22, of which 4 were waited for; matrix products, arithmetic and copies ran while one was open for 3% of the time, Pallas kernels for 51%

profile of v5, /device:TPU:0, one launch (start us, length us, event | category | flops | bytes accessed | tf_op | source)
XLA Modules:
  0.0 104.8 jit_solution(15582434425536736137)
XLA Ops:
  6.4 1.6 %mark.1 = (bf16[16,256,512]{2,1,0:T(8,128)(2,1)S(1)}, f32[768,128]{1,0:T(8,128)S(1)}, f32[768,128]{1,0:T(8,128)S(1)}, bf16[2,512,256]{2,1,0:T(8,128)(2,1)S(1)}, bf16[2,512,256]{2,1,0:T(8,128)(2,1)S(1)}) custom-call(s32[20]{0:T(128)S(1)} %concatenate.17.meta, s32[256,16]{1,0:T(8,128)S(1)} %copy.15.slot_t, f32[768,128]{1,0:T(8,128)S(1)} %broadcast_in_dim.51.ae, ...), custom_call_target="tpu_custom_call" | custom-call | flops 4600000000 | bytes 12000000 | tf_op jit(solution)/shard_map/mark/pallas_call | solution.py:63
  8.0 4.0 %collective-permute-start = (bf16[2,512,256]{2,1,0:T(8,128)(2,1)S(1)}, bf16[2,512,256]{2,1,0:T(8,128)(2,1)S(1)}, u32[]{:S(2)}, u32[]{:S(2)}) collective-permute-start(bf16[2,512,256]{2,1,0:T(8,128)(2,1)S(1)} %get-tuple-element.41), channel_id=1, source_target_pairs={{0,1},{2,3},{4,5},{6,7},{1,0},{3,2},{5,4},{7,6},{8,9},{10,11},{12,... | collective-permute-start | bytes 1572872 | tf_op jit(solution)/shard_map/ppermute | solution.py:515
  13.0 7.9 %propagate.3 = (bf16[16,768,256]{2,1,0:T(8,128)(2,1)}, bf16[256,512]{1,0:T(8,128)(2,1)S(1)}, bf16[256,512]{1,0:T(8,128)(2,1)S(1)}, bf16[256,512]{1,0:T(8,128)(2,1)S(1)}, bf16[256,512]{1,0:T(8,128)(2,1)S(1)}) custom-call(s32[20]{0:T(128)S(1)} %concatenate.17.meta, bf16[16,768,256]{2,1,0:T(8,128)(2,1)S(1)} %bitcast.16, ...), custom_call_target="tpu_custom_call" | custom-call | flops 10119999488 | bytes 26400000 | tf_op jit(solution)/shard_map/propagate/pallas_call | solution.py:294
  20.9 1.6 %collective-permute-start.4 = (bf16[256,512]{1,0:T(8,128)(2,1)S(1)}, bf16[256,512]{1,0:T(8,128)(2,1)S(1)}, u32[]{:S(2)}, u32[]{:S(2)}) collective-permute-start(bf16[256,512]{1,0:T(8,128)(2,1)S(1)} %get-tuple-element.47), channel_id=1, source_target_pairs={{0,8},{8,0},{16,24},{24,16},{1,9},{9,1},{17,25},{25,17},{2,10},{10... | collective-permute-start | bytes 786440 | tf_op jit(solution)/shard_map/ppermute | solution.py:585
  22.4 1.5 %collective-permute-start.5 = (bf16[256,512]{1,0:T(8,128)(2,1)S(1)}, bf16[256,512]{1,0:T(8,128)(2,1)S(1)}, u32[]{:S(2)}, u32[]{:S(2)}) collective-permute-start(bf16[256,512]{1,0:T(8,128)(2,1)S(1)} %get-tuple-element.48), channel_id=1, source_target_pairs={{0,16},{8,24},{16,0},{24,8},{1,17},{9,25},{17,1},{25,9},{2,18},{10... | collective-permute-start | bytes 786440 | tf_op jit(solution)/shard_map/ppermute | solution.py:585
  24.4 7.9 %propagate.4 = (bf16[16,768,256]{2,1,0:T(8,128)(2,1)}, bf16[256,512]{1,0:T(8,128)(2,1)S(1)}, bf16[256,512]{1,0:T(8,128)(2,1)S(1)}, bf16[256,512]{1,0:T(8,128)(2,1)S(1)}, bf16[256,512]{1,0:T(8,128)(2,1)S(1)}) custom-call(s32[20]{0:T(128)S(1)} %concatenate.17.meta, bf16[16,768,256]{2,1,0:T(8,128)(2,1)S(1)} %bitcast.16, ...), custom_call_target="tpu_custom_call", output_to_operand_aliasing={{0}: (11, {})} | custom-call | flops 10119999488 | bytes 26400000 | tf_op jit(solution)/shard_map/propagate/pallas_call | solution.py:294
  32.3 1.6 %collective-permute-start.7 = (bf16[256,512]{1,0:T(8,128)(2,1)S(1)}, bf16[256,512]{1,0:T(8,128)(2,1)S(1)}, u32[]{:S(2)}, u32[]{:S(2)}) collective-permute-start(bf16[256,512]{1,0:T(8,128)(2,1)S(1)} %get-tuple-element.58), channel_id=1, source_target_pairs={{0,8},{8,0},{16,24},{24,16},{1,9},{9,1},{17,25},{25,17},{2,10},{10... | collective-permute-start | bytes 786440 | tf_op jit(solution)/shard_map/ppermute | solution.py:585
  33.9 1.5 %collective-permute-start.8 = (bf16[256,512]{1,0:T(8,128)(2,1)S(1)}, bf16[256,512]{1,0:T(8,128)(2,1)S(1)}, u32[]{:S(2)}, u32[]{:S(2)}) collective-permute-start(bf16[256,512]{1,0:T(8,128)(2,1)S(1)} %get-tuple-element.59), channel_id=1, source_target_pairs={{0,16},{8,24},{16,0},{24,8},{1,17},{9,25},{17,1},{25,9},{2,18},{10... | collective-permute-start | bytes 786440 | tf_op jit(solution)/shard_map/ppermute | solution.py:585
  35.9 8.0 %propagate.5 = (bf16[16,768,256]{2,1,0:T(8,128)(2,1)}, bf16[256,512]{1,0:T(8,128)(2,1)S(1)}, bf16[256,512]{1,0:T(8,128)(2,1)S(1)}, bf16[256,512]{1,0:T(8,128)(2,...) custom-call(s32[20]{0:T(128)S(1)} %concatenate.17.meta, ...), custom_call_target="tpu_custom_call", output_to_operand_aliasing={{0}: (15, {})} | custom-call | flops 10119999488 | bytes 26400000 | tf_op jit(solution)/shard_map/propagate/pallas_call | solution.py:294
  43.9 1.6 %collective-permute-start.10 = (bf16[256,512]{1,0:T(8,128)(2,1)S(1)}, bf16[256,512]{1,0:T(8,128)(2,1)S(1)}, u32[]{:S(2)}, u32[]{:S(2)}) collective-permute-start(bf16[256,512]{1,0:T(8,128)(2,1)S(1)} %get-tuple-element.61), channel_id=1, source_target_pairs={{0,8},{8,0},{16,24},{24,16},{1,9},{9,1},{17,25},{25,17},{2,10},{10... | collective-permute-start | bytes 786440 | tf_op jit(solution)/shard_map/ppermute | solution.py:585
  47.5 2.6 %setup.1 = (bf16[16,512,256]{2,1,0:T(8,128)(2,1)S(1)}, f32[48,3072]{1,0:T(8,128)S(1)}, bf16[2,64,6144]{2,1,0:T(8,128)(2,1)S(1)}) custom-call(s32[20]{0:T(128)S(1)} %concatenate.17.meta, s32[16,256]{1,0:T(8,128)S(1)} %fusion.1.slot, s32[24,48]{1,0:T(8,128)S(1)} %bitcast.20, bf16[48,64,64]{2,1,0:T(8,128)(2,1)S(1)} %copy-done, ...), custom_call_target="tpu_custom_call" | custom-call | flops 230000000 | bytes 600000 | tf_op jit(solution)/shard_map/setup/pallas_call | solution.py:109
  51.8 1.7 %weave.4.w = bf16[1536,3072]{1,0:T(8,128)(2,1)S(1)} custom-call(f32[48,3072]{1,0:T(8,128)S(1)} %get-tuple-element.55.sel, bf16[2,64,6144]{2,1,0:T(8,128)(2,1)S(1)} %get-tuple-element.56.tt, bf16[256,512]{1,0:T(8,128)(2,1)S(1)} %get-tuple-element.52.after.rest_4_.rest_0_), custom_call_target="tpu_custom_call" | custom-call | flops 115000000 | bytes 300000 | tf_op jit(solution)/shard_map/weave/pallas_call | solution.py:139
  54.2 2.3 %begin_couple.1.partial = f32[768,512]{1,0:T(8,128)S(1)} custom-call(s32[20]{0:T(128)S(1)} %concatenate.17.meta, bf16[768,3072]{1,0:T(8,128)(2,1)S(1)} %weave.3.w, bf16[256,512]{1,0:T(8,128)(2,1)S(1)} %get-tuple-element.46.rest_0_, bf16[256,512]{1,0:T(8,128)(2,1)S(1)} %collective-permute-done.4.rest_1_, bf16[256,512]{1,0:T(8,128)(2,1)S(1)} %collective-permute-done.5.rest_2_, ...), custom_call_target="tpu_custom_call" | custom-call | flops 230000000 | bytes 600000 | tf_op jit(solution)/shard_map/begin_couple/pallas_call | solution.py:411
  56.5 3.7 %collective-permute-done.11.rest_6_.rest_2_ = bf16[256,512]{1,0:T(8,128)(2,1)S(1)} collective-permute-done((bf16[256,512]{1,0:T(8,128)(2,1)S(1)}, bf16[256,512]{1,0:T(8,128)(2,1)S(1)}, u32[]{:S(2)}, u32[]{:S(2)}) %collective-permute-start.11) | collective-permute-done | bytes 262176 | tf_op jit(solution)/shard_map/ppermute | solution.py:585
  60.3 1.9 %end_couple.1 = (bf16[192,512]{1,0:T(8,128)(2,1)S(1)}, bf16[192,512]{1,0:T(8,128)(2,1)S(1)}, bf16[192,512]{1,0:T(8,128)(2,1)S(1)}, bf16[192,512]{1,0:T(8,128)(2,1)S(1)}) custom-call(s32[20]{0:T(128)S(1)} %concatenate.17.meta, bf16[768,3072]{1,0:T(8,128)(2,1)S(1)} %weave.3.w, f32[768,512]{1,0:T(8,128)S(1)} %begin_couple.1.partial, ...), custom_call_target="tpu_custom_call" | custom-call | flops 2300000000 | bytes 6000000 | tf_op jit(solution)/shard_map/end_couple/pallas_call | solution.py:440
  64.1 1.6 %collective-permute-start.15 = (bf16[192,512]{1,0:T(8,128)(2,1)S(1)}, bf16[192,512]{1,0:T(8,128)(2,1)S(1)}, u32[]{:S(2)}, u32[]{:S(2)}) collective-permute-start(bf16[192,512]{1,0:T(8,128)(2,1)S(1)} %get-tuple-element.67), channel_id=1, source_target_pairs={{0,24},{8,16},{16,8},{24,0},{1,25},{9,17},{17,9},{25,1},{2,26},{10... | collective-permute-start | bytes 589832 | tf_op jit(solution)/shard_map/ppermute | solution.py:616
  66.6 5.8 %couple.2 = (bf16[384,512]{1,0:T(8,128)(2,1)S(1)}, bf16[384,512]{1,0:T(8,128)(2,1)S(1)}, bf16[384,512]{1,0:T(8,128)(2,1)S(1)}, bf16[384,512]{1,0:T(8,128)(2,1)S(1)}) custom-call(s32[20]{0:T(128)S(1)} %concatenate.17.meta, bf16[1536,3072]{1,0:T(8,128)(2,1)S(1)} %weave.4.w, bf16[3072,512]{1,0:T(8,128)(2,1)S(1)} %collect.3.rest_0_, ...), custom_call_target="tpu_custom_call" | custom-call | flops 6899999744 | bytes 18000000 | tf_op jit(solution)/shard_map/couple/pallas_call | solution.py:377
  74.4 1.6 %collective-permute-start.18 = (bf16[384,512]{1,0:T(8,128)(2,1)S(1)}, bf16[384,512]{1,0:T(8,128)(2,1)S(1)}, u32[]{:S(2)}, u32[]{:S(2)}) collective-permute-start(bf16[384,512]{1,0:T(8,128)(2,1)S(1)} %get-tuple-element.72), channel_id=1, source_target_pairs={{0,24},{8,16},{16,8},{24,0},{1,25},{9,17},{17,9},{25,1},{2,26},{10... | collective-permute-start | bytes 1179656 | tf_op jit(solution)/shard_map/ppermute | solution.py:616
  76.0 3.2 %couple.3 = (bf16[192,512]{1,0:T(8,128)(2,1)S(1)}, bf16[192,512]{1,0:T(8,128)(2,1)S(1)}, bf16[192,512]{1,0:T(8,128)(2,1)S(1)}, bf16[192,512]{1,0:T(8,128)(2,1)S(1)}) custom-call(s32[20]{0:T(128)S(1)} %concatenate.17.meta, bf16[768,3072]{1,0:T(8,128)(2,1)S(1)} %weave.5.w, bf16[3072,512]{1,0:T(8,128)(2,1)S(1)} %collect.3.rest_0_, ...), custom_call_target="tpu_custom_call" | custom-call | flops 3449999872 | bytes 9000000 | tf_op jit(solution)/shard_map/couple/pallas_call | solution.py:377
  81.2 4.0 %finish.3.moved = bf16[16,768,256]{2,1,0:T(8,128)(2,1)} custom-call(s32[20]{0:T(128)S(1)} %concatenate.17.meta, s32[16,256]{1,0:T(8,128)S(1)} %fusion.1.slot, bf16[16,512,256]{2,1,0:T(8,128)(2,1)S(1)} %get-tuple-element.53.spread, bf16[16,768,256]{2,1,0:T(8,128)(2,1)} %get-tuple-element.54.moved, ...), custom_call_target="tpu_custom_call", output_to_operand_aliasing={{}: (3, {})} | custom-call | flops 3449999872 | bytes 9000000 | tf_op jit(solution)/shard_map/finish/pallas_call | solution.py:491
  85.2 1.6 %collective-permute-start.21 = (bf16[192,512]{1,0:T(8,128)(2,1)S(1)}, bf16[192,512]{1,0:T(8,128)(2,1)S(1)}, u32[]{:S(2)}, u32[]{:S(2)}) collective-permute-start(bf16[192,512]{1,0:T(8,128)(2,1)S(1)} %get-tuple-element.76), channel_id=1, source_target_pairs={{0,24},{8,16},{16,8},{24,0},{1,25},{9,17},{17,9},{25,1},{2,26},{10... | collective-permute-start | bytes 589832 | tf_op jit(solution)/shard_map/ppermute | solution.py:616
  86.9 6.6 %collective-permute-done.17.rest_2_ = bf16[384,512]{1,0:T(8,128)(2,1)S(1)} collective-permute-done((bf16[384,512]{1,0:T(8,128)(2,1)S(1)}, bf16[384,512]{1,0:T(8,128)(2,1)S(1)}, u32[]{:S(2)}, u32[]{:S(2)}) %collective-permute-start.17) | collective-permute-done | bytes 393248 | tf_op jit(solution)/shard_map/ppermute | solution.py:616
  94.0 5.1 %finish.4.moved = bf16[16,768,256]{2,1,0:T(8,128)(2,1)} custom-call(s32[20]{0:T(128)S(1)} %concatenate.17.meta, s32[16,256]{1,0:T(8,128)S(1)} %fusion.1.slot, bf16[16,512,256]{2,1,0:T(8,128)(2,1)S(1)} %get-tuple-element.53.spread, bf16[16,768,256]{2,1,0:T(8,128)(2,1)} %finish.3.moved, ...), custom_call_target="tpu_custom_call", output_to_operand_aliasing={{}: (3, {})} | custom-call | flops 6899999744 | bytes 18000000 | tf_op jit(solution)/shard_map/finish/pallas_call | solution.py:491
  100.6 4.0 %finish.5 = bf16[16,768,256]{2,1,0:T(8,128)(2,1)} custom-call(s32[20]{0:T(128)S(1)} %concatenate.17.meta, s32[16,256]{1,0:T(8,128)S(1)} %fusion.1.slot, bf16[16,512,256]{2,1,0:T(8,128)(2,1)S(1)} %get-tuple-element.53.spread, bf16[16,768,256]{2,1,0:T(8,128)(2,1)} %finish.4.moved, ...), custom_call_target="tpu_custom_call", output_to_operand_aliasing={{}: (3, {})} | custom-call | flops 3449999872 | bytes 9000000 | tf_op jit(solution)/shard_map/finish/pallas_call | solution.py:491
  (71 shorter events, 21.3 us)
Async XLA Ops:
  2.0 10.9 %collective-permute-start.2 = (bf16[2,272,256]{2,1,0:T(8,128)(2,1)S(1)}, bf16[2,272,256]{2,1,0:T(8,128)(2,1)S(1)}, u32[]{:S(2)}, u32[]{:S(2)}) collective-permute-start(bf16[2,272,256]{2,1,0:T(8,128)(2,1)S(1)} %pad_maximum_fusion), channel_id=1, source_target_pairs={{0,1},{2,3},{4,5},{6,7},{1,0},{3,2},{5,4},{7,6},{8,9},{10,11},{12,... | collective-permute-start | bytes 835592 | tf_op jit(solution)/shard_map/ppermute | solution.py:515
  2.6 10.3 %collective-permute-start.3 = (bf16[2,272,256]{2,1,0:T(8,128)(2,1)S(1)}, bf16[2,272,256]{2,1,0:T(8,128)(2,1)S(1)}, u32[]{:S(2)}, u32[]{:S(2)}) collective-permute-start(bf16[2,272,256]{2,1,0:T(8,128)(2,1)S(1)} %pad_maximum_fusion.1), channel_id=1, source_target_pairs={{1,2},{3,4},{5,6},{2,1},{4,3},{6,5},{9,10},{11,12},{13,14},{10,9},... | collective-permute-start | bytes 835592 | tf_op jit(solution)/shard_map/ppermute | solution.py:515
  8.0 16.4 %collective-permute-start = (bf16[2,512,256]{2,1,0:T(8,128)(2,1)S(1)}, bf16[2,512,256]{2,1,0:T(8,128)(2,1)S(1)}, u32[]{:S(2)}, u32[]{:S(2)}) collective-permute-start(bf16[2,512,256]{2,1,0:T(8,128)(2,1)S(1)} %get-tuple-element.41), channel_id=1, source_target_pairs={{0,1},{2,3},{4,5},{6,7},{1,0},{3,2},{5,4},{7,6},{8,9},{10,11},{12,... | collective-permute-start | bytes 1572872 | tf_op jit(solution)/shard_map/ppermute | solution.py:515
  12.0 12.4 %collective-permute-start.1 = (bf16[2,512,256]{2,1,0:T(8,128)(2,1)S(1)}, bf16[2,512,256]{2,1,0:T(8,128)(2,1)S(1)}, u32[]{:S(2)}, u32[]{:S(2)}) collective-permute-start(bf16[2,512,256]{2,1,0:T(8,128)(2,1)S(1)} %get-tuple-element.42), channel_id=1, source_target_pairs={{1,2},{3,4},{5,6},{2,1},{4,3},{6,5},{9,10},{11,12},{13,14},{10,9},... | collective-permute-start | bytes 1572872 | tf_op jit(solution)/shard_map/ppermute | solution.py:515
  20.9 14.5 %collective-permute-start.4 = (bf16[256,512]{1,0:T(8,128)(2,1)S(1)}, bf16[256,512]{1,0:T(8,128)(2,1)S(1)}, u32[]{:S(2)}, u32[]{:S(2)}) collective-permute-start(bf16[256,512]{1,0:T(8,128)(2,1)S(1)} %get-tuple-element.47), channel_id=1, source_target_pairs={{0,8},{8,0},{16,24},{24,16},{1,9},{9,1},{17,25},{25,17},{2,10},{10... | collective-permute-start | bytes 786440 | tf_op jit(solution)/shard_map/ppermute | solution.py:585
  22.4 13.5 %collective-permute-start.5 = (bf16[256,512]{1,0:T(8,128)(2,1)S(1)}, bf16[256,512]{1,0:T(8,128)(2,1)S(1)}, u32[]{:S(2)}, u32[]{:S(2)}) collective-permute-start(bf16[256,512]{1,0:T(8,128)(2,1)S(1)} %get-tuple-element.48), channel_id=1, source_target_pairs={{0,16},{8,24},{16,0},{24,8},{1,17},{9,25},{17,1},{25,9},{2,18},{10... | collective-permute-start | bytes 786440 | tf_op jit(solution)/shard_map/ppermute | solution.py:585
  24.0 11.9 %collective-permute-start.6 = (bf16[256,512]{1,0:T(8,128)(2,1)S(1)}, bf16[256,512]{1,0:T(8,128)(2,1)S(1)}, u32[]{:S(2)}, u32[]{:S(2)}) collective-permute-start(bf16[256,512]{1,0:T(8,128)(2,1)S(1)} %get-tuple-element.49), channel_id=1, source_target_pairs={{0,24},{8,16},{16,8},{24,0},{1,25},{9,17},{17,9},{25,1},{2,26},{10... | collective-permute-start | bytes 786440 | tf_op jit(solution)/shard_map/ppermute | solution.py:585
  32.3 14.7 %collective-permute-start.7 = (bf16[256,512]{1,0:T(8,128)(2,1)S(1)}, bf16[256,512]{1,0:T(8,128)(2,1)S(1)}, u32[]{:S(2)}, u32[]{:S(2)}) collective-permute-start(bf16[256,512]{1,0:T(8,128)(2,1)S(1)} %get-tuple-element.58), channel_id=1, source_target_pairs={{0,8},{8,0},{16,24},{24,16},{1,9},{9,1},{17,25},{25,17},{2,10},{10... | collective-permute-start | bytes 786440 | tf_op jit(solution)/shard_map/ppermute | solution.py:585
  33.9 19.6 %collective-permute-start.8 = (bf16[256,512]{1,0:T(8,128)(2,1)S(1)}, bf16[256,512]{1,0:T(8,128)(2,1)S(1)}, u32[]{:S(2)}, u32[]{:S(2)}) collective-permute-start(bf16[256,512]{1,0:T(8,128)(2,1)S(1)} %get-tuple-element.59), channel_id=1, source_target_pairs={{0,16},{8,24},{16,0},{24,8},{1,17},{9,25},{17,1},{25,9},{2,18},{10... | collective-permute-start | bytes 786440 | tf_op jit(solution)/shard_map/ppermute | solution.py:585
  35.4 18.1 %collective-permute-start.9 = (bf16[256,512]{1,0:T(8,128)(2,1)S(1)}, bf16[256,512]{1,0:T(8,128)(2,1)S(1)}, u32[]{:S(2)}, u32[]{:S(2)}) collective-permute-start(bf16[256,512]{1,0:T(8,128)(2,1)S(1)} %get-tuple-element.60), channel_id=1, source_target_pairs={{0,24},{8,16},{16,8},{24,0},{1,25},{9,17},{17,9},{25,1},{2,26},{10... | collective-permute-start | bytes 786440 | tf_op jit(solution)/shard_map/ppermute | solution.py:585
  35.9 11.6 %copy-start = (bf16[48,64,64]{2,1,0:T(8,128)(2,1)S(1)}, bf16[48,64,64]{2,1,0:T(8,128)(2,1)}, u32[]{:S(2)}) copy-start(bf16[48,64,64]{2,1,0:T(8,128)(2,1)} %table.1) | copy-start | bytes 1179652
  35.9 11.6 %copy-start.3 = (s32[48,24]{0,1:T(8,128)S(1)}, s32[48,24]{0,1:T(8,128)}, u32[]{:S(2)}) copy-start(s32[48,24]{0,1:T(8,128)} %param.10) | copy-start | bytes 13828
  43.9 12.6 %collective-permute-start.10 = (bf16[256,512]{1,0:T(8,128)(2,1)S(1)}, bf16[256,512]{1,0:T(8,128)(2,1)S(1)}, u32[]{:S(2)}, u32[]{:S(2)}) collective-permute-start(bf16[256,512]{1,0:T(8,128)(2,1)S(1)} %get-tuple-element.61), channel_id=1, source_target_pairs={{0,8},{8,0},{16,24},{24,16},{1,9},{9,1},{17,25},{25,17},{2,10},{10... | collective-permute-start | bytes 786440 | tf_op jit(solution)/shard_map/ppermute | solution.py:585
  45.5 14.8 %collective-permute-start.11 = (bf16[256,512]{1,0:T(8,128)(2,1)S(1)}, bf16[256,512]{1,0:T(8,128)(2,1)S(1)}, u32[]{:S(2)}, u32[]{:S(2)}) collective-permute-start(bf16[256,512]{1,0:T(8,128)(2,1)S(1)} %get-tuple-element.62), channel_id=1, source_target_pairs={{0,16},{8,24},{16,0},{24,8},{1,17},{9,25},{17,1},{25,9},{2,18},{10... | collective-permute-start | bytes 786440 | tf_op jit(solution)/shard_map/ppermute | solution.py:585
  47.0 13.2 %collective-permute-start.12 = (bf16[256,512]{1,0:T(8,128)(2,1)S(1)}, bf16[256,512]{1,0:T(8,128)(2,1)S(1)}, u32[]{:S(2)}, u32[]{:S(2)}) collective-permute-start(bf16[256,512]{1,0:T(8,128)(2,1)S(1)} %get-tuple-element.63), channel_id=1, source_target_pairs={{0,24},{8,16},{16,8},{24,0},{1,25},{9,17},{17,9},{25,1},{2,26},{10... | collective-permute-start | bytes 786440 | tf_op jit(solution)/shard_map/ppermute | solution.py:585
  62.1 12.3 %collective-permute-start.13 = (bf16[192,512]{1,0:T(8,128)(2,1)S(1)}, bf16[192,512]{1,0:T(8,128)(2,1)S(1)}, u32[]{:S(2)}, u32[]{:S(2)}) collective-permute-start(bf16[192,512]{1,0:T(8,128)(2,1)S(1)} %get-tuple-element.65), channel_id=1, source_target_pairs={{0,8},{8,0},{16,24},{24,16},{1,9},{9,1},{17,25},{25,17},{2,10},{10... | collective-permute-start | bytes 589832 | tf_op jit(solution)/shard_map/ppermute | solution.py:616
  63.0 13.0 %collective-permute-start.14 = (bf16[192,512]{1,0:T(8,128)(2,1)S(1)}, bf16[192,512]{1,0:T(8,128)(2,1)S(1)}, u32[]{:S(2)}, u32[]{:S(2)}) collective-permute-start(bf16[192,512]{1,0:T(8,128)(2,1)S(1)} %get-tuple-element.66), channel_id=1, source_target_pairs={{0,16},{8,24},{16,0},{24,8},{1,17},{9,25},{17,1},{25,9},{2,18},{10... | collective-permute-start | bytes 589832 | tf_op jit(solution)/shard_map/ppermute | solution.py:616
  64.1 11.9 %collective-permute-start.15 = (bf16[192,512]{1,0:T(8,128)(2,1)S(1)}, bf16[192,512]{1,0:T(8,128)(2,1)S(1)}, u32[]{:S(2)}, u32[]{:S(2)}) collective-permute-start(bf16[192,512]{1,0:T(8,128)(2,1)S(1)} %get-tuple-element.67), channel_id=1, source_target_pairs={{0,24},{8,16},{16,8},{24,0},{1,25},{9,17},{17,9},{25,1},{2,26},{10... | collective-permute-start | bytes 589832 | tf_op jit(solution)/shard_map/ppermute | solution.py:616
  72.4 12.8 %collective-permute-start.16 = (bf16[384,512]{1,0:T(8,128)(2,1)S(1)}, bf16[384,512]{1,0:T(8,128)(2,1)S(1)}, u32[]{:S(2)}, u32[]{:S(2)}) collective-permute-start(bf16[384,512]{1,0:T(8,128)(2,1)S(1)} %get-tuple-element.70), channel_id=1, source_target_pairs={{0,8},{8,0},{16,24},{24,16},{1,9},{9,1},{17,25},{25,17},{2,10},{10... | collective-permute-start | bytes 1179656 | tf_op jit(solution)/shard_map/ppermute | solution.py:616
  73.3 20.2 %collective-permute-start.17 = (bf16[384,512]{1,0:T(8,128)(2,1)S(1)}, bf16[384,512]{1,0:T(8,128)(2,1)S(1)}, u32[]{:S(2)}, u32[]{:S(2)}) collective-permute-start(bf16[384,512]{1,0:T(8,128)(2,1)S(1)} %get-tuple-element.71), channel_id=1, source_target_pairs={{0,16},{8,24},{16,0},{24,8},{1,17},{9,25},{17,1},{25,9},{2,18},{10... | collective-permute-start | bytes 1179656 | tf_op jit(solution)/shard_map/ppermute | solution.py:616
  74.4 19.6 %collective-permute-start.18 = (bf16[384,512]{1,0:T(8,128)(2,1)S(1)}, bf16[384,512]{1,0:T(8,128)(2,1)S(1)}, u32[]{:S(2)}, u32[]{:S(2)}) collective-permute-start(bf16[384,512]{1,0:T(8,128)(2,1)S(1)} %get-tuple-element.72), channel_id=1, source_target_pairs={{0,24},{8,16},{16,8},{24,0},{1,25},{9,17},{17,9},{25,1},{2,26},{10... | collective-permute-start | bytes 1179656 | tf_op jit(solution)/shard_map/ppermute | solution.py:616
  79.2 19.9 %collective-permute-start.19 = (bf16[192,512]{1,0:T(8,128)(2,1)S(1)}, bf16[192,512]{1,0:T(8,128)(2,1)S(1)}, u32[]{:S(2)}, u32[]{:S(2)}) collective-permute-start(bf16[192,512]{1,0:T(8,128)(2,1)S(1)} %get-tuple-element.74), channel_id=1, source_target_pairs={{0,8},{8,0},{16,24},{24,16},{1,9},{9,1},{17,25},{25,17},{2,10},{10... | collective-permute-start | bytes 589832 | tf_op jit(solution)/shard_map/ppermute | solution.py:616
  80.0 19.1 %collective-permute-start.20 = (bf16[192,512]{1,0:T(8,128)(2,1)S(1)}, bf16[192,512]{1,0:T(8,128)(2,1)S(1)}, u32[]{:S(2)}, u32[]{:S(2)}) collective-permute-start(bf16[192,512]{1,0:T(8,128)(2,1)S(1)} %get-tuple-element.75), channel_id=1, source_target_pairs={{0,16},{8,24},{16,0},{24,8},{1,17},{9,25},{17,1},{25,9},{2,18},{10... | collective-permute-start | bytes 589832 | tf_op jit(solution)/shard_map/ppermute | solution.py:616
  85.2 15.4 %collective-permute-start.21 = (bf16[192,512]{1,0:T(8,128)(2,1)S(1)}, bf16[192,512]{1,0:T(8,128)(2,1)S(1)}, u32[]{:S(2)}, u32[]{:S(2)}) collective-permute-start(bf16[192,512]{1,0:T(8,128)(2,1)S(1)} %get-tuple-element.76), channel_id=1, source_target_pairs={{0,24},{8,16},{16,8},{24,0},{1,25},{9,17},{17,9},{25,1},{2,26},{10... | collective-permute-start | bytes 589832 | tf_op jit(solution)/shard_map/ppermute | solution.py:616
  (4 other events, 26.5 us)

commit v6 on v5

--- a/solution.py
+++ b/solution.py
@@ -12,7 +12,7 @@
 SEA = 2048
 WINDOW = 512
 STEP = 256
-SUBK = 16
+SUBK = 32
 courant_scale = 0.45
 MIB = 1024 * 1024
 

time: 105 us -> 105 us (level)
  no operation moved by 1% of the time
where the time goes in v6:
time: 105 us
  Pallas kernels  59.3 us (56%)
  starting transfers between devices  27.4 us (26%)
  waiting for transfers between devices  12.4 us (12%)
  local copies, waits for them, and re-layouts  3.02 us (3%)
  other arithmetic  1.97 us (2%)
    pallas_call x3, Pallas kernels, propagate(): pl.pallas_call(functools.partial(propagate_kernel, peers, share, begin *...  23.7 us
    pallas_call x3, Pallas kernels, finish(): pl.pallas_call(functools.partial(finish_kernel, peers, share, begin * NF,...  13.2 us
    ppermute x9, starting transfers between devices, local(): lax.ppermute(renewed[k], 'spec', [(i, i ^ k) for i in range(peers)])  10.7 us
    ppermute x9, starting transfers between devices, local(): lax.ppermute(packed[k], 'spec', [(i, i ^ k) for i in range(peers)])  10.7 us
    pallas_call x2, Pallas kernels, couple(): pl.pallas_call(functools.partial(couple_kernel, peers, dirs, begin, size,...  9.02 us
    ppermute x9, waiting for transfers between devices, local(): lax.ppermute(renewed[k], 'spec', [(i, i ^ k) for i in range(peers)])  8.65 us
    ppermute x4, starting transfers between devices, swap(): return lax.ppermute(array, 'tile', pairs + [(j, i) for i, j in pairs])  6.07 us
    ppermute x9, waiting for transfers between devices, local(): lax.ppermute(packed[k], 'spec', [(i, i ^ k) for i in range(peers)])  3.77 us
  transfers between devices with their start and end apart: 22, of which 4 were waited for; matrix products, arithmetic and copies ran while one was open for 3% of the time, Pallas kernels for 51%

profile of v6, /device:TPU:0, one launch (start us, length us, event | category | flops | bytes accessed | tf_op | source)
XLA Modules:
  0.0 104.8 jit_solution(6522244258645727106)
XLA Ops:
  6.4 1.6 %mark.1 = (bf16[16,256,512]{2,1,0:T(8,128)(2,1)S(1)}, f32[768,128]{1,0:T(8,128)S(1)}, f32[768,128]{1,0:T(8,128)S(1)}, bf16[2,512,256]{2,1,0:T(8,128)(2,1)S(1)}, bf16[2,512,256]{2,1,0:T(8,128)(2,1)S(1)}) custom-call(s32[20]{0:T(128)S(1)} %concatenate.17.meta, s32[256,16]{1,0:T(8,128)S(1)} %copy.15.slot_t, f32[768,128]{1,0:T(8,128)S(1)} %broadcast_in_dim.51.ae, ...), custom_call_target="tpu_custom_call" | custom-call | flops 4600000000 | bytes 12000000 | tf_op jit(solution)/shard_map/mark/pallas_call | solution.py:63
  8.0 4.0 %collective-permute-start = (bf16[2,512,256]{2,1,0:T(8,128)(2,1)S(1)}, bf16[2,512,256]{2,1,0:T(8,128)(2,1)S(1)}, u32[]{:S(2)}, u32[]{:S(2)}) collective-permute-start(bf16[2,512,256]{2,1,0:T(8,128)(2,1)S(1)} %get-tuple-element.41), channel_id=1, source_target_pairs={{0,1},{2,3},{4,5},{6,7},{1,0},{3,2},{5,4},{7,6},{8,9},{10,11},{12,... | collective-permute-start | bytes 1572872 | tf_op jit(solution)/shard_map/ppermute | solution.py:515
  13.0 7.9 %propagate.3 = (bf16[16,768,256]{2,1,0:T(8,128)(2,1)}, bf16[256,512]{1,0:T(8,128)(2,1)S(1)}, bf16[256,512]{1,0:T(8,128)(2,1)S(1)}, bf16[256,512]{1,0:T(8,128)(2,1)S(1)}, bf16[256,512]{1,0:T(8,128)(2,1)S(1)}) custom-call(s32[20]{0:T(128)S(1)} %concatenate.17.meta, bf16[16,768,256]{2,1,0:T(8,128)(2,1)S(1)} %bitcast.16, ...), custom_call_target="tpu_custom_call" | custom-call | flops 10119999488 | bytes 26400000 | tf_op jit(solution)/shard_map/propagate/pallas_call | solution.py:294
  20.8 1.6 %collective-permute-start.4 = (bf16[256,512]{1,0:T(8,128)(2,1)S(1)}, bf16[256,512]{1,0:T(8,128)(2,1)S(1)}, u32[]{:S(2)}, u32[]{:S(2)}) collective-permute-start(bf16[256,512]{1,0:T(8,128)(2,1)S(1)} %get-tuple-element.47), channel_id=1, source_target_pairs={{0,8},{8,0},{16,24},{24,16},{1,9},{9,1},{17,25},{25,17},{2,10},{10... | collective-permute-start | bytes 786440 | tf_op jit(solution)/shard_map/ppermute | solution.py:585
  24.4 7.9 %propagate.4 = (bf16[16,768,256]{2,1,0:T(8,128)(2,1)}, bf16[256,512]{1,0:T(8,128)(2,1)S(1)}, bf16[256,512]{1,0:T(8,128)(2,1)S(1)}, bf16[256,512]{1,0:T(8,128)(2,1)S(1)}, bf16[256,512]{1,0:T(8,128)(2,1)S(1)}) custom-call(s32[20]{0:T(128)S(1)} %concatenate.17.meta, bf16[16,768,256]{2,1,0:T(8,128)(2,1)S(1)} %bitcast.16, ...), custom_call_target="tpu_custom_call", output_to_operand_aliasing={{0}: (11, {})} | custom-call | flops 10119999488 | bytes 26400000 | tf_op jit(solution)/shard_map/propagate/pallas_call | solution.py:294
  32.3 1.6 %collective-permute-start.7 = (bf16[256,512]{1,0:T(8,128)(2,1)S(1)}, bf16[256,512]{1,0:T(8,128)(2,1)S(1)}, u32[]{:S(2)}, u32[]{:S(2)}) collective-permute-start(bf16[256,512]{1,0:T(8,128)(2,1)S(1)} %get-tuple-element.58), channel_id=1, source_target_pairs={{0,8},{8,0},{16,24},{24,16},{1,9},{9,1},{17,25},{25,17},{2,10},{10... | collective-permute-start | bytes 786440 | tf_op jit(solution)/shard_map/ppermute | solution.py:585
  33.8 1.5 %collective-permute-start.8 = (bf16[256,512]{1,0:T(8,128)(2,1)S(1)}, bf16[256,512]{1,0:T(8,128)(2,1)S(1)}, u32[]{:S(2)}, u32[]{:S(2)}) collective-permute-start(bf16[256,512]{1,0:T(8,128)(2,1)S(1)} %get-tuple-element.59), channel_id=1, source_target_pairs={{0,16},{8,24},{16,0},{24,8},{1,17},{9,25},{17,1},{25,9},{2,18},{10... | collective-permute-start | bytes 786440 | tf_op jit(solution)/shard_map/ppermute | solution.py:585
  35.8 8.0 %propagate.5 = (bf16[16,768,256]{2,1,0:T(8,128)(2,1)}, bf16[256,512]{1,0:T(8,128)(2,1)S(1)}, bf16[256,512]{1,0:T(8,128)(2,1)S(1)}, bf16[256,512]{1,0:T(8,128)(2,...) custom-call(s32[20]{0:T(128)S(1)} %concatenate.17.meta, ...), custom_call_target="tpu_custom_call", output_to_operand_aliasing={{0}: (15, {})} | custom-call | flops 10119999488 | bytes 26400000 | tf_op jit(solution)/shard_map/propagate/pallas_call | solution.py:294
  43.9 1.6 %collective-permute-start.10 = (bf16[256,512]{1,0:T(8,128)(2,1)S(1)}, bf16[256,512]{1,0:T(8,128)(2,1)S(1)}, u32[]{:S(2)}, u32[]{:S(2)}) collective-permute-start(bf16[256,512]{1,0:T(8,128)(2,1)S(1)} %get-tuple-element.61), channel_id=1, source_target_pairs={{0,8},{8,0},{16,24},{24,16},{1,9},{9,1},{17,25},{25,17},{2,10},{10... | collective-permute-start | bytes 786440 | tf_op jit(solution)/shard_map/ppermute | solution.py:585
  45.4 1.5 %collective-permute-start.11 = (bf16[256,512]{1,0:T(8,128)(2,1)S(1)}, bf16[256,512]{1,0:T(8,128)(2,1)S(1)}, u32[]{:S(2)}, u32[]{:S(2)}) collective-permute-start(bf16[256,512]{1,0:T(8,128)(2,1)S(1)} %get-tuple-element.62), channel_id=1, source_target_pairs={{0,16},{8,24},{16,0},{24,8},{1,17},{9,25},{17,1},{25,9},{2,18},{10... | collective-permute-start | bytes 786440 | tf_op jit(solution)/shard_map/ppermute | solution.py:585
  47.4 2.6 %setup.1 = (bf16[16,512,256]{2,1,0:T(8,128)(2,1)S(1)}, f32[48,3072]{1,0:T(8,128)S(1)}, bf16[2,64,6144]{2,1,0:T(8,128)(2,1)S(1)}) custom-call(s32[20]{0:T(128)S(1)} %concatenate.17.meta, s32[16,256]{1,0:T(8,128)S(1)} %fusion.1.slot, s32[24,48]{1,0:T(8,128)S(1)} %bitcast.20, bf16[48,64,64]{2,1,0:T(8,128)(2,1)S(1)} %copy-done, ...), custom_call_target="tpu_custom_call" | custom-call | flops 230000000 | bytes 600000 | tf_op jit(solution)/shard_map/setup/pallas_call | solution.py:109
  51.7 1.7 %weave.4.w = bf16[1536,3072]{1,0:T(8,128)(2,1)S(1)} custom-call(f32[48,3072]{1,0:T(8,128)S(1)} %get-tuple-element.55.sel, bf16[2,64,6144]{2,1,0:T(8,128)(2,1)S(1)} %get-tuple-element.56.tt, bf16[256,512]{1,0:T(8,128)(2,1)S(1)} %get-tuple-element.52.after.rest_4_.rest_0_), custom_call_target="tpu_custom_call" | custom-call | flops 115000000 | bytes 300000 | tf_op jit(solution)/shard_map/weave/pallas_call | solution.py:139
  54.1 2.3 %begin_couple.1.partial = f32[768,512]{1,0:T(8,128)S(1)} custom-call(s32[20]{0:T(128)S(1)} %concatenate.17.meta, bf16[768,3072]{1,0:T(8,128)(2,1)S(1)} %weave.3.w, bf16[256,512]{1,0:T(8,128)(2,1)S(1)} %get-tuple-element.46.rest_0_, bf16[256,512]{1,0:T(8,128)(2,1)S(1)} %collective-permute-done.4.rest_1_, bf16[256,512]{1,0:T(8,128)(2,1)S(1)} %collective-permute-done.5.rest_2_, ...), custom_call_target="tpu_custom_call" | custom-call | flops 230000000 | bytes 600000 | tf_op jit(solution)/shard_map/begin_couple/pallas_call | solution.py:411
  56.5 3.7 %collective-permute-done.11.rest_6_.rest_2_ = bf16[256,512]{1,0:T(8,128)(2,1)S(1)} collective-permute-done((bf16[256,512]{1,0:T(8,128)(2,1)S(1)}, bf16[256,512]{1,0:T(8,128)(2,1)S(1)}, u32[]{:S(2)}, u32[]{:S(2)}) %collective-permute-start.11) | collective-permute-done | bytes 262176 | tf_op jit(solution)/shard_map/ppermute | solution.py:585
  60.2 1.9 %end_couple.1 = (bf16[192,512]{1,0:T(8,128)(2,1)S(1)}, bf16[192,512]{1,0:T(8,128)(2,1)S(1)}, bf16[192,512]{1,0:T(8,128)(2,1)S(1)}, bf16[192,512]{1,0:T(8,128)(2,1)S(1)}) custom-call(s32[20]{0:T(128)S(1)} %concatenate.17.meta, bf16[768,3072]{1,0:T(8,128)(2,1)S(1)} %weave.3.w, f32[768,512]{1,0:T(8,128)S(1)} %begin_couple.1.partial, ...), custom_call_target="tpu_custom_call" | custom-call | flops 2300000000 | bytes 6000000 | tf_op jit(solution)/shard_map/end_couple/pallas_call | solution.py:440
  64.0 1.6 %collective-permute-start.15 = (bf16[192,512]{1,0:T(8,128)(2,1)S(1)}, bf16[192,512]{1,0:T(8,128)(2,1)S(1)}, u32[]{:S(2)}, u32[]{:S(2)}) collective-permute-start(bf16[192,512]{1,0:T(8,128)(2,1)S(1)} %get-tuple-element.67), channel_id=1, source_target_pairs={{0,24},{8,16},{16,8},{24,0},{1,25},{9,17},{17,9},{25,1},{2,26},{10... | collective-permute-start | bytes 589832 | tf_op jit(solution)/shard_map/ppermute | solution.py:616
  66.5 5.8 %couple.2 = (bf16[384,512]{1,0:T(8,128)(2,1)S(1)}, bf16[384,512]{1,0:T(8,128)(2,1)S(1)}, bf16[384,512]{1,0:T(8,128)(2,1)S(1)}, bf16[384,512]{1,0:T(8,128)(2,1)S(1)}) custom-call(s32[20]{0:T(128)S(1)} %concatenate.17.meta, bf16[1536,3072]{1,0:T(8,128)(2,1)S(1)} %weave.4.w, bf16[3072,512]{1,0:T(8,128)(2,1)S(1)} %collect.3.rest_0_, ...), custom_call_target="tpu_custom_call" | custom-call | flops 6899999744 | bytes 18000000 | tf_op jit(solution)/shard_map/couple/pallas_call | solution.py:377
  74.3 1.6 %collective-permute-start.18 = (bf16[384,512]{1,0:T(8,128)(2,1)S(1)}, bf16[384,512]{1,0:T(8,128)(2,1)S(1)}, u32[]{:S(2)}, u32[]{:S(2)}) collective-permute-start(bf16[384,512]{1,0:T(8,128)(2,1)S(1)} %get-tuple-element.72), channel_id=1, source_target_pairs={{0,24},{8,16},{16,8},{24,0},{1,25},{9,17},{17,9},{25,1},{2,26},{10... | collective-permute-start | bytes 1179656 | tf_op jit(solution)/shard_map/ppermute | solution.py:616
  76.0 3.2 %couple.3 = (bf16[192,512]{1,0:T(8,128)(2,1)S(1)}, bf16[192,512]{1,0:T(8,128)(2,1)S(1)}, bf16[192,512]{1,0:T(8,128)(2,1)S(1)}, bf16[192,512]{1,0:T(8,128)(2,1)S(1)}) custom-call(s32[20]{0:T(128)S(1)} %concatenate.17.meta, bf16[768,3072]{1,0:T(8,128)(2,1)S(1)} %weave.5.w, bf16[3072,512]{1,0:T(8,128)(2,1)S(1)} %collect.3.rest_0_, ...), custom_call_target="tpu_custom_call" | custom-call | flops 3449999872 | bytes 9000000 | tf_op jit(solution)/shard_map/couple/pallas_call | solution.py:377
  81.1 4.0 %finish.3.moved = bf16[16,768,256]{2,1,0:T(8,128)(2,1)} custom-call(s32[20]{0:T(128)S(1)} %concatenate.17.meta, s32[16,256]{1,0:T(8,128)S(1)} %fusion.1.slot, bf16[16,512,256]{2,1,0:T(8,128)(2,1)S(1)} %get-tuple-element.53.spread, bf16[16,768,256]{2,1,0:T(8,128)(2,1)} %get-tuple-element.54.moved, ...), custom_call_target="tpu_custom_call", output_to_operand_aliasing={{}: (3, {})} | custom-call | flops 3449999872 | bytes 9000000 | tf_op jit(solution)/shard_map/finish/pallas_call | solution.py:491
  85.1 1.7 %collective-permute-start.21 = (bf16[192,512]{1,0:T(8,128)(2,1)S(1)}, bf16[192,512]{1,0:T(8,128)(2,1)S(1)}, u32[]{:S(2)}, u32[]{:S(2)}) collective-permute-start(bf16[192,512]{1,0:T(8,128)(2,1)S(1)} %get-tuple-element.76), channel_id=1, source_target_pairs={{0,24},{8,16},{16,8},{24,0},{1,25},{9,17},{17,9},{25,1},{2,26},{10... | collective-permute-start | bytes 589832 | tf_op jit(solution)/shard_map/ppermute | solution.py:616
  86.8 6.5 %collective-permute-done.17.rest_2_ = bf16[384,512]{1,0:T(8,128)(2,1)S(1)} collective-permute-done((bf16[384,512]{1,0:T(8,128)(2,1)S(1)}, bf16[384,512]{1,0:T(8,128)(2,1)S(1)}, u32[]{:S(2)}, u32[]{:S(2)}) %collective-permute-start.17) | collective-permute-done | bytes 393248 | tf_op jit(solution)/shard_map/ppermute | solution.py:616
  93.9 5.1 %finish.4.moved = bf16[16,768,256]{2,1,0:T(8,128)(2,1)} custom-call(s32[20]{0:T(128)S(1)} %concatenate.17.meta, s32[16,256]{1,0:T(8,128)S(1)} %fusion.1.slot, bf16[16,512,256]{2,1,0:T(8,128)(2,1)S(1)} %get-tuple-element.53.spread, bf16[16,768,256]{2,1,0:T(8,128)(2,1)} %finish.3.moved, ...), custom_call_target="tpu_custom_call", output_to_operand_aliasing={{}: (3, {})} | custom-call | flops 6899999744 | bytes 18000000 | tf_op jit(solution)/shard_map/finish/pallas_call | solution.py:491
  100.6 4.0 %finish.5 = bf16[16,768,256]{2,1,0:T(8,128)(2,1)} custom-call(s32[20]{0:T(128)S(1)} %concatenate.17.meta, s32[16,256]{1,0:T(8,128)S(1)} %fusion.1.slot, bf16[16,512,256]{2,1,0:T(8,128)(2,1)S(1)} %get-tuple-element.53.spread, bf16[16,768,256]{2,1,0:T(8,128)(2,1)} %finish.4.moved, ...), custom_call_target="tpu_custom_call", output_to_operand_aliasing={{}: (3, {})} | custom-call | flops 3449999872 | bytes 9000000 | tf_op jit(solution)/shard_map/finish/pallas_call | solution.py:491
  (71 shorter events, 21.3 us)
Async XLA Ops:
  2.0 10.9 %collective-permute-start.2 = (bf16[2,272,256]{2,1,0:T(8,128)(2,1)S(1)}, bf16[2,272,256]{2,1,0:T(8,128)(2,1)S(1)}, u32[]{:S(2)}, u32[]{:S(2)}) collective-permute-start(bf16[2,272,256]{2,1,0:T(8,128)(2,1)S(1)} %pad_maximum_fusion), channel_id=1, source_target_pairs={{0,1},{2,3},{4,5},{6,7},{1,0},{3,2},{5,4},{7,6},{8,9},{10,11},{12,... | collective-permute-start | bytes 835592 | tf_op jit(solution)/shard_map/ppermute | solution.py:515
  2.6 10.3 %collective-permute-start.3 = (bf16[2,272,256]{2,1,0:T(8,128)(2,1)S(1)}, bf16[2,272,256]{2,1,0:T(8,128)(2,1)S(1)}, u32[]{:S(2)}, u32[]{:S(2)}) collective-permute-start(bf16[2,272,256]{2,1,0:T(8,128)(2,1)S(1)} %pad_maximum_fusion.1), channel_id=1, source_target_pairs={{1,2},{3,4},{5,6},{2,1},{4,3},{6,5},{9,10},{11,12},{13,14},{10,9},... | collective-permute-start | bytes 835592 | tf_op jit(solution)/shard_map/ppermute | solution.py:515
  8.0 16.4 %collective-permute-start = (bf16[2,512,256]{2,1,0:T(8,128)(2,1)S(1)}, bf16[2,512,256]{2,1,0:T(8,128)(2,1)S(1)}, u32[]{:S(2)}, u32[]{:S(2)}) collective-permute-start(bf16[2,512,256]{2,1,0:T(8,128)(2,1)S(1)} %get-tuple-element.41), channel_id=1, source_target_pairs={{0,1},{2,3},{4,5},{6,7},{1,0},{3,2},{5,4},{7,6},{8,9},{10,11},{12,... | collective-permute-start | bytes 1572872 | tf_op jit(solution)/shard_map/ppermute | solution.py:515
  12.0 12.4 %collective-permute-start.1 = (bf16[2,512,256]{2,1,0:T(8,128)(2,1)S(1)}, bf16[2,512,256]{2,1,0:T(8,128)(2,1)S(1)}, u32[]{:S(2)}, u32[]{:S(2)}) collective-permute-start(bf16[2,512,256]{2,1,0:T(8,128)(2,1)S(1)} %get-tuple-element.42), channel_id=1, source_target_pairs={{1,2},{3,4},{5,6},{2,1},{4,3},{6,5},{9,10},{11,12},{13,14},{10,9},... | collective-permute-start | bytes 1572872 | tf_op jit(solution)/shard_map/ppermute | solution.py:515
  20.8 14.5 %collective-permute-start.4 = (bf16[256,512]{1,0:T(8,128)(2,1)S(1)}, bf16[256,512]{1,0:T(8,128)(2,1)S(1)}, u32[]{:S(2)}, u32[]{:S(2)}) collective-permute-start(bf16[256,512]{1,0:T(8,128)(2,1)S(1)} %get-tuple-element.47), channel_id=1, source_target_pairs={{0,8},{8,0},{16,24},{24,16},{1,9},{9,1},{17,25},{25,17},{2,10},{10... | collective-permute-start | bytes 786440 | tf_op jit(solution)/shard_map/ppermute | solution.py:585
  22.4 13.4 %collective-permute-start.5 = (bf16[256,512]{1,0:T(8,128)(2,1)S(1)}, bf16[256,512]{1,0:T(8,128)(2,1)S(1)}, u32[]{:S(2)}, u32[]{:S(2)}) collective-permute-start(bf16[256,512]{1,0:T(8,128)(2,1)S(1)} %get-tuple-element.48), channel_id=1, source_target_pairs={{0,16},{8,24},{16,0},{24,8},{1,17},{9,25},{17,1},{25,9},{2,18},{10... | collective-permute-start | bytes 786440 | tf_op jit(solution)/shard_map/ppermute | solution.py:585
  23.9 11.9 %collective-permute-start.6 = (bf16[256,512]{1,0:T(8,128)(2,1)S(1)}, bf16[256,512]{1,0:T(8,128)(2,1)S(1)}, u32[]{:S(2)}, u32[]{:S(2)}) collective-permute-start(bf16[256,512]{1,0:T(8,128)(2,1)S(1)} %get-tuple-element.49), channel_id=1, source_target_pairs={{0,24},{8,16},{16,8},{24,0},{1,25},{9,17},{17,9},{25,1},{2,26},{10... | collective-permute-start | bytes 786440 | tf_op jit(solution)/shard_map/ppermute | solution.py:585
  32.3 14.7 %collective-permute-start.7 = (bf16[256,512]{1,0:T(8,128)(2,1)S(1)}, bf16[256,512]{1,0:T(8,128)(2,1)S(1)}, u32[]{:S(2)}, u32[]{:S(2)}) collective-permute-start(bf16[256,512]{1,0:T(8,128)(2,1)S(1)} %get-tuple-element.58), channel_id=1, source_target_pairs={{0,8},{8,0},{16,24},{24,16},{1,9},{9,1},{17,25},{25,17},{2,10},{10... | collective-permute-start | bytes 786440 | tf_op jit(solution)/shard_map/ppermute | solution.py:585
  33.8 19.6 %collective-permute-start.8 = (bf16[256,512]{1,0:T(8,128)(2,1)S(1)}, bf16[256,512]{1,0:T(8,128)(2,1)S(1)}, u32[]{:S(2)}, u32[]{:S(2)}) collective-permute-start(bf16[256,512]{1,0:T(8,128)(2,1)S(1)} %get-tuple-element.59), channel_id=1, source_target_pairs={{0,16},{8,24},{16,0},{24,8},{1,17},{9,25},{17,1},{25,9},{2,18},{10... | collective-permute-start | bytes 786440 | tf_op jit(solution)/shard_map/ppermute | solution.py:585
  35.3 18.1 %collective-permute-start.9 = (bf16[256,512]{1,0:T(8,128)(2,1)S(1)}, bf16[256,512]{1,0:T(8,128)(2,1)S(1)}, u32[]{:S(2)}, u32[]{:S(2)}) collective-permute-start(bf16[256,512]{1,0:T(8,128)(2,1)S(1)} %get-tuple-element.60), channel_id=1, source_target_pairs={{0,24},{8,16},{16,8},{24,0},{1,25},{9,17},{17,9},{25,1},{2,26},{10... | collective-permute-start | bytes 786440 | tf_op jit(solution)/shard_map/ppermute | solution.py:585
  35.8 11.6 %copy-start = (bf16[48,64,64]{2,1,0:T(8,128)(2,1)S(1)}, bf16[48,64,64]{2,1,0:T(8,128)(2,1)}, u32[]{:S(2)}) copy-start(bf16[48,64,64]{2,1,0:T(8,128)(2,1)} %table.1) | copy-start | bytes 1179652
  35.8 11.6 %copy-start.3 = (s32[48,24]{0,1:T(8,128)S(1)}, s32[48,24]{0,1:T(8,128)}, u32[]{:S(2)}) copy-start(s32[48,24]{0,1:T(8,128)} %param.10) | copy-start | bytes 13828
  43.9 12.6 %collective-permute-start.10 = (bf16[256,512]{1,0:T(8,128)(2,1)S(1)}, bf16[256,512]{1,0:T(8,128)(2,1)S(1)}, u32[]{:S(2)}, u32[]{:S(2)}) collective-permute-start(bf16[256,512]{1,0:T(8,128)(2,1)S(1)} %get-tuple-element.61), channel_id=1, source_target_pairs={{0,8},{8,0},{16,24},{24,16},{1,9},{9,1},{17,25},{25,17},{2,10},{10... | collective-permute-start | bytes 786440 | tf_op jit(solution)/shard_map/ppermute | solution.py:585
  45.4 14.8 %collective-permute-start.11 = (bf16[256,512]{1,0:T(8,128)(2,1)S(1)}, bf16[256,512]{1,0:T(8,128)(2,1)S(1)}, u32[]{:S(2)}, u32[]{:S(2)}) collective-permute-start(bf16[256,512]{1,0:T(8,128)(2,1)S(1)} %get-tuple-element.62), channel_id=1, source_target_pairs={{0,16},{8,24},{16,0},{24,8},{1,17},{9,25},{17,1},{25,9},{2,18},{10... | collective-permute-start | bytes 786440 | tf_op jit(solution)/shard_map/ppermute | solution.py:585
  47.0 13.3 %collective-permute-start.12 = (bf16[256,512]{1,0:T(8,128)(2,1)S(1)}, bf16[256,512]{1,0:T(8,128)(2,1)S(1)}, u32[]{:S(2)}, u32[]{:S(2)}) collective-permute-start(bf16[256,512]{1,0:T(8,128)(2,1)S(1)} %get-tuple-element.63), channel_id=1, source_target_pairs={{0,24},{8,16},{16,8},{24,0},{1,25},{9,17},{17,9},{25,1},{2,26},{10... | collective-permute-start | bytes 786440 | tf_op jit(solution)/shard_map/ppermute | solution.py:585
  62.1 12.2 %collective-permute-start.13 = (bf16[192,512]{1,0:T(8,128)(2,1)S(1)}, bf16[192,512]{1,0:T(8,128)(2,1)S(1)}, u32[]{:S(2)}, u32[]{:S(2)}) collective-permute-start(bf16[192,512]{1,0:T(8,128)(2,1)S(1)} %get-tuple-element.65), channel_id=1, source_target_pairs={{0,8},{8,0},{16,24},{24,16},{1,9},{9,1},{17,25},{25,17},{2,10},{10... | collective-permute-start | bytes 589832 | tf_op jit(solution)/shard_map/ppermute | solution.py:616
  62.8 13.1 %collective-permute-start.14 = (bf16[192,512]{1,0:T(8,128)(2,1)S(1)}, bf16[192,512]{1,0:T(8,128)(2,1)S(1)}, u32[]{:S(2)}, u32[]{:S(2)}) collective-permute-start(bf16[192,512]{1,0:T(8,128)(2,1)S(1)} %get-tuple-element.66), channel_id=1, source_target_pairs={{0,16},{8,24},{16,0},{24,8},{1,17},{9,25},{17,1},{25,9},{2,18},{10... | collective-permute-start | bytes 589832 | tf_op jit(solution)/shard_map/ppermute | solution.py:616
  64.0 12.0 %collective-permute-start.15 = (bf16[192,512]{1,0:T(8,128)(2,1)S(1)}, bf16[192,512]{1,0:T(8,128)(2,1)S(1)}, u32[]{:S(2)}, u32[]{:S(2)}) collective-permute-start(bf16[192,512]{1,0:T(8,128)(2,1)S(1)} %get-tuple-element.67), channel_id=1, source_target_pairs={{0,24},{8,16},{16,8},{24,0},{1,25},{9,17},{17,9},{25,1},{2,26},{10... | collective-permute-start | bytes 589832 | tf_op jit(solution)/shard_map/ppermute | solution.py:616
  72.4 12.7 %collective-permute-start.16 = (bf16[384,512]{1,0:T(8,128)(2,1)S(1)}, bf16[384,512]{1,0:T(8,128)(2,1)S(1)}, u32[]{:S(2)}, u32[]{:S(2)}) collective-permute-start(bf16[384,512]{1,0:T(8,128)(2,1)S(1)} %get-tuple-element.70), channel_id=1, source_target_pairs={{0,8},{8,0},{16,24},{24,16},{1,9},{9,1},{17,25},{25,17},{2,10},{10... | collective-permute-start | bytes 1179656 | tf_op jit(solution)/shard_map/ppermute | solution.py:616
  73.1 20.2 %collective-permute-start.17 = (bf16[384,512]{1,0:T(8,128)(2,1)S(1)}, bf16[384,512]{1,0:T(8,128)(2,1)S(1)}, u32[]{:S(2)}, u32[]{:S(2)}) collective-permute-start(bf16[384,512]{1,0:T(8,128)(2,1)S(1)} %get-tuple-element.71), channel_id=1, source_target_pairs={{0,16},{8,24},{16,0},{24,8},{1,17},{9,25},{17,1},{25,9},{2,18},{10... | collective-permute-start | bytes 1179656 | tf_op jit(solution)/shard_map/ppermute | solution.py:616
  74.3 19.6 %collective-permute-start.18 = (bf16[384,512]{1,0:T(8,128)(2,1)S(1)}, bf16[384,512]{1,0:T(8,128)(2,1)S(1)}, u32[]{:S(2)}, u32[]{:S(2)}) collective-permute-start(bf16[384,512]{1,0:T(8,128)(2,1)S(1)} %get-tuple-element.72), channel_id=1, source_target_pairs={{0,24},{8,16},{16,8},{24,0},{1,25},{9,17},{17,9},{25,1},{2,26},{10... | collective-permute-start | bytes 1179656 | tf_op jit(solution)/shard_map/ppermute | solution.py:616
  79.1 19.9 %collective-permute-start.19 = (bf16[192,512]{1,0:T(8,128)(2,1)S(1)}, bf16[192,512]{1,0:T(8,128)(2,1)S(1)}, u32[]{:S(2)}, u32[]{:S(2)}) collective-permute-start(bf16[192,512]{1,0:T(8,128)(2,1)S(1)} %get-tuple-element.74), channel_id=1, source_target_pairs={{0,8},{8,0},{16,24},{24,16},{1,9},{9,1},{17,25},{25,17},{2,10},{10... | collective-permute-start | bytes 589832 | tf_op jit(solution)/shard_map/ppermute | solution.py:616
  79.9 19.2 %collective-permute-start.20 = (bf16[192,512]{1,0:T(8,128)(2,1)S(1)}, bf16[192,512]{1,0:T(8,128)(2,1)S(1)}, u32[]{:S(2)}, u32[]{:S(2)}) collective-permute-start(bf16[192,512]{1,0:T(8,128)(2,1)S(1)} %get-tuple-element.75), channel_id=1, source_target_pairs={{0,16},{8,24},{16,0},{24,8},{1,17},{9,25},{17,1},{25,9},{2,18},{10... | collective-permute-start | bytes 589832 | tf_op jit(solution)/shard_map/ppermute | solution.py:616
  85.1 15.5 %collective-permute-start.21 = (bf16[192,512]{1,0:T(8,128)(2,1)S(1)}, bf16[192,512]{1,0:T(8,128)(2,1)S(1)}, u32[]{:S(2)}, u32[]{:S(2)}) collective-permute-start(bf16[192,512]{1,0:T(8,128)(2,1)S(1)} %get-tuple-element.76), channel_id=1, source_target_pairs={{0,24},{8,16},{16,8},{24,0},{1,25},{9,17},{17,9},{25,1},{2,26},{10... | collective-permute-start | bytes 589832 | tf_op jit(solution)/shard_map/ppermute | solution.py:616
  (4 other events, 26.5 us)

commit v7 on v5

--- a/solution.py
+++ b/solution.py
@@ -523,7 +523,7 @@
     tiles = lax.axis_size("tile")
     dirs = comps // NF
     parts_out = split_directions(dirs, (4, 4, 4))
-    parts_back = split_directions(dirs, (3, 6, 3))
+    parts_back = split_directions(dirs, (4, 6, 2))
 
     ahead = parts_out[0] * NF
     parity = (tile % 2).astype(jnp.int32)

time: 105 us -> 105 us (level)
  no operation moved by 1% of the time
where the time goes in v7:
time: 105 us; the launch traced here: 104 us
  Pallas kernels  59.3 us (56%)
  starting transfers between devices  27.5 us (26%)
  waiting for transfers between devices  11.8 us (11%)
  local copies, waits for them, and re-layouts  3.02 us (3%)
  other arithmetic  1.97 us (2%)
    pallas_call x3, Pallas kernels, propagate(): pl.pallas_call(functools.partial(propagate_kernel, peers, share, begin *...  23.8 us
    pallas_call x3, Pallas kernels, finish(): pl.pallas_call(functools.partial(finish_kernel, peers, share, begin * NF,...  13.2 us
    ppermute x9, starting transfers between devices, local(): lax.ppermute(renewed[k], 'spec', [(i, i ^ k) for i in range(peers)])  10.7 us
    ppermute x9, starting transfers between devices, local(): lax.ppermute(packed[k], 'spec', [(i, i ^ k) for i in range(peers)])  10.7 us
    ppermute x9, waiting for transfers between devices, local(): lax.ppermute(renewed[k], 'spec', [(i, i ^ k) for i in range(peers)])  8.47 us
    pallas_call x2, Pallas kernels, couple(): pl.pallas_call(functools.partial(couple_kernel, peers, dirs, begin, size,...  8.18 us
    ppermute x4, starting transfers between devices, swap(): return lax.ppermute(array, 'tile', pairs + [(j, i) for i, j in pairs])  6.07 us
    ppermute x9, waiting for transfers between devices, local(): lax.ppermute(packed[k], 'spec', [(i, i ^ k) for i in range(peers)])  3.34 us
  transfers between devices with their start and end apart: 22, of which 4 were waited for; matrix products, arithmetic and copies ran while one was open for 3% of the time, Pallas kernels for 51%

profile of v7, /device:TPU:0, one launch (start us, length us, event | category | flops | bytes accessed | tf_op | source)
XLA Modules:
  0.0 104.2 jit_solution(1467655741938342928)
XLA Ops:
  6.4 1.6 %mark.1 = (bf16[16,256,512]{2,1,0:T(8,128)(2,1)S(1)}, f32[768,128]{1,0:T(8,128)S(1)}, f32[768,128]{1,0:T(8,128)S(1)}, bf16[2,512,256]{2,1,0:T(8,128)(2,1)S(1)}, bf16[2,512,256]{2,1,0:T(8,128)(2,1)S(1)}) custom-call(s32[20]{0:T(128)S(1)} %concatenate.17.meta, s32[256,16]{1,0:T(8,128)S(1)} %copy.15.slot_t, f32[768,128]{1,0:T(8,128)S(1)} %broadcast_in_dim.51.ae, ...), custom_call_target="tpu_custom_call" | custom-call | flops 4600000000 | bytes 12000000 | tf_op jit(solution)/shard_map/mark/pallas_call | solution.py:63
  8.0 4.0 %collective-permute-start = (bf16[2,512,256]{2,1,0:T(8,128)(2,1)S(1)}, bf16[2,512,256]{2,1,0:T(8,128)(2,1)S(1)}, u32[]{:S(2)}, u32[]{:S(2)}) collective-permute-start(bf16[2,512,256]{2,1,0:T(8,128)(2,1)S(1)} %get-tuple-element.41), channel_id=1, source_target_pairs={{0,1},{2,3},{4,5},{6,7},{1,0},{3,2},{5,4},{7,6},{8,9},{10,11},{12,... | collective-permute-start | bytes 1572872 | tf_op jit(solution)/shard_map/ppermute | solution.py:515
  13.0 7.9 %propagate.3 = (bf16[16,768,256]{2,1,0:T(8,128)(2,1)}, bf16[256,512]{1,0:T(8,128)(2,1)S(1)}, bf16[256,512]{1,0:T(8,128)(2,1)S(1)}, bf16[256,512]{1,0:T(8,128)(2,1)S(1)}, bf16[256,512]{1,0:T(8,128)(2,1)S(1)}) custom-call(s32[20]{0:T(128)S(1)} %concatenate.17.meta, bf16[16,768,256]{2,1,0:T(8,128)(2,1)S(1)} %bitcast.16, ...), custom_call_target="tpu_custom_call" | custom-call | flops 10119999488 | bytes 26400000 | tf_op jit(solution)/shard_map/propagate/pallas_call | solution.py:294
  20.9 1.6 %collective-permute-start.4 = (bf16[256,512]{1,0:T(8,128)(2,1)S(1)}, bf16[256,512]{1,0:T(8,128)(2,1)S(1)}, u32[]{:S(2)}, u32[]{:S(2)}) collective-permute-start(bf16[256,512]{1,0:T(8,128)(2,1)S(1)} %get-tuple-element.47), channel_id=1, source_target_pairs={{0,8},{8,0},{16,24},{24,16},{1,9},{9,1},{17,25},{25,17},{2,10},{10... | collective-permute-start | bytes 786440 | tf_op jit(solution)/shard_map/ppermute | solution.py:585
  24.4 7.9 %propagate.4 = (bf16[16,768,256]{2,1,0:T(8,128)(2,1)}, bf16[256,512]{1,0:T(8,128)(2,1)S(1)}, bf16[256,512]{1,0:T(8,128)(2,1)S(1)}, bf16[256,512]{1,0:T(8,128)(2,1)S(1)}, bf16[256,512]{1,0:T(8,128)(2,1)S(1)}) custom-call(s32[20]{0:T(128)S(1)} %concatenate.17.meta, bf16[16,768,256]{2,1,0:T(8,128)(2,1)S(1)} %bitcast.16, ...), custom_call_target="tpu_custom_call", output_to_operand_aliasing={{0}: (11, {})} | custom-call | flops 10119999488 | bytes 26400000 | tf_op jit(solution)/shard_map/propagate/pallas_call | solution.py:294
  32.3 1.6 %collective-permute-start.7 = (bf16[256,512]{1,0:T(8,128)(2,1)S(1)}, bf16[256,512]{1,0:T(8,128)(2,1)S(1)}, u32[]{:S(2)}, u32[]{:S(2)}) collective-permute-start(bf16[256,512]{1,0:T(8,128)(2,1)S(1)} %get-tuple-element.58), channel_id=1, source_target_pairs={{0,8},{8,0},{16,24},{24,16},{1,9},{9,1},{17,25},{25,17},{2,10},{10... | collective-permute-start | bytes 786440 | tf_op jit(solution)/shard_map/ppermute | solution.py:585
  33.9 1.5 %collective-permute-start.8 = (bf16[256,512]{1,0:T(8,128)(2,1)S(1)}, bf16[256,512]{1,0:T(8,128)(2,1)S(1)}, u32[]{:S(2)}, u32[]{:S(2)}) collective-permute-start(bf16[256,512]{1,0:T(8,128)(2,1)S(1)} %get-tuple-element.59), channel_id=1, source_target_pairs={{0,16},{8,24},{16,0},{24,8},{1,17},{9,25},{17,1},{25,9},{2,18},{10... | collective-permute-start | bytes 786440 | tf_op jit(solution)/shard_map/ppermute | solution.py:585
  35.9 8.0 %propagate.5 = (bf16[16,768,256]{2,1,0:T(8,128)(2,1)}, bf16[256,512]{1,0:T(8,128)(2,1)S(1)}, bf16[256,512]{1,0:T(8,128)(2,1)S(1)}, bf16[256,512]{1,0:T(8,128)(2,...) custom-call(s32[20]{0:T(128)S(1)} %concatenate.17.meta, ...), custom_call_target="tpu_custom_call", output_to_operand_aliasing={{0}: (15, {})} | custom-call | flops 10119999488 | bytes 26400000 | tf_op jit(solution)/shard_map/propagate/pallas_call | solution.py:294
  43.9 1.6 %collective-permute-start.10 = (bf16[256,512]{1,0:T(8,128)(2,1)S(1)}, bf16[256,512]{1,0:T(8,128)(2,1)S(1)}, u32[]{:S(2)}, u32[]{:S(2)}) collective-permute-start(bf16[256,512]{1,0:T(8,128)(2,1)S(1)} %get-tuple-element.61), channel_id=1, source_target_pairs={{0,8},{8,0},{16,24},{24,16},{1,9},{9,1},{17,25},{25,17},{2,10},{10... | collective-permute-start | bytes 786440 | tf_op jit(solution)/shard_map/ppermute | solution.py:585
  47.5 2.6 %setup.1 = (bf16[16,512,256]{2,1,0:T(8,128)(2,1)S(1)}, f32[48,3072]{1,0:T(8,128)S(1)}, bf16[2,64,6144]{2,1,0:T(8,128)(2,1)S(1)}) custom-call(s32[20]{0:T(128)S(1)} %concatenate.17.meta, s32[16,256]{1,0:T(8,128)S(1)} %fusion.1.slot, s32[24,48]{1,0:T(8,128)S(1)} %bitcast.20, bf16[48,64,64]{2,1,0:T(8,128)(2,1)S(1)} %copy-done, ...), custom_call_target="tpu_custom_call" | custom-call | flops 230000000 | bytes 600000 | tf_op jit(solution)/shard_map/setup/pallas_call | solution.py:109
  51.7 1.7 %weave.4.w = bf16[1536,3072]{1,0:T(8,128)(2,1)S(1)} custom-call(f32[48,3072]{1,0:T(8,128)S(1)} %get-tuple-element.55.sel, bf16[2,64,6144]{2,1,0:T(8,128)(2,1)S(1)} %get-tuple-element.56.tt, bf16[256,512]{1,0:T(8,128)(2,1)S(1)} %get-tuple-element.52.after.rest_4_.rest_0_), custom_call_target="tpu_custom_call" | custom-call | flops 115000000 | bytes 300000 | tf_op jit(solution)/shard_map/weave/pallas_call | solution.py:139
  54.1 2.9 %begin_couple.1.partial = f32[1024,512]{1,0:T(8,128)S(1)} custom-call(s32[20]{0:T(128)S(1)} %concatenate.17.meta, bf16[1024,3072]{1,0:T(8,128)(2,1)S(1)} %weave.3.w, bf16[256,512]{1,0:T(8,128)(2,1)S(1)} %get-tuple-element.46.rest_0_, bf16[256,512]{1,0:T(8,128)(2,1)S(1)} %collective-permute-done.4.rest_1_, ...), custom_call_target="tpu_custom_call" | custom-call | flops 230000000 | bytes 600000 | tf_op jit(solution)/shard_map/begin_couple/pallas_call | solution.py:411
  57.0 3.3 %collective-permute-done.11.rest_6_.rest_2_ = bf16[256,512]{1,0:T(8,128)(2,1)S(1)} collective-permute-done((bf16[256,512]{1,0:T(8,128)(2,1)S(1)}, bf16[256,512]{1,0:T(8,128)(2,1)S(1)}, u32[]{:S(2)}, u32[]{:S(2)}) %collective-permute-start.11) | collective-permute-done | bytes 262176 | tf_op jit(solution)/shard_map/ppermute | solution.py:585
  60.3 2.3 %end_couple.1 = (bf16[256,512]{1,0:T(8,128)(2,1)S(1)}, bf16[256,512]{1,0:T(8,128)(2,1)S(1)}, bf16[256,512]{1,0:T(8,128)(2,1)S(1)}, bf16[256,512]{1,0:T(8,128)(2,1)S(1)}) custom-call(s32[20]{0:T(128)S(1)} %concatenate.17.meta, bf16[1024,3072]{1,0:T(8,128)(2,1)S(1)} %weave.3.w, f32[1024,512]{1,0:T(8,128)S(1)} %begin_couple.1.partial, ...), custom_call_target="tpu_custom_call" | custom-call | flops 2300000000 | bytes 6000000 | tf_op jit(solution)/shard_map/end_couple/pallas_call | solution.py:440
  64.5 1.6 %collective-permute-start.15 = (bf16[256,512]{1,0:T(8,128)(2,1)S(1)}, bf16[256,512]{1,0:T(8,128)(2,1)S(1)}, u32[]{:S(2)}, u32[]{:S(2)}) collective-permute-start(bf16[256,512]{1,0:T(8,128)(2,1)S(1)} %get-tuple-element.67), channel_id=1, source_target_pairs={{0,24},{8,16},{16,8},{24,0},{1,25},{9,17},{17,9},{25,1},{2,26},{10... | collective-permute-start | bytes 786440 | tf_op jit(solution)/shard_map/ppermute | solution.py:616
  67.0 5.8 %couple.2 = (bf16[384,512]{1,0:T(8,128)(2,1)S(1)}, bf16[384,512]{1,0:T(8,128)(2,1)S(1)}, bf16[384,512]{1,0:T(8,128)(2,1)S(1)}, bf16[384,512]{1,0:T(8,128)(2,1)S(1)}) custom-call(s32[20]{0:T(128)S(1)} %concatenate.17.meta, bf16[1536,3072]{1,0:T(8,128)(2,1)S(1)} %weave.4.w, bf16[3072,512]{1,0:T(8,128)(2,1)S(1)} %collect.3.rest_0_, ...), custom_call_target="tpu_custom_call" | custom-call | flops 6899999744 | bytes 18000000 | tf_op jit(solution)/shard_map/couple/pallas_call | solution.py:377
  74.8 1.6 %collective-permute-start.18 = (bf16[384,512]{1,0:T(8,128)(2,1)S(1)}, bf16[384,512]{1,0:T(8,128)(2,1)S(1)}, u32[]{:S(2)}, u32[]{:S(2)}) collective-permute-start(bf16[384,512]{1,0:T(8,128)(2,1)S(1)} %get-tuple-element.72), channel_id=1, source_target_pairs={{0,24},{8,16},{16,8},{24,0},{1,25},{9,17},{17,9},{25,1},{2,26},{10... | collective-permute-start | bytes 1179656 | tf_op jit(solution)/shard_map/ppermute | solution.py:616
  76.4 1.9 %collective-permute-done.15.rest_3_ = bf16[256,512]{1,0:T(8,128)(2,1)S(1)} collective-permute-done((bf16[256,512]{1,0:T(8,128)(2,1)S(1)}, bf16[256,512]{1,0:T(8,128)(2,1)S(1)}, u32[]{:S(2)}, u32[]{:S(2)}) %collective-permute-start.15) | collective-permute-done | bytes 262176 | tf_op jit(solution)/shard_map/ppermute | solution.py:616
  78.3 2.4 %couple.3 = (bf16[128,512]{1,0:T(8,128)(2,1)S(1)}, bf16[128,512]{1,0:T(8,128)(2,1)S(1)}, bf16[128,512]{1,0:T(8,128)(2,1)S(1)}, bf16[128,512]{1,0:T(8,128)(2,1)S(1)}) custom-call(s32[20]{0:T(128)S(1)} %concatenate.17.meta, bf16[512,3072]{1,0:T(8,128)(2,1)S(1)} %weave.5.w, bf16[3072,512]{1,0:T(8,128)(2,1)S(1)} %collect.3.rest_0_, ...), custom_call_target="tpu_custom_call" | custom-call | flops 2300000000 | bytes 6000000 | tf_op jit(solution)/shard_map/couple/pallas_call | solution.py:377
  81.2 2.0 %collective-permute-start.20 = (bf16[128,512]{1,0:T(8,128)(2,1)S(1)}, bf16[128,512]{1,0:T(8,128)(2,1)S(1)}, u32[]{:S(2)}, u32[]{:S(2)}) collective-permute-start(bf16[128,512]{1,0:T(8,128)(2,1)S(1)} %get-tuple-element.75), channel_id=1, source_target_pairs={{0,16},{8,24},{16,0},{24,8},{1,17},{9,25},{17,1},{25,9},{2,18},{10... | collective-permute-start | bytes 393224 | tf_op jit(solution)/shard_map/ppermute | solution.py:616
  83.2 4.4 %finish.3.moved = bf16[16,768,256]{2,1,0:T(8,128)(2,1)} custom-call(s32[20]{0:T(128)S(1)} %concatenate.17.meta, s32[16,256]{1,0:T(8,128)S(1)} %fusion.1.slot, bf16[16,512,256]{2,1,0:T(8,128)(2,1)S(1)} %get-tuple-element.53.spread, bf16[16,768,256]{2,1,0:T(8,128)(2,1)} %get-tuple-element.54.moved, ...), custom_call_target="tpu_custom_call", output_to_operand_aliasing={{}: (3, {})} | custom-call | flops 4600000000 | bytes 12000000 | tf_op jit(solution)/shard_map/finish/pallas_call | solution.py:491
  88.7 5.2 %collective-permute-done.17.rest_2_ = bf16[384,512]{1,0:T(8,128)(2,1)S(1)} collective-permute-done((bf16[384,512]{1,0:T(8,128)(2,1)S(1)}, bf16[384,512]{1,0:T(8,128)(2,1)S(1)}, u32[]{:S(2)}, u32[]{:S(2)}) %collective-permute-start.17) | collective-permute-done | bytes 393248 | tf_op jit(solution)/shard_map/ppermute | solution.py:616
  95.2 5.1 %finish.4.moved = bf16[16,768,256]{2,1,0:T(8,128)(2,1)} custom-call(s32[20]{0:T(128)S(1)} %concatenate.17.meta, s32[16,256]{1,0:T(8,128)S(1)} %fusion.1.slot, bf16[16,512,256]{2,1,0:T(8,128)(2,1)S(1)} %get-tuple-element.53.spread, bf16[16,768,256]{2,1,0:T(8,128)(2,1)} %finish.3.moved, ...), custom_call_target="tpu_custom_call", output_to_operand_aliasing={{}: (3, {})} | custom-call | flops 6899999744 | bytes 18000000 | tf_op jit(solution)/shard_map/finish/pallas_call | solution.py:491
  100.4 3.6 %finish.5 = bf16[16,768,256]{2,1,0:T(8,128)(2,1)} custom-call(s32[20]{0:T(128)S(1)} %concatenate.17.meta, s32[16,256]{1,0:T(8,128)S(1)} %fusion.1.slot, bf16[16,512,256]{2,1,0:T(8,128)(2,1)S(1)} %get-tuple-element.53.spread, bf16[16,768,256]{2,1,0:T(8,128)(2,1)} %finish.4.moved, ...), custom_call_target="tpu_custom_call", output_to_operand_aliasing={{}: (3, {})} | custom-call | flops 2300000000 | bytes 6000000 | tf_op jit(solution)/shard_map/finish/pallas_call | solution.py:491
  (71 shorter events, 21.6 us)
Async XLA Ops:
  2.0 10.9 %collective-permute-start.2 = (bf16[2,272,256]{2,1,0:T(8,128)(2,1)S(1)}, bf16[2,272,256]{2,1,0:T(8,128)(2,1)S(1)}, u32[]{:S(2)}, u32[]{:S(2)}) collective-permute-start(bf16[2,272,256]{2,1,0:T(8,128)(2,1)S(1)} %pad_maximum_fusion), channel_id=1, source_target_pairs={{0,1},{2,3},{4,5},{6,7},{1,0},{3,2},{5,4},{7,6},{8,9},{10,11},{12,... | collective-permute-start | bytes 835592 | tf_op jit(solution)/shard_map/ppermute | solution.py:515
  2.6 10.3 %collective-permute-start.3 = (bf16[2,272,256]{2,1,0:T(8,128)(2,1)S(1)}, bf16[2,272,256]{2,1,0:T(8,128)(2,1)S(1)}, u32[]{:S(2)}, u32[]{:S(2)}) collective-permute-start(bf16[2,272,256]{2,1,0:T(8,128)(2,1)S(1)} %pad_maximum_fusion.1), channel_id=1, source_target_pairs={{1,2},{3,4},{5,6},{2,1},{4,3},{6,5},{9,10},{11,12},{13,14},{10,9},... | collective-permute-start | bytes 835592 | tf_op jit(solution)/shard_map/ppermute | solution.py:515
  8.0 16.4 %collective-permute-start = (bf16[2,512,256]{2,1,0:T(8,128)(2,1)S(1)}, bf16[2,512,256]{2,1,0:T(8,128)(2,1)S(1)}, u32[]{:S(2)}, u32[]{:S(2)}) collective-permute-start(bf16[2,512,256]{2,1,0:T(8,128)(2,1)S(1)} %get-tuple-element.41), channel_id=1, source_target_pairs={{0,1},{2,3},{4,5},{6,7},{1,0},{3,2},{5,4},{7,6},{8,9},{10,11},{12,... | collective-permute-start | bytes 1572872 | tf_op jit(solution)/shard_map/ppermute | solution.py:515
  12.0 12.4 %collective-permute-start.1 = (bf16[2,512,256]{2,1,0:T(8,128)(2,1)S(1)}, bf16[2,512,256]{2,1,0:T(8,128)(2,1)S(1)}, u32[]{:S(2)}, u32[]{:S(2)}) collective-permute-start(bf16[2,512,256]{2,1,0:T(8,128)(2,1)S(1)} %get-tuple-element.42), channel_id=1, source_target_pairs={{1,2},{3,4},{5,6},{2,1},{4,3},{6,5},{9,10},{11,12},{13,14},{10,9},... | collective-permute-start | bytes 1572872 | tf_op jit(solution)/shard_map/ppermute | solution.py:515
  20.9 14.5 %collective-permute-start.4 = (bf16[256,512]{1,0:T(8,128)(2,1)S(1)}, bf16[256,512]{1,0:T(8,128)(2,1)S(1)}, u32[]{:S(2)}, u32[]{:S(2)}) collective-permute-start(bf16[256,512]{1,0:T(8,128)(2,1)S(1)} %get-tuple-element.47), channel_id=1, source_target_pairs={{0,8},{8,0},{16,24},{24,16},{1,9},{9,1},{17,25},{25,17},{2,10},{10... | collective-permute-start | bytes 786440 | tf_op jit(solution)/shard_map/ppermute | solution.py:585
  22.4 13.4 %collective-permute-start.5 = (bf16[256,512]{1,0:T(8,128)(2,1)S(1)}, bf16[256,512]{1,0:T(8,128)(2,1)S(1)}, u32[]{:S(2)}, u32[]{:S(2)}) collective-permute-start(bf16[256,512]{1,0:T(8,128)(2,1)S(1)} %get-tuple-element.48), channel_id=1, source_target_pairs={{0,16},{8,24},{16,0},{24,8},{1,17},{9,25},{17,1},{25,9},{2,18},{10... | collective-permute-start | bytes 786440 | tf_op jit(solution)/shard_map/ppermute | solution.py:585
  24.0 11.9 %collective-permute-start.6 = (bf16[256,512]{1,0:T(8,128)(2,1)S(1)}, bf16[256,512]{1,0:T(8,128)(2,1)S(1)}, u32[]{:S(2)}, u32[]{:S(2)}) collective-permute-start(bf16[256,512]{1,0:T(8,128)(2,1)S(1)} %get-tuple-element.49), channel_id=1, source_target_pairs={{0,24},{8,16},{16,8},{24,0},{1,25},{9,17},{17,9},{25,1},{2,26},{10... | collective-permute-start | bytes 786440 | tf_op jit(solution)/shard_map/ppermute | solution.py:585
  32.3 14.7 %collective-permute-start.7 = (bf16[256,512]{1,0:T(8,128)(2,1)S(1)}, bf16[256,512]{1,0:T(8,128)(2,1)S(1)}, u32[]{:S(2)}, u32[]{:S(2)}) collective-permute-start(bf16[256,512]{1,0:T(8,128)(2,1)S(1)} %get-tuple-element.58), channel_id=1, source_target_pairs={{0,8},{8,0},{16,24},{24,16},{1,9},{9,1},{17,25},{25,17},{2,10},{10... | collective-permute-start | bytes 786440 | tf_op jit(solution)/shard_map/ppermute | solution.py:585
  33.9 19.5 %collective-permute-start.8 = (bf16[256,512]{1,0:T(8,128)(2,1)S(1)}, bf16[256,512]{1,0:T(8,128)(2,1)S(1)}, u32[]{:S(2)}, u32[]{:S(2)}) collective-permute-start(bf16[256,512]{1,0:T(8,128)(2,1)S(1)} %get-tuple-element.59), channel_id=1, source_target_pairs={{0,16},{8,24},{16,0},{24,8},{1,17},{9,25},{17,1},{25,9},{2,18},{10... | collective-permute-start | bytes 786440 | tf_op jit(solution)/shard_map/ppermute | solution.py:585
  35.4 18.0 %collective-permute-start.9 = (bf16[256,512]{1,0:T(8,128)(2,1)S(1)}, bf16[256,512]{1,0:T(8,128)(2,1)S(1)}, u32[]{:S(2)}, u32[]{:S(2)}) collective-permute-start(bf16[256,512]{1,0:T(8,128)(2,1)S(1)} %get-tuple-element.60), channel_id=1, source_target_pairs={{0,24},{8,16},{16,8},{24,0},{1,25},{9,17},{17,9},{25,1},{2,26},{10... | collective-permute-start | bytes 786440 | tf_op jit(solution)/shard_map/ppermute | solution.py:585
  35.9 11.6 %copy-start = (bf16[48,64,64]{2,1,0:T(8,128)(2,1)S(1)}, bf16[48,64,64]{2,1,0:T(8,128)(2,1)}, u32[]{:S(2)}) copy-start(bf16[48,64,64]{2,1,0:T(8,128)(2,1)} %table.1) | copy-start | bytes 1179652
  35.9 11.6 %copy-start.3 = (s32[48,24]{0,1:T(8,128)S(1)}, s32[48,24]{0,1:T(8,128)}, u32[]{:S(2)}) copy-start(s32[48,24]{0,1:T(8,128)} %param.10) | copy-start | bytes 13828
  43.9 13.0 %collective-permute-start.10 = (bf16[256,512]{1,0:T(8,128)(2,1)S(1)}, bf16[256,512]{1,0:T(8,128)(2,1)S(1)}, u32[]{:S(2)}, u32[]{:S(2)}) collective-permute-start(bf16[256,512]{1,0:T(8,128)(2,1)S(1)} %get-tuple-element.61), channel_id=1, source_target_pairs={{0,8},{8,0},{16,24},{24,16},{1,9},{9,1},{17,25},{25,17},{2,10},{10... | collective-permute-start | bytes 786440 | tf_op jit(solution)/shard_map/ppermute | solution.py:585
  45.5 14.8 %collective-permute-start.11 = (bf16[256,512]{1,0:T(8,128)(2,1)S(1)}, bf16[256,512]{1,0:T(8,128)(2,1)S(1)}, u32[]{:S(2)}, u32[]{:S(2)}) collective-permute-start(bf16[256,512]{1,0:T(8,128)(2,1)S(1)} %get-tuple-element.62), channel_id=1, source_target_pairs={{0,16},{8,24},{16,0},{24,8},{1,17},{9,25},{17,1},{25,9},{2,18},{10... | collective-permute-start | bytes 786440 | tf_op jit(solution)/shard_map/ppermute | solution.py:585
  47.0 13.3 %collective-permute-start.12 = (bf16[256,512]{1,0:T(8,128)(2,1)S(1)}, bf16[256,512]{1,0:T(8,128)(2,1)S(1)}, u32[]{:S(2)}, u32[]{:S(2)}) collective-permute-start(bf16[256,512]{1,0:T(8,128)(2,1)S(1)} %get-tuple-element.63), channel_id=1, source_target_pairs={{0,24},{8,16},{16,8},{24,0},{1,25},{9,17},{17,9},{25,1},{2,26},{10... | collective-permute-start | bytes 786440 | tf_op jit(solution)/shard_map/ppermute | solution.py:585
  62.5 12.2 %collective-permute-start.13 = (bf16[256,512]{1,0:T(8,128)(2,1)S(1)}, bf16[256,512]{1,0:T(8,128)(2,1)S(1)}, u32[]{:S(2)}, u32[]{:S(2)}) collective-permute-start(bf16[256,512]{1,0:T(8,128)(2,1)S(1)} %get-tuple-element.65), channel_id=1, source_target_pairs={{0,8},{8,0},{16,24},{24,16},{1,9},{9,1},{17,25},{25,17},{2,10},{10... | collective-permute-start | bytes 786440 | tf_op jit(solution)/shard_map/ppermute | solution.py:616
  63.3 13.1 %collective-permute-start.14 = (bf16[256,512]{1,0:T(8,128)(2,1)S(1)}, bf16[256,512]{1,0:T(8,128)(2,1)S(1)}, u32[]{:S(2)}, u32[]{:S(2)}) collective-permute-start(bf16[256,512]{1,0:T(8,128)(2,1)S(1)} %get-tuple-element.66), channel_id=1, source_target_pairs={{0,16},{8,24},{16,0},{24,8},{1,17},{9,25},{17,1},{25,9},{2,18},{10... | collective-permute-start | bytes 786440 | tf_op jit(solution)/shard_map/ppermute | solution.py:616
  64.5 13.9 %collective-permute-start.15 = (bf16[256,512]{1,0:T(8,128)(2,1)S(1)}, bf16[256,512]{1,0:T(8,128)(2,1)S(1)}, u32[]{:S(2)}, u32[]{:S(2)}) collective-permute-start(bf16[256,512]{1,0:T(8,128)(2,1)S(1)} %get-tuple-element.67), channel_id=1, source_target_pairs={{0,24},{8,16},{16,8},{24,0},{1,25},{9,17},{17,9},{25,1},{2,26},{10... | collective-permute-start | bytes 786440 | tf_op jit(solution)/shard_map/ppermute | solution.py:616
  72.8 14.7 %collective-permute-start.16 = (bf16[384,512]{1,0:T(8,128)(2,1)S(1)}, bf16[384,512]{1,0:T(8,128)(2,1)S(1)}, u32[]{:S(2)}, u32[]{:S(2)}) collective-permute-start(bf16[384,512]{1,0:T(8,128)(2,1)S(1)} %get-tuple-element.70), channel_id=1, source_target_pairs={{0,8},{8,0},{16,24},{24,16},{1,9},{9,1},{17,25},{25,17},{2,10},{10... | collective-permute-start | bytes 1179656 | tf_op jit(solution)/shard_map/ppermute | solution.py:616
  73.6 20.4 %collective-permute-start.17 = (bf16[384,512]{1,0:T(8,128)(2,1)S(1)}, bf16[384,512]{1,0:T(8,128)(2,1)S(1)}, u32[]{:S(2)}, u32[]{:S(2)}) collective-permute-start(bf16[384,512]{1,0:T(8,128)(2,1)S(1)} %get-tuple-element.71), channel_id=1, source_target_pairs={{0,16},{8,24},{16,0},{24,8},{1,17},{9,25},{17,1},{25,9},{2,18},{10... | collective-permute-start | bytes 1179656 | tf_op jit(solution)/shard_map/ppermute | solution.py:616
  74.8 20.4 %collective-permute-start.18 = (bf16[384,512]{1,0:T(8,128)(2,1)S(1)}, bf16[384,512]{1,0:T(8,128)(2,1)S(1)}, u32[]{:S(2)}, u32[]{:S(2)}) collective-permute-start(bf16[384,512]{1,0:T(8,128)(2,1)S(1)} %get-tuple-element.72), channel_id=1, source_target_pairs={{0,24},{8,16},{16,8},{24,0},{1,25},{9,17},{17,9},{25,1},{2,26},{10... | collective-permute-start | bytes 1179656 | tf_op jit(solution)/shard_map/ppermute | solution.py:616
  80.7 19.7 %collective-permute-start.19 = (bf16[128,512]{1,0:T(8,128)(2,1)S(1)}, bf16[128,512]{1,0:T(8,128)(2,1)S(1)}, u32[]{:S(2)}, u32[]{:S(2)}) collective-permute-start(bf16[128,512]{1,0:T(8,128)(2,1)S(1)} %get-tuple-element.74), channel_id=1, source_target_pairs={{0,8},{8,0},{16,24},{24,16},{1,9},{9,1},{17,25},{25,17},{2,10},{10... | collective-permute-start | bytes 393224 | tf_op jit(solution)/shard_map/ppermute | solution.py:616
  81.2 19.2 %collective-permute-start.20 = (bf16[128,512]{1,0:T(8,128)(2,1)S(1)}, bf16[128,512]{1,0:T(8,128)(2,1)S(1)}, u32[]{:S(2)}, u32[]{:S(2)}) collective-permute-start(bf16[128,512]{1,0:T(8,128)(2,1)S(1)} %get-tuple-element.75), channel_id=1, source_target_pairs={{0,16},{8,24},{16,0},{24,8},{1,17},{9,25},{17,1},{25,9},{2,18},{10... | collective-permute-start | bytes 393224 | tf_op jit(solution)/shard_map/ppermute | solution.py:616
  87.5 12.9 %collective-permute-start.21 = (bf16[128,512]{1,0:T(8,128)(2,1)S(1)}, bf16[128,512]{1,0:T(8,128)(2,1)S(1)}, u32[]{:S(2)}, u32[]{:S(2)}) collective-permute-start(bf16[128,512]{1,0:T(8,128)(2,1)S(1)} %get-tuple-element.76), channel_id=1, source_target_pairs={{0,24},{8,16},{16,8},{24,0},{1,25},{9,17},{17,9},{25,1},{2,26},{10... | collective-permute-start | bytes 393224 | tf_op jit(solution)/shard_map/ppermute | solution.py:616
  (4 other events, 26.5 us)
